TPU v7x, 32 devices: a whole 2x2x4 slice. The times are simulated.
32 devices in a mesh: elem: 32 (over z, y, x, core).
Axes of the slice: x: 2, y: 2, z: 4, core: 2. Of those that a mesh axis runs over, the one named last changes fastest.
Arguments:
- elem_mats: bfloat16 [384, 750, 750], P('elem'), may hold values from -0.14 to 0.64
- face_blocks: bfloat16 [864, 125, 125], P('elem'), may hold values from -0.45 to 1.25
- rhs: bfloat16 [864, 16, 125], P('elem'), may hold values from -6 to 6
- elem_faces: int32 [384, 6], replicated, may hold values from 0 to 863, as said below
- orient: int32 [384, 6], replicated, may hold values from 0 to 7
- counts: int32 [32], replicated, may hold values from 3 to 9, as said below
Outputs:
- traces: float32 [864, 16, 125], P('elem')
Inputs may be any that keep to these rules, and one draw needn't show every extreme that they name: Element slots 0 to counts[d] - 1 of device d (rows d * 12 onward) are live, the others empty; counts[2 i] + counts[2 i + 1] = 12. `elem_faces`: face f is owned by device f // 27. A live element slot of device d has all its faces owned by devices d - 2 to d + 2; device d has exactly 4 live element faces owned by each other device within that distance; a face is listed by at most two live element faces. Rows of empty slots hold arbitrary faces.
All inputs are finite; a program needn't handle non-finite values.
Results may differ from a plain program's by a relative error of at most 0.0017.
Values may be sent and summed in bfloat16 or wider, within the bound.
No kernel may reach another device: no remote copies, remote signals or barrier semaphores. Data moves between devices by JAX's collectives and lax.ppermute only.
A program may use at most 128 MiB of HBM per device.

v0:
```python
import jax
import jax.numpy as jnp
import numpy as np
from jax import lax
from jax.sharding import PartitionSpec as P

COMP = 5
EDGE = 5
ITERS = 2
REACH = 2
SLOT = 4


def passed_along(block, axis, distance):
    devices = range(lax.axis_size(axis))
    route = [(i - distance, i) for i in devices if i - distance in devices]
    return lax.ppermute(block, axis, route)


def orient_tables(edge_nodes, components):
    node_ids = np.arange(edge_nodes * edge_nodes)
    row_pos = node_ids // edge_nodes
    col_pos = node_ids % edge_nodes
    table_rows = []
    for orient_code in range(8):
        if orient_code & 4:
            first_pos, second_pos = (col_pos, row_pos)
        else:
            first_pos, second_pos = (row_pos, col_pos)
        if orient_code & 1:
            first_pos = edge_nodes - 1 - first_pos
        if orient_code & 2:
            second_pos = edge_nodes - 1 - second_pos
        moved_node = first_pos * edge_nodes + second_pos
        table_rows.append(
            np.concatenate(
                [
                    part_index * edge_nodes * edge_nodes + moved_node
                    for part_index in range(components)
                ]
            )
        )
    forward = np.stack(table_rows).astype(np.int32)
    backward = np.argsort(forward, axis=1).astype(np.int32)
    return (forward, backward)


def face_offsets():
    return [step_size for step_size in range(1, REACH + 1)] + [
        -step_size for step_size in range(1, REACH + 1)
    ]


def pick_slots(chosen, values):
    rank_in = jnp.cumsum(chosen.astype(jnp.int32)) - 1
    slot_ids = jnp.arange(SLOT, dtype=jnp.int32)
    matches = chosen[None, :] & (rank_in[None, :] == slot_ids[:, None])
    present = jnp.any(matches, axis=1)
    picked = jnp.sum(jnp.where(matches, values[None, :], 0), axis=1)
    return (picked, present, rank_in)


def device_rows(elem_faces, counts, device, elem_cap, face_dev):
    devices_all = counts.shape[0]
    safe_device = jnp.clip(device, 0, devices_all - 1)
    faces_here = lax.dynamic_slice_in_dim(elem_faces, safe_device * elem_cap, elem_cap, 0).reshape(
        -1
    )
    slot_elem = jnp.arange(elem_cap * 6, dtype=jnp.int32) // 6
    is_live = (slot_elem < counts[safe_device]) & (device >= 0) & (device < devices_all)
    return (faces_here // face_dev, faces_here % face_dev, is_live)


def move_direct(piece, step_by, back):
    if back:
        return passed_along(piece, "elem", step_by)
    return passed_along(piece, "elem", step_by)


def deliver(pieces, back):
    offsets = face_offsets()
    results = []
    for offset, piece in zip(offsets, pieces):
        results.append(move_direct(piece, -offset if back else offset, back))
    return results


def element_terms(elem_frame, matrices, trace_len):
    blocks = matrices.reshape(matrices.shape[0], 6, trace_len, 6, trace_len)
    return jnp.einsum("akni,akilj->alnj", elem_frame, blocks, preferred_element_type=jnp.float32)


def per_device(elem_mats, face_blocks, rhs, elem_faces, orient, counts):
    my_index = lax.axis_index("elem")
    elem_cap = elem_mats.shape[0]
    face_dev = face_blocks.shape[0]
    trace_len = face_blocks.shape[1]
    functionals = rhs.shape[1]
    top_live = elem_cap - elem_cap // 4
    incidences = elem_cap * 6
    forward, backward = orient_tables(EDGE, COMP)
    my_orient = lax.dynamic_slice_in_dim(orient, my_index * elem_cap, elem_cap, 0).reshape(-1)
    to_element = jnp.asarray(forward)[my_orient]
    to_face = jnp.asarray(backward)[my_orient]
    owners, local_faces, is_live = device_rows(elem_faces, counts, my_index, elem_cap, face_dev)
    offsets = face_offsets()
    at_home = is_live & (owners == my_index)
    table_index = jnp.where(at_home, local_faces, 0)
    home_ids = jnp.where(at_home, local_faces, face_dev)
    send_picks = []
    send_present = []
    for group_index, offset in enumerate(offsets):
        chosen = is_live & (owners == my_index + offset)
        picked, present, rank_in = pick_slots(chosen, jnp.arange(incidences, dtype=jnp.int32))
        send_picks.append(picked)
        send_present.append(present)
        table_index = jnp.where(chosen, face_dev + group_index * SLOT + rank_in, table_index)
    recv_faces = []
    for offset in offsets:
        src_owners, src_local, src_live = device_rows(
            elem_faces, counts, my_index - offset, elem_cap, face_dev
        )
        chosen = src_live & (src_owners == my_index)
        picked, present, rank_in = pick_slots(chosen, src_local)
        recv_faces.append(jnp.where(present, picked, face_dev))
    my_count = counts[my_index]
    live_rows = jnp.arange(elem_cap, dtype=jnp.int32) < my_count
    traces = jnp.zeros((face_dev, functionals, trace_len), jnp.float32)
    for sweep_index in range(ITERS):
        rounded = traces.astype(jnp.bfloat16)
        back_buckets = [rounded[jnp.clip(face_ids, 0, face_dev - 1)] for face_ids in recv_faces]
        returned = deliver(back_buckets, True)
        source_table = jnp.concatenate([rounded] + returned, axis=0)
        gathered = source_table[table_index]
        elem_frame = jnp.take_along_axis(gathered, to_element[:, None, :], axis=2).reshape(
            elem_cap, 6, functionals, trace_len
        )
        upper_terms = element_terms(elem_frame[:top_live], elem_mats[:top_live], trace_len).astype(
            jnp.bfloat16
        )
        padding = jnp.zeros((elem_cap - top_live,) + upper_terms.shape[1:], jnp.bfloat16)
        elem_terms = jnp.concatenate([upper_terms, padding], axis=0)
        elem_terms = jnp.where(
            live_rows[:, None, None, None], elem_terms, jnp.zeros_like(elem_terms)
        )
        face_terms = jnp.take_along_axis(
            elem_terms.reshape(incidences, functionals, trace_len), to_face[:, None, :], axis=2
        )
        buckets = []
        for picked, present in zip(send_picks, send_present):
            chosen_rows = face_terms[picked]
            buckets.append(
                jnp.where(present[:, None, None], chosen_rows, jnp.zeros_like(chosen_rows))
            )
        arrived = deliver(buckets, False)
        summed = jax.ops.segment_sum(
            face_terms.astype(jnp.float32), home_ids, num_segments=face_dev
        )
        for face_ids, arrived_piece in zip(recv_faces, arrived):
            summed = summed + jax.ops.segment_sum(
                arrived_piece.astype(jnp.float32), face_ids, num_segments=face_dev
            )
        residual = (rhs.astype(jnp.float32) - summed).astype(jnp.bfloat16)
        traces = traces + jnp.einsum(
            "fni,fij->fnj", residual, face_blocks, preferred_element_type=jnp.float32
        )
    return traces


def solution(mesh):
    in_specs = (P("elem", None, None), P("elem", None, None), P("elem", None, None), P(), P(), P())
    out_specs = P("elem", None, None)
    return jax.shard_map(
        per_device, mesh=mesh, in_specs=in_specs, out_specs=out_specs, check_vma=False
    )
```

profile of v0, /device:TPU:25, one launch (start us, length us, event | category | flops | bytes accessed | tf_op | source)
XLA Modules:
  0.0 555.8 jit_solution(17241728358445328683)
XLA Ops:
  9.2 3.7 collective-permute-start.2
  18.5 4.0 collective-permute-start.1
  37.0 8.5 %slice.18 = bf16[9,750,750]{2,1,0:T(8,128)(2,1)} slice(bf16[12,750,750]{2,1,0:T(8,128)(2,1)} %param.10), slice={[0:9], [0:750], [0:750]} | slice | bytes 20250000 | tf_op jit(solution)/shard_map/slice | solution.py:138
  45.4 17.1 %reshape.1200 = bf16[9,6,125,6,125]{4,3,2,1,0:T(8,128)(2,1)} reshape(bf16[9,750,750]{2,1,0:T(8,128)(2,1)} %slice.18) | data formatting | bytes 20250000 | tf_op jit(solution)/shard_map/reshape | solution.py:89
  64.1 2.6 copy.238
  66.7 97.9 %gather_fusion.20 = bf16[9000,16]{1,0:T(8,128)(2,1)} fusion(bf16[72,16,125]{1,0,2:T(8,128)(2,1)S(1)} %copy.238, s32[9000]{0:T(1024)S(1)} %reshape.1464), kind=kCustom, calls=%fused_computation.clone | custom fusion | bytes 648000 | tf_op jit(solution)/shard_map/jit(take_along_axis)/gather | solution.py:135
  167.3 6.5 %fusion.16 = bf16[9,6,16,125]{3,2,1,0:T(8,128)(2,1)S(1)} fusion(bf16[9,6,16,125,1]{3,2,1,4,0:T(8,128)(2,1)S(1)} %bitcast.124, bf16[9,6,125,6,125]{4,3,2,1,0:T(8,128)(2,1)} %reshape.1200), kind=kOutput, calls=%fused_computation.39 | convolution fusion | flops 162108000 | bytes 10557000 | tf_op jit(solution)/shard_map/akni,akilj->alnj/dot_general | solution.py:90
  174.6 2.6 copy.242
  177.2 97.9 %gather_fusion.21 = bf16[9000,16]{1,0:T(8,128)(2,1)} fusion(bf16[72,16,125]{1,0,2:T(8,128)(2,1)S(1)} %copy.242, s32[9000]{0:T(1024)S(1)} %reshape.1469), kind=kCustom, calls=%fused_computation.1.clone | custom fusion | bytes 648000 | tf_op jit(solution)/shard_map/jit(take_along_axis)/gather | solution.py:146
  278.4 3.4 collective-permute-start.5
  282.5 3.1 collective-permute-start.6
  286.2 4.8 collective-permute-start.7
  293.7 3.6 scatter_fusion
  300.8 3.6 collective-permute-start.8
  308.0 4.2 collective-permute-start.10
  312.3 5.2 collective-permute-start.9
  319.7 2.6 copy.247
  322.3 97.9 %gather_fusion.22 = bf16[9000,16]{1,0:T(8,128)(2,1)} fusion(bf16[72,16,125]{1,0,2:T(8,128)(2,1)S(1)} %copy.247, s32[9000]{0:T(1024)S(1)} %reshape.1464), kind=kCustom, calls=%fused_computation.2.clone | custom fusion | bytes 648000 | tf_op jit(solution)/shard_map/jit(take_along_axis)/gather | solution.py:135
  422.8 6.5 %fusion.19 = bf16[9,6,16,125]{3,2,1,0:T(8,128)(2,1)S(1)} fusion(bf16[9,6,16,125,1]{3,2,1,4,0:T(8,128)(2,1)S(1)} %bitcast.123, bf16[9,6,125,6,125]{4,3,2,1,0:T(8,128)(2,1)} %reshape.1200), kind=kOutput, calls=%fused_computation.40 | convolution fusion | flops 162108000 | bytes 10557000 | tf_op jit(solution)/shard_map/akni,akilj->alnj/dot_general | solution.py:90
  431.3 97.9 %gather_fusion.23 = bf16[9000,16]{1,0:T(8,128)(2,1)} fusion(bf16[72,16,125]{1,0,2:T(8,128)(2,1)S(1)} %copy.251, s32[9000]{0:T(1024)S(1)} %reshape.1469), kind=kCustom, calls=%fused_computation.3.clone | custom fusion | bytes 648000 | tf_op jit(solution)/shard_map/jit(take_along_axis)/gather | solution.py:146
  536.3 3.1 collective-permute-start.14
  539.5 2.4 collective-permute-start.12
  542.0 7.2 %collective-permute-start.15 = (bf16[4,16,125]{2,1,0:T(8,128)(2,1)S(1)}, bf16[4,16,125]{2,1,0:T(8,128)(2,1)S(1)}, u32[]{:S(2)}, u32[]{:S(2)}) collective-permute-start(bf16[4,16,125]{2,1,0:T(8,128)(2,1)S(1)} %broadcast_select_fusion), channel_id=1, source_target_pairs={{2,0},{3,1},{4,2},{5,3},{6,4},{7,5},{8,6},{9,7},{10,8},{11,9},{12,... | collective-permute-start | bytes 48008 | tf_op jit(solution)/shard_map/ppermute | solution.py:17
  549.3 3.6 scatter_fusion.3
  (249 shorter events, 64.7 us)
Async XLA Ops:
  0.0 299.2 %copy-start = (bf16[27,125,125]{2,1,0:T(8,128)(2,1)S(1)}, bf16[27,125,125]{2,1,0:T(8,128)(2,1)}, u32[]{:S(2)}) copy-start(bf16[27,125,125]{2,1,0:T(8,128)(2,1)} %param.11) | copy-start | bytes 2531254
  9.2 53.6 %collective-permute-start.2 = (bf16[4,16,125]{2,1,0:T(8,128)(2,1)S(1)}, bf16[4,16,125]{2,1,0:T(8,128)(2,1)S(1)}, u32[]{:S(2)}, u32[]{:S(2)}) collective-permute-start(bf16[4,16,125]{2,1,0:T(8,128)(2,1)S(1)} %gather_fusion.2), channel_id=1, source_target_pairs={{0,1},{1,2},{2,3},{3,4},{4,5},{5,6},{6,7},{7,8},{8,9},{9,10},{10,1... | collective-permute-start | bytes 48008 | tf_op jit(solution)/shard_map/ppermute | solution.py:17
  18.5 44.2 %collective-permute-start.1 = (bf16[4,16,125]{2,1,0:T(8,128)(2,1)S(1)}, bf16[4,16,125]{2,1,0:T(8,128)(2,1)S(1)}, u32[]{:S(2)}, u32[]{:S(2)}) collective-permute-start(bf16[4,16,125]{2,1,0:T(8,128)(2,1)S(1)} %gather_fusion.1), channel_id=1, source_target_pairs={{2,0},{3,1},{4,2},{5,3},{6,4},{7,5},{8,6},{9,7},{10,8},{11,9},{12,... | collective-permute-start | bytes 48008 | tf_op jit(solution)/shard_map/ppermute | solution.py:17
  23.2 39.5 %collective-permute-start = (bf16[4,16,125]{2,1,0:T(8,128)(2,1)S(1)}, bf16[4,16,125]{2,1,0:T(8,128)(2,1)S(1)}, u32[]{:S(2)}, u32[]{:S(2)}) collective-permute-start(bf16[4,16,125]{2,1,0:T(8,128)(2,1)S(1)} %gather_fusion), channel_id=1, source_target_pairs={{1,0},{2,1},{3,2},{4,3},{5,4},{6,5},{7,6},{8,7},{9,8},{10,9},{11,1... | collective-permute-start | bytes 48008 | tf_op jit(solution)/shard_map/ppermute | solution.py:17
  25.8 36.9 %collective-permute-start.3 = (bf16[4,16,125]{2,1,0:T(8,128)(2,1)S(1)}, bf16[4,16,125]{2,1,0:T(8,128)(2,1)S(1)}, u32[]{:S(2)}, u32[]{:S(2)}) collective-permute-start(bf16[4,16,125]{2,1,0:T(8,128)(2,1)S(1)} %gather_fusion.3), channel_id=1, source_target_pairs={{0,2},{1,3},{2,4},{3,5},{4,6},{5,7},{6,8},{7,9},{8,10},{9,11},{10,... | collective-permute-start | bytes 48008 | tf_op jit(solution)/shard_map/ppermute | solution.py:17
  35.1 258.7 %copy-start.6 = (s32[72]{0:T(128)}, s32[72]{0:T(128)S(1)}, u32[]{:S(2)}) copy-start(s32[72]{0:T(128)S(1)} %get-tuple-element.7) | copy-start | bytes 868
  35.3 243.0 %copy-start.10 = (pred[4]{0:T(512)(128)(4,1)}, pred[4]{0:T(512)(128)(4,1)S(1)}, u32[]{:S(2)}) copy-start(pred[4]{0:T(512)(128)(4,1)S(1)} %fusion.56) | copy-start | bytes 16
  35.6 246.8 %copy-start.12 = (pred[4]{0:T(512)(128)(4,1)}, pred[4]{0:T(512)(128)(4,1)S(1)}, u32[]{:S(2)}) copy-start(pred[4]{0:T(512)(128)(4,1)S(1)} %fusion.55) | copy-start | bytes 16
  35.8 250.3 %copy-start.8 = (pred[4]{0:T(512)(128)(4,1)}, pred[4]{0:T(512)(128)(4,1)S(1)}, u32[]{:S(2)}) copy-start(pred[4]{0:T(512)(128)(4,1)S(1)} %fusion.54) | copy-start | bytes 16
  36.0 255.6 %copy-start.14 = (pred[4]{0:T(512)(128)(4,1)}, pred[4]{0:T(512)(128)(4,1)S(1)}, u32[]{:S(2)}) copy-start(pred[4]{0:T(512)(128)(4,1)S(1)} %fusion.57) | copy-start | bytes 16
  36.8 137.0 %copy-start.16 = (pred[12]{0:T(512)(128)(4,1)}, pred[12]{0:T(512)(128)(4,1)S(1)}, u32[]{:S(2)}) copy-start(pred[12]{0:T(512)(128)(4,1)S(1)} %iota_compare_fusion.8) | copy-start | bytes 40
  278.4 19.7 %collective-permute-start.5 = (bf16[4,16,125]{2,1,0:T(8,128)(2,1)S(1)}, bf16[4,16,125]{2,1,0:T(8,128)(2,1)S(1)}, u32[]{:S(2)}, u32[]{:S(2)}) collective-permute-start(bf16[4,16,125]{2,1,0:T(8,128)(2,1)S(1)} %broadcast_select_fusion.5), channel_id=1, source_target_pairs={{0,2},{1,3},{2,4},{3,5},{4,6},{5,7},{6,8},{7,9},{8,10},{9,11},{10,... | collective-permute-start | bytes 48008 | tf_op jit(solution)/shard_map/ppermute | solution.py:17
  282.5 15.7 %collective-permute-start.6 = (bf16[4,16,125]{2,1,0:T(8,128)(2,1)S(1)}, bf16[4,16,125]{2,1,0:T(8,128)(2,1)S(1)}, u32[]{:S(2)}, u32[]{:S(2)}) collective-permute-start(bf16[4,16,125]{2,1,0:T(8,128)(2,1)S(1)} %broadcast_select_fusion.3), channel_id=1, source_target_pairs={{1,0},{2,1},{3,2},{4,3},{5,4},{6,5},{7,6},{8,7},{9,8},{10,9},{11,1... | collective-permute-start | bytes 48008 | tf_op jit(solution)/shard_map/ppermute | solution.py:17
  286.2 11.9 %collective-permute-start.7 = (bf16[4,16,125]{2,1,0:T(8,128)(2,1)S(1)}, bf16[4,16,125]{2,1,0:T(8,128)(2,1)S(1)}, u32[]{:S(2)}, u32[]{:S(2)}) collective-permute-start(bf16[4,16,125]{2,1,0:T(8,128)(2,1)S(1)} %broadcast_select_fusion.1), channel_id=1, source_target_pairs={{2,0},{3,1},{4,2},{5,3},{6,4},{7,5},{8,6},{9,7},{10,8},{11,9},{12,... | collective-permute-start | bytes 48008 | tf_op jit(solution)/shard_map/ppermute | solution.py:17
  291.7 5.7 %collective-permute-start.4 = (bf16[4,16,125]{2,1,0:T(8,128)(2,1)S(1)}, bf16[4,16,125]{2,1,0:T(8,128)(2,1)S(1)}, u32[]{:S(2)}, u32[]{:S(2)}) collective-permute-start(bf16[4,16,125]{2,1,0:T(8,128)(2,1)S(1)} %broadcast_select_fusion.7), channel_id=1, source_target_pairs={{0,1},{1,2},{2,3},{3,4},{4,5},{5,6},{6,7},{7,8},{8,9},{9,10},{10,1... | collective-permute-start | bytes 48008 | tf_op jit(solution)/shard_map/ppermute | solution.py:17
  293.7 126.4 %copy-start.4 = (s32[12]{0:T(128)}, s32[12]{0:T(128)S(1)}, u32[]{:S(2)}) copy-start(s32[12]{0:T(128)S(1)} %add_bitcast_fusion) | copy-start | bytes 148
  300.8 16.6 %collective-permute-start.8 = (bf16[4,16,125]{2,1,0:T(8,128)(2,1)S(1)}, bf16[4,16,125]{2,1,0:T(8,128)(2,1)S(1)}, u32[]{:S(2)}, u32[]{:S(2)}) collective-permute-start(bf16[4,16,125]{2,1,0:T(8,128)(2,1)S(1)} %gather_fusion.11), channel_id=1, source_target_pairs={{1,0},{2,1},{3,2},{4,3},{5,4},{6,5},{7,6},{8,7},{9,8},{10,9},{11,1... | collective-permute-start | bytes 48008 | tf_op jit(solution)/shard_map/ppermute | solution.py:17
  306.1 12.2 %collective-permute-start.11 = (bf16[4,16,125]{2,1,0:T(8,128)(2,1)S(1)}, bf16[4,16,125]{2,1,0:T(8,128)(2,1)S(1)}, u32[]{:S(2)}, u32[]{:S(2)}) collective-permute-start(bf16[4,16,125]{2,1,0:T(8,128)(2,1)S(1)} %gather_fusion.14), channel_id=1, source_target_pairs={{0,2},{1,3},{2,4},{3,5},{4,6},{5,7},{6,8},{7,9},{8,10},{9,11},{10,... | collective-permute-start | bytes 48008 | tf_op jit(solution)/shard_map/ppermute | solution.py:17
  308.0 10.3 %collective-permute-start.10 = (bf16[4,16,125]{2,1,0:T(8,128)(2,1)S(1)}, bf16[4,16,125]{2,1,0:T(8,128)(2,1)S(1)}, u32[]{:S(2)}, u32[]{:S(2)}) collective-permute-start(bf16[4,16,125]{2,1,0:T(8,128)(2,1)S(1)} %gather_fusion.13), channel_id=1, source_target_pairs={{0,1},{1,2},{2,3},{3,4},{4,5},{5,6},{6,7},{7,8},{8,9},{9,10},{10,1... | collective-permute-start | bytes 48008 | tf_op jit(solution)/shard_map/ppermute | solution.py:17
  312.3 6.1 %collective-permute-start.9 = (bf16[4,16,125]{2,1,0:T(8,128)(2,1)S(1)}, bf16[4,16,125]{2,1,0:T(8,128)(2,1)S(1)}, u32[]{:S(2)}, u32[]{:S(2)}) collective-permute-start(bf16[4,16,125]{2,1,0:T(8,128)(2,1)S(1)} %gather_fusion.12), channel_id=1, source_target_pairs={{2,0},{3,1},{4,2},{5,3},{6,4},{7,5},{8,6},{9,7},{10,8},{11,9},{12,... | collective-permute-start | bytes 48008 | tf_op jit(solution)/shard_map/ppermute | solution.py:17
  534.3 19.4 %collective-permute-start.13 = (bf16[4,16,125]{2,1,0:T(8,128)(2,1)S(1)}, bf16[4,16,125]{2,1,0:T(8,128)(2,1)S(1)}, u32[]{:S(2)}, u32[]{:S(2)}) collective-permute-start(bf16[4,16,125]{2,1,0:T(8,128)(2,1)S(1)} %broadcast_select_fusion.4), channel_id=1, source_target_pairs={{0,2},{1,3},{2,4},{3,5},{4,6},{5,7},{6,8},{7,9},{8,10},{9,11},{10,... | collective-permute-start | bytes 48008 | tf_op jit(solution)/shard_map/ppermute | solution.py:17
  536.3 17.4 %collective-permute-start.14 = (bf16[4,16,125]{2,1,0:T(8,128)(2,1)S(1)}, bf16[4,16,125]{2,1,0:T(8,128)(2,1)S(1)}, u32[]{:S(2)}, u32[]{:S(2)}) collective-permute-start(bf16[4,16,125]{2,1,0:T(8,128)(2,1)S(1)} %broadcast_select_fusion.2), channel_id=1, source_target_pairs={{1,0},{2,1},{3,2},{4,3},{5,4},{6,5},{7,6},{8,7},{9,8},{10,9},{11,1... | collective-permute-start | bytes 48008 | tf_op jit(solution)/shard_map/ppermute | solution.py:17
  539.5 13.4 %collective-permute-start.12 = (bf16[4,16,125]{2,1,0:T(8,128)(2,1)S(1)}, bf16[4,16,125]{2,1,0:T(8,128)(2,1)S(1)}, u32[]{:S(2)}, u32[]{:S(2)}) collective-permute-start(bf16[4,16,125]{2,1,0:T(8,128)(2,1)S(1)} %broadcast_select_fusion.6), channel_id=1, source_target_pairs={{0,1},{1,2},{2,3},{3,4},{4,5},{5,6},{6,7},{7,8},{8,9},{9,10},{10,1... | collective-permute-start | bytes 48008 | tf_op jit(solution)/shard_map/ppermute | solution.py:17
  542.0 11.7 %collective-permute-start.15 = (bf16[4,16,125]{2,1,0:T(8,128)(2,1)S(1)}, bf16[4,16,125]{2,1,0:T(8,128)(2,1)S(1)}, u32[]{:S(2)}, u32[]{:S(2)}) collective-permute-start(bf16[4,16,125]{2,1,0:T(8,128)(2,1)S(1)} %broadcast_select_fusion), channel_id=1, source_target_pairs={{2,0},{3,1},{4,2},{5,3},{6,4},{7,5},{8,6},{9,7},{10,8},{11,9},{12,... | collective-permute-start | bytes 48008 | tf_op jit(solution)/shard_map/ppermute | solution.py:17
  (10 other events, 650.8 us)
where the time goes:
time: 557 us; the launch traced here: 556 us
  local copies, waits for them, and re-layouts  459 us (82%)
  starting transfers between devices  54.3 us (10%)
  other arithmetic  25.8 us (5%)
  matrix products  15.1 us (3%)
    gather x7, local copies, waits for them, and re-layouts, per_device(): jnp.take_along_axis(elem_terms.reshape(incidences, functionals, trace_len...  201 us
    gather x7, local copies, waits for them, and re-layouts, per_device(): jnp.take_along_axis(gathered, to_element[:, None, :], axis=2)  201 us
    ppermute x16, starting transfers between devices, passed_along(): return lax.ppermute(block, axis, route)  54.3 us
    reshape x1, local copies, waits for them, and re-layouts, element_terms(): blocks = matrices.reshape(matrices.shape[0], 6, trace_len, 6, trace_len)  17.1 us
    dot_general x2, matrix products, element_terms(): jnp.einsum('akni,akilj->alnj', elem_frame, blocks, preferred_element_type...  13 us
  transfers between devices with their start and end apart: 16, of which 1 were waited for; matrix products, arithmetic and copies ran while one was open for 10% of the time, Pallas kernels for 0%

commit v1 on v0

v1 whole, which is shorter than its diff:
```python
import functools

import jax
import jax.numpy as jnp
import numpy as np
from jax import lax
from jax.experimental import pallas as pl
from jax.experimental.pallas import tpu as pltpu
from jax.sharding import PartitionSpec as P

COMP = 5
EDGE = 5
SLOT = 4
LANES = 128
SIB, CROSS, EVEN, ODD = range(4)


def orient_tables(edge_nodes, components):
    node_ids = np.arange(edge_nodes * edge_nodes)
    row_pos = node_ids // edge_nodes
    col_pos = node_ids % edge_nodes
    table_rows = []
    for orient_code in range(8):
        if orient_code & 4:
            first_pos, second_pos = (col_pos, row_pos)
        else:
            first_pos, second_pos = (row_pos, col_pos)
        if orient_code & 1:
            first_pos = edge_nodes - 1 - first_pos
        if orient_code & 2:
            second_pos = edge_nodes - 1 - second_pos
        moved_node = first_pos * edge_nodes + second_pos
        table_rows.append(
            np.concatenate(
                [
                    part_index * edge_nodes * edge_nodes + moved_node
                    for part_index in range(components)
                ]
            )
        )
    forward = np.stack(table_rows).astype(np.int32)
    backward = np.argsort(forward, axis=1).astype(np.int32)
    return (forward, backward)


def lane_tables(trace_len):
    forward, backward = orient_tables(EDGE, COMP)
    gap = LANES - trace_len
    spare = np.arange(trace_len, LANES)
    lanes = np.arange(LANES)
    into = np.zeros((6 * 8, LANES), np.int32)
    outof = np.zeros((6 * 8, LANES), np.int32)
    for k in range(6):
        for code in range(8):
            full = np.concatenate([forward[code], spare])
            into[k * 8 + code] = full[(lanes + gap * k) % LANES]
            full = np.concatenate([backward[code], spare])
            outof[k * 8 + code] = (full - gap * k) % LANES
    return into, outof


def swap_routes(devices):
    routes = [[(i, i ^ 1) for i in range(devices)]]
    for shift in (0, 2):
        route = []
        for i in range(devices):
            other = ((i - shift) ^ 2) + shift
            route.append((i, other if 0 <= i - shift and 0 <= other < devices else i ^ 1))
        routes.append(route)
    return routes


def partners(me):
    core = me & 1
    odd_chip = (me >> 1) & 1
    return (
        me ^ 1,
        me - 1 + 2 * core,
        me + 2 - 4 * odd_chip,
        me - 2 + 4 * odd_chip,
    )


def first_kernel(
    elem_cap, devices, faces, counts, rhs, blocks, traces, rounded, swap, even, odd, slots, found
):
    me = lax.axis_index("elem")
    face_dev, functionals, trace_len = rhs.shape
    for f in range(face_dev):
        value = jnp.dot(rhs[f], blocks[f], preferred_element_type=jnp.float32)
        traces[f] = jnp.zeros((functionals, LANES), jnp.float32)
        traces[f, :, :trace_len] = value
        rounded[f] = traces[f].astype(jnp.bfloat16)
    for group, device in enumerate(partners(me)):
        valid = (device >= 0) & (device < devices)
        safe = jnp.clip(device, 0, devices - 1)
        live = jnp.where(valid, counts[safe], 0)
        for r in range(SLOT):
            found[group * 8 + r] = 0

        def scan(e, rank):
            for k in range(6):
                local = faces[k, safe * elem_cap + e] - me * face_dev
                hit = (local >= 0) & (local < face_dev)
                found[group * 8 + rank] = local
                rank = rank + hit.astype(jnp.int32)
            return rank

        lax.fori_loop(0, live, scan, jnp.int32(0))
        for r in range(SLOT):
            slot = jnp.where(valid, found[group * 8 + r], 0)
            slots[group * SLOT + r] = jnp.where(valid, slot, face_dev)
            tile = rounded[slot]
            if group < 2:
                swap[group * SLOT + r] = tile
            elif group == EVEN:
                even[r] = tile
            else:
                odd[r] = tile


def second_kernel(
    elem_cap,
    faces,
    orient,
    counts,
    rounded,
    from_sib,
    from_even,
    from_odd,
    into,
    outof,
    mats,
    home,
    swap,
    even,
    odd,
    table,
    acc,
    rows,
    heads,
):
    me = lax.axis_index("elem")
    face_dev, functionals, _ = rounded.shape
    live = elem_cap - elem_cap // 4
    trace_len = mats.shape[1] // 6
    gap = LANES - trace_len
    spare = face_dev + 4 * SLOT
    core = me & 1
    odd_chip = (me >> 1) & 1

    table[:face_dev] = rounded[...]
    table[face_dev : face_dev + SLOT] = from_sib[:SLOT]
    crossing = jnp.broadcast_to((core ^ odd_chip) == 1, (SLOT, functionals, LANES))
    table[face_dev + SLOT : face_dev + 2 * SLOT] = jnp.where(
        crossing, from_even[SLOT:], from_odd[SLOT:]
    )
    table[face_dev + 2 * SLOT : face_dev + 3 * SLOT] = from_even[:SLOT]
    table[face_dev + 3 * SLOT : face_dev + 4 * SLOT] = from_odd[:SLOT]
    table[spare] = jnp.zeros((functionals, LANES), jnp.bfloat16)
    acc[...] = jnp.zeros_like(acc)

    heads[0] = face_dev + SLOT * jnp.where(odd_chip == 1, EVEN, ODD)
    heads[1] = face_dev + SLOT * jnp.where(core == 1, SIB, CROSS)
    heads[3] = face_dev + SLOT * jnp.where(core == 1, CROSS, SIB)
    heads[4] = face_dev + SLOT * jnp.where(odd_chip == 1, ODD, EVEN)
    count = counts[me]
    magic = (1 << 16) // face_dev + 1
    places = []
    codes = []
    for e in range(live):
        for k in range(6):
            rel = faces[k, me * elem_cap + e] - (me - 2) * face_dev
            used = e < count
            rel = jnp.where(used, rel, 2 * face_dev)
            owner = (rel * magic) >> 16
            head = heads[owner]
            heads[owner] = head + 1
            place = jnp.where(owner == 2, rel - 2 * face_dev, head)
            places.append(jnp.where(used, place, spare))
            codes.append(orient[k, me * elem_cap + e])

    lane = lax.broadcasted_iota(jnp.int32, (functionals, LANES), 1)
    for e in range(live):
        parts = []
        for k in range(6):
            tile = table[places[6 * e + k]].astype(jnp.float32)
            index = jnp.broadcast_to(
                into[pl.ds(k * 8 + codes[6 * e + k], 1), :], (functionals, LANES)
            )
            parts.append(jnp.take_along_axis(tile, index, axis=1, mode="promise_in_bounds"))
        for k in range(6):
            later = parts[k + 1] if k < 5 else jnp.zeros_like(parts[k])
            merged = jnp.where(lane < trace_len - gap * k, parts[k], later)
            rows[e, :, k * LANES : (k + 1) * LANES] = merged.astype(jnp.bfloat16)
    for e in range(live):
        terms = jnp.dot(
            rows[e, :, : 6 * trace_len], mats[e], preferred_element_type=jnp.float32
        )
        terms = jnp.concatenate(
            [terms, jnp.zeros((functionals, 6 * gap), jnp.float32)], axis=1
        ).astype(jnp.bfloat16).astype(jnp.float32)
        for k in range(6):
            tile = terms[:, k * LANES : (k + 1) * LANES]
            if k:
                before = terms[:, (k - 1) * LANES : k * LANES]
                tile = jnp.where(lane >= LANES - gap * k, before, tile)
            index = jnp.broadcast_to(
                outof[pl.ds(k * 8 + codes[6 * e + k], 1), :], (functionals, LANES)
            )
            tile = jnp.take_along_axis(tile, index, axis=1, mode="promise_in_bounds")
            place = places[6 * e + k]
            acc[place] = acc[place] + tile
    home[...] = acc[:face_dev]
    swap[...] = acc[face_dev : face_dev + 2 * SLOT].astype(jnp.bfloat16)
    even[...] = acc[face_dev + 2 * SLOT : face_dev + 3 * SLOT].astype(jnp.bfloat16)
    odd[...] = acc[face_dev + 3 * SLOT : face_dev + 4 * SLOT].astype(jnp.bfloat16)


def third_kernel(slots, home, from_sib, from_even, from_odd, rhs, blocks, traces, out, acc):
    me = lax.axis_index("elem")
    face_dev, functionals, trace_len = rhs.shape
    core = me & 1
    odd_chip = (me >> 1) & 1
    acc[:face_dev] = home[...]
    crossing = jnp.broadcast_to((core ^ odd_chip) == 1, (functionals, LANES))
    for r in range(SLOT):
        arrived = [
            from_sib[r],
            jnp.where(crossing, from_even[SLOT + r], from_odd[SLOT + r]),
            from_even[r],
            from_odd[r],
        ]
        for group in range(4):
            place = slots[group * SLOT + r]
            acc[place] = acc[place] + arrived[group].astype(jnp.float32)
    for f in range(face_dev):
        residual = rhs[f].astype(jnp.float32) - acc[f, :, :trace_len]
        update = jnp.dot(
            residual.astype(jnp.bfloat16), blocks[f], preferred_element_type=jnp.float32
        )
        out[f] = traces[f, :, :trace_len] + update


def exchange(routes, swap, even, odd):
    sibling, even_chips, odd_chips = routes
    got = lax.ppermute(swap, "elem", sibling)
    relay = got[SLOT:]
    from_even = lax.ppermute(jnp.concatenate([even, relay]), "elem", even_chips)
    from_odd = lax.ppermute(jnp.concatenate([odd, relay]), "elem", odd_chips)
    return got, from_even, from_odd


def per_device(devices, elem_mats, face_blocks, rhs, elem_faces, orient, counts):
    elem_cap, dof, _ = elem_mats.shape
    face_dev, functionals, trace_len = rhs.shape
    live = elem_cap - elem_cap // 4
    routes = swap_routes(devices)
    faces = elem_faces.T
    codes = orient.T
    into, outof = lane_tables(trace_len)
    vmem = pl.BlockSpec(memory_space=pltpu.VMEM)
    smem = pl.BlockSpec(memory_space=pltpu.SMEM)

    def tiles(count, kind):
        return jax.ShapeDtypeStruct((count, functionals, LANES), kind)

    params = pltpu.CompilerParams(vmem_limit_bytes=48 << 20)
    traces, rounded, swap, even, odd, slots = pl.pallas_call(
        functools.partial(first_kernel, elem_cap, devices),
        out_shape=(
            tiles(face_dev, jnp.float32),
            tiles(face_dev, jnp.bfloat16),
            tiles(2 * SLOT, jnp.bfloat16),
            tiles(SLOT, jnp.bfloat16),
            tiles(SLOT, jnp.bfloat16),
            jax.ShapeDtypeStruct((4 * SLOT,), jnp.int32),
        ),
        in_specs=[smem, smem, vmem, vmem],
        out_specs=(vmem, vmem, vmem, vmem, vmem, smem),
        scratch_shapes=[pltpu.SMEM((32,), jnp.int32)],
        compiler_params=params,
        name="first_sweep",
    )(faces, counts, rhs, face_blocks)
    from_sib, from_even, from_odd = exchange(routes, swap, even, odd)
    home, swap, even, odd = pl.pallas_call(
        functools.partial(second_kernel, elem_cap),
        out_shape=(
            tiles(face_dev, jnp.float32),
            tiles(2 * SLOT, jnp.bfloat16),
            tiles(SLOT, jnp.bfloat16),
            tiles(SLOT, jnp.bfloat16),
        ),
        in_specs=[smem, smem, smem] + [vmem] * 7,
        out_specs=(vmem,) * 4,
        scratch_shapes=[
            pltpu.VMEM((face_dev + 4 * SLOT + 1, functionals, LANES), jnp.bfloat16),
            pltpu.VMEM((face_dev + 4 * SLOT + 1, functionals, LANES), jnp.float32),
            pltpu.VMEM((live, functionals, 6 * LANES), jnp.bfloat16),
            pltpu.SMEM((8,), jnp.int32),
        ],
        compiler_params=params,
        name="element_terms",
    )(
        faces,
        codes,
        counts,
        rounded,
        from_sib,
        from_even,
        from_odd,
        jnp.asarray(into),
        jnp.asarray(outof),
        elem_mats,
    )
    from_sib, from_even, from_odd = exchange(routes, swap, even, odd)
    return pl.pallas_call(
        third_kernel,
        out_shape=jax.ShapeDtypeStruct(rhs.shape, jnp.float32),
        in_specs=[smem] + [vmem] * 7,
        out_specs=vmem,
        scratch_shapes=[pltpu.VMEM((face_dev + 1, functionals, LANES), jnp.float32)],
        compiler_params=params,
        name="last_update",
    )(slots, home, from_sib, from_even, from_odd, rhs, face_blocks, traces)


def solution(mesh):
    in_specs = (P("elem", None, None), P("elem", None, None), P("elem", None, None), P(), P(), P())
    out_specs = P("elem", None, None)
    return jax.shard_map(
        functools.partial(per_device, mesh.shape["elem"]),
        mesh=mesh,
        in_specs=in_specs,
        out_specs=out_specs,
        check_vma=False,
    )
```

time: 557 us -> 31.5 us (0.06)
  the two profiles are of different devices: /device:TPU:25 before, /device:TPU:16 now
where the time goes in v1:
time: 31.5 us; the launch traced here: 31.1 us
  Pallas kernels  10.6 us (34%)
  waiting for transfers between devices  9.43 us (30%)
  local copies, waits for them, and re-layouts  5.62 us (18%)
  starting transfers between devices  5.38 us (17%)
    pallas_call x1, Pallas kernels, per_device(): pl.pallas_call(functools.partial(second_kernel, elem_cap), out_shape=(til...  6.65 us
    ppermute x2, waiting for transfers between devices, exchange(): from_odd = lax.ppermute(jnp.concatenate([odd, relay]), 'elem', odd_chips)  6.35 us
    unnamed x18, local copies, waits for them, and re-layouts  5.61 us
    ppermute x2, starting transfers between devices, exchange(): from_odd = lax.ppermute(jnp.concatenate([odd, relay]), 'elem', odd_chips)  4.44 us
    ppermute x2, waiting for transfers between devices, exchange(): got = lax.ppermute(swap, 'elem', sibling)  2.39 us
    pallas_call x1, Pallas kernels, per_device(): pl.pallas_call(functools.partial(first_kernel, elem_cap, devices), out_sh...  2.31 us
    pallas_call x1, Pallas kernels, per_device(): pl.pallas_call(third_kernel, out_shape=jax.ShapeDtypeStruct(rhs.shape, jn...  1.64 us
    ppermute x2, starting transfers between devices, exchange(): from_even = lax.ppermute(jnp.concatenate([even, relay]), 'elem', even_chips)  0.8 us
  transfers between devices with their start and end apart: 6, of which 5 were waited for; matrix products, arithmetic and copies ran while one was open for 0% of the time, Pallas kernels for 0%

profile of v1, /device:TPU:16, one launch (start us, length us, event | category | flops | bytes accessed | tf_op | source)
XLA Modules:
  0.0 31.1 jit_solution(5000215481989377649)
XLA Ops:
  0.0 1.2 %copy-done = bf16[27,125,125]{2,1,0:T(8,128)(2,1)S(1)} copy-done((bf16[27,125,125]{2,1,0:T(8,128)(2,1)S(1)}, bf16[27,125,125]{2,1,0:T(8,128)(2,1)}, u32[]{:S(2)}) %copy-start) | copy-done | bytes 843774
  1.2 0.9 %copy-done.2 = bf16[27,16,125]{2,1,0:T(8,128)(2,1)S(1)} copy-done((bf16[27,16,125]{2,1,0:T(8,128)(2,1)S(1)}, bf16[27,16,125]{2,1,0:T(8,128)(2,1)}, u32[]{:S(2)}) %copy-start.2) | copy-done | bytes 108024
  2.1 0.7 %copy-done.4 = s32[384,6]{0,1:T(8,128)S(1)} copy-done((s32[384,6]{0,1:T(8,128)S(1)}, s32[384,6]{0,1:T(8,128)}, u32[]{:S(2)}) %copy-start.4) | copy-done | bytes 9240
  2.8 0.7 %copy-done.8 = s32[32]{0:T(128)S(1)} copy-done((s32[32]{0:T(128)S(1)}, s32[32]{0:T(128)}, u32[]{:S(2)}) %copy-start.8) | copy-done | bytes 152
  3.4 2.3 %first_sweep.1 = (f32[27,16,128]{2,1,0:T(8,128)S(1)}, bf16[27,16,128]{2,1,0:T(8,128)(2,1)S(1)}, bf16[8,16,128]{2,1,0:T(8,128)(2,1)S(1)}, bf16[4,16,128]{2,1,0:T(...) custom-call(s32[6,384]{1,0:T(8,128)S(1)} %bitcast.2, s32[32]{0:T(128)S(1)} %copy-done.8, ...), custom_call_target="tpu_custom_call" | custom-call | tf_op jit(solution)/shard_map/first_sweep/pallas_call | solution.py:269
  5.8 0.1 collective-permute-start
  5.8 1.2 %collective-permute-done.from_sib = bf16[8,16,128]{2,1,0:T(8,128)(2,1)S(1)} collective-permute-done((bf16[8,16,128]{2,1,0:T(8,128)(2,1)S(1)}, bf16[8,16,128]{2,1,0:T(8,128)(2,1)S(1)}, u32[]{:S(2)}, u32[]{:S(2)}) %collective-permute-start) | collective-permute-done | bytes 32800 | tf_op jit(solution)/shard_map/ppermute | solution.py:247
  7.0 2.6 %collective-permute-start.2 = (bf16[8,16,128]{2,1,0:T(8,128)(2,1)S(1)}, bf16[8,16,128]{2,1,0:T(8,128)(2,1)S(1)}, u32[]{:S(2)}, u32[]{:S(2)}) collective-permute-start(bf16[8,16,128]{2,1,0:T(8,128)(2,1)S(1)} %get-tuple-element.27), channel_id=1, source_target_pairs={{0,1},{1,0},{2,4},{3,5},{4,2},{5,3},{6,8},{7,9},{8,6},{9,7},{10,12... | collective-permute-start | bytes 98312 | tf_op jit(solution)/shard_map/ppermute | solution.py:250
  9.6 0.5 %collective-permute-start.1 = (bf16[8,16,128]{2,1,0:T(8,128)(2,1)S(1)}, bf16[8,16,128]{2,1,0:T(8,128)(2,1)S(1)}, u32[]{:S(2)}, u32[]{:S(2)}) collective-permute-start(bf16[8,16,128]{2,1,0:T(8,128)(2,1)S(1)} %get-tuple-element.28), channel_id=1, source_target_pairs={{0,2},{1,3},{2,0},{3,1},{4,6},{5,7},{6,4},{7,5},{8,10},{9,11},{10,... | collective-permute-start | bytes 98312 | tf_op jit(solution)/shard_map/ppermute | solution.py:249
  10.1 2.7 %collective-permute-done.2.from_odd = bf16[8,16,128]{2,1,0:T(8,128)(2,1)S(1)} collective-permute-done((bf16[8,16,128]{2,1,0:T(8,128)(2,1)S(1)}, bf16[8,16,128]{2,1,0:T(8,128)(2,1)S(1)}, u32[]{:S(2)}, u32[]{:S(2)}) %collective-permute-start.2) | collective-permute-done | bytes 32800 | tf_op jit(solution)/shard_map/ppermute | solution.py:250
  12.8 0.7 %collective-permute-done.1.from_even = bf16[8,16,128]{2,1,0:T(8,128)(2,1)S(1)} collective-permute-done((bf16[8,16,128]{2,1,0:T(8,128)(2,1)S(1)}, bf16[8,16,128]{2,1,0:T(8,128)(2,1)S(1)}, u32[]{:S(2)}, u32[]{:S(2)}) %collective-permute-start.1) | collective-permute-done | bytes 32800 | tf_op jit(solution)/shard_map/ppermute | solution.py:249
  13.5 0.7 %copy-done.5 = s32[48,128]{1,0:T(8,128)S(1)} copy-done((s32[48,128]{1,0:T(8,128)S(1)}, s32[48,128]{1,0:T(8,128)}, u32[]{:S(2)}) %copy-start.5) | copy-done | bytes 24600
  14.2 0.7 %copy-done.6 = s32[48,128]{1,0:T(8,128)S(1)} copy-done((s32[48,128]{1,0:T(8,128)S(1)}, s32[48,128]{1,0:T(8,128)}, u32[]{:S(2)}) %copy-start.6) | copy-done | bytes 24600
  15.0 0.7 %copy-done.7 = s32[384,6]{0,1:T(8,128)S(1)} copy-done((s32[384,6]{0,1:T(8,128)S(1)}, s32[384,6]{0,1:T(8,128)}, u32[]{:S(2)}) %copy-start.7) | copy-done | bytes 9240
  15.7 6.6 %element_terms.1 = (f32[27,16,128]{2,1,0:T(8,128)S(1)}, bf16[8,16,128]{2,1,0:T(8,128)(2,1)S(1)}, bf16[4,16,128]{2,1,0:T(8,128)(2,1)S(1)}, bf16[4,16,128]{2,1,0:T(8,128)(2,1)S(1)}) custom-call(s32[6,384]{1,0:T(8,128)S(1)} %bitcast.3, s32[6,384]{1,0:T(8,128)S(1)} %bitcast.4, s32[32]{0:T(128)S(1)} %copy-done.8, ...), custom_call_target="tpu_custom_call" | custom-call | tf_op jit(solution)/shard_map/element_terms/pallas_call | solution.py:286
  22.3 0.1 collective-permute-start.3
  22.4 1.2 %collective-permute-done.3.from_sib = bf16[8,16,128]{2,1,0:T(8,128)(2,1)S(1)} collective-permute-done((bf16[8,16,128]{2,1,0:T(8,128)(2,1)S(1)}, bf16[8,16,128]{2,1,0:T(8,128)(2,1)S(1)}, u32[]{:S(2)}, u32[]{:S(2)}) %collective-permute-start.3) | collective-permute-done | bytes 32800 | tf_op jit(solution)/shard_map/ppermute | solution.py:247
  23.6 1.9 %collective-permute-start.5 = (bf16[8,16,128]{2,1,0:T(8,128)(2,1)S(1)}, bf16[8,16,128]{2,1,0:T(8,128)(2,1)S(1)}, u32[]{:S(2)}, u32[]{:S(2)}) collective-permute-start(bf16[8,16,128]{2,1,0:T(8,128)(2,1)S(1)} %get-tuple-element.25), channel_id=1, source_target_pairs={{0,1},{1,0},{2,4},{3,5},{4,2},{5,3},{6,8},{7,9},{8,6},{9,7},{10,12... | collective-permute-start | bytes 98312 | tf_op jit(solution)/shard_map/ppermute | solution.py:250
  25.5 0.3 collective-permute-start.4
  25.8 3.7 %collective-permute-done.5.from_odd = bf16[8,16,128]{2,1,0:T(8,128)(2,1)S(1)} collective-permute-done((bf16[8,16,128]{2,1,0:T(8,128)(2,1)S(1)}, bf16[8,16,128]{2,1,0:T(8,128)(2,1)S(1)}, u32[]{:S(2)}, u32[]{:S(2)}) %collective-permute-start.5) | collective-permute-done | bytes 32800 | tf_op jit(solution)/shard_map/ppermute | solution.py:250
  29.4 0.0 collective-permute-done.4.from_even
  29.4 0.0 copy-done.1
  29.4 0.0 copy-done.3
  29.5 1.6 %last_update.1 = f32[27,16,125]{2,1,0:T(8,128)} custom-call(s32[16]{0:T(128)S(1)} %get-tuple-element.15.slots, f32[27,16,128]{2,1,0:T(8,128)S(1)} %get-tuple-element.20.home, bf16[8,16,128]{2,1,0:T(8,128)(2,1)S(1)} %collective-permute-done.3.from_sib, bf16[8,16,128]{2,1,0:T(8,128)(2,1)S(1)} %collective-permute-done.4.from_even, ...), custom_call_target="tpu_custom_call" | custom-call | tf_op jit(solution)/shard_map/last_update/pallas_call | solution.py:317
  (13 shorter events, 0.0 us)
Async XLA Ops:
  0.0 1.2 %copy-start = (bf16[27,125,125]{2,1,0:T(8,128)(2,1)S(1)}, bf16[27,125,125]{2,1,0:T(8,128)(2,1)}, u32[]{:S(2)}) copy-start(bf16[27,125,125]{2,1,0:T(8,128)(2,1)} %blocks.3) | copy-start | bytes 2531254
  1.2 0.9 %copy-start.2 = (bf16[27,16,125]{2,1,0:T(8,128)(2,1)S(1)}, bf16[27,16,125]{2,1,0:T(8,128)(2,1)}, u32[]{:S(2)}) copy-start(bf16[27,16,125]{2,1,0:T(8,128)(2,1)} %rhs.3) | copy-start | bytes 324004
  2.1 0.7 %copy-start.4 = (s32[384,6]{0,1:T(8,128)S(1)}, s32[384,6]{0,1:T(8,128)}, u32[]{:S(2)}) copy-start(s32[384,6]{0,1:T(8,128)} %param.11) | copy-start | bytes 27652
  2.8 0.7 %copy-start.8 = (s32[32]{0:T(128)S(1)}, s32[32]{0:T(128)}, u32[]{:S(2)}) copy-start(s32[32]{0:T(128)} %counts.3) | copy-start | bytes 388
  3.4 26.0 %copy-start.1 = (bf16[27,125,125]{2,1,0:T(8,128)(2,1)S(1)}, bf16[27,125,125]{2,1,0:T(8,128)(2,1)}, u32[]{:S(2)}) copy-start(bf16[27,125,125]{2,1,0:T(8,128)(2,1)} %blocks.3) | copy-start | bytes 2531254
  3.4 26.0 %copy-start.3 = (bf16[27,16,125]{2,1,0:T(8,128)(2,1)S(1)}, bf16[27,16,125]{2,1,0:T(8,128)(2,1)}, u32[]{:S(2)}) copy-start(bf16[27,16,125]{2,1,0:T(8,128)(2,1)} %rhs.3) | copy-start | bytes 324004
  5.8 1.3 %collective-permute-start = (bf16[8,16,128]{2,1,0:T(8,128)(2,1)S(1)}, bf16[8,16,128]{2,1,0:T(8,128)(2,1)S(1)}, u32[]{:S(2)}, u32[]{:S(2)}) collective-permute-start(bf16[8,16,128]{2,1,0:T(8,128)(2,1)S(1)} %get-tuple-element.17), channel_id=1, source_target_pairs={{0,1},{1,0},{2,3},{3,2},{4,5},{5,4},{6,7},{7,6},{8,9},{9,8},{10,11... | collective-permute-start | bytes 98312 | tf_op jit(solution)/shard_map/ppermute | solution.py:247
  7.0 5.8 %collective-permute-start.2 = (bf16[8,16,128]{2,1,0:T(8,128)(2,1)S(1)}, bf16[8,16,128]{2,1,0:T(8,128)(2,1)S(1)}, u32[]{:S(2)}, u32[]{:S(2)}) collective-permute-start(bf16[8,16,128]{2,1,0:T(8,128)(2,1)S(1)} %get-tuple-element.27), channel_id=1, source_target_pairs={{0,1},{1,0},{2,4},{3,5},{4,2},{5,3},{6,8},{7,9},{8,6},{9,7},{10,12... | collective-permute-start | bytes 98312 | tf_op jit(solution)/shard_map/ppermute | solution.py:250
  9.6 3.9 %collective-permute-start.1 = (bf16[8,16,128]{2,1,0:T(8,128)(2,1)S(1)}, bf16[8,16,128]{2,1,0:T(8,128)(2,1)S(1)}, u32[]{:S(2)}, u32[]{:S(2)}) collective-permute-start(bf16[8,16,128]{2,1,0:T(8,128)(2,1)S(1)} %get-tuple-element.28), channel_id=1, source_target_pairs={{0,2},{1,3},{2,0},{3,1},{4,6},{5,7},{6,4},{7,5},{8,10},{9,11},{10,... | collective-permute-start | bytes 98312 | tf_op jit(solution)/shard_map/ppermute | solution.py:249
  13.5 0.7 %copy-start.5 = (s32[48,128]{1,0:T(8,128)S(1)}, s32[48,128]{1,0:T(8,128)}, u32[]{:S(2)}) copy-start(s32[48,128]{1,0:T(8,128)} %constant.5.clone.outof) | copy-start | bytes 73732
  14.2 0.7 %copy-start.6 = (s32[48,128]{1,0:T(8,128)S(1)}, s32[48,128]{1,0:T(8,128)}, u32[]{:S(2)}) copy-start(s32[48,128]{1,0:T(8,128)} %constant.4.clone.into) | copy-start | bytes 73732
  15.0 0.7 %copy-start.7 = (s32[384,6]{0,1:T(8,128)S(1)}, s32[384,6]{0,1:T(8,128)}, u32[]{:S(2)}) copy-start(s32[384,6]{0,1:T(8,128)} %param.12) | copy-start | bytes 27652
  22.3 1.3 %collective-permute-start.3 = (bf16[8,16,128]{2,1,0:T(8,128)(2,1)S(1)}, bf16[8,16,128]{2,1,0:T(8,128)(2,1)S(1)}, u32[]{:S(2)}, u32[]{:S(2)}) collective-permute-start(bf16[8,16,128]{2,1,0:T(8,128)(2,1)S(1)} %get-tuple-element.21), channel_id=1, source_target_pairs={{0,1},{1,0},{2,3},{3,2},{4,5},{5,4},{6,7},{7,6},{8,9},{9,8},{10,11... | collective-permute-start | bytes 98312 | tf_op jit(solution)/shard_map/ppermute | solution.py:247
  23.6 5.8 %collective-permute-start.5 = (bf16[8,16,128]{2,1,0:T(8,128)(2,1)S(1)}, bf16[8,16,128]{2,1,0:T(8,128)(2,1)S(1)}, u32[]{:S(2)}, u32[]{:S(2)}) collective-permute-start(bf16[8,16,128]{2,1,0:T(8,128)(2,1)S(1)} %get-tuple-element.25), channel_id=1, source_target_pairs={{0,1},{1,0},{2,4},{3,5},{4,2},{5,3},{6,8},{7,9},{8,6},{9,7},{10,12... | collective-permute-start | bytes 98312 | tf_op jit(solution)/shard_map/ppermute | solution.py:250
  25.5 3.9 %collective-permute-start.4 = (bf16[8,16,128]{2,1,0:T(8,128)(2,1)S(1)}, bf16[8,16,128]{2,1,0:T(8,128)(2,1)S(1)}, u32[]{:S(2)}, u32[]{:S(2)}) collective-permute-start(bf16[8,16,128]{2,1,0:T(8,128)(2,1)S(1)} %get-tuple-element.26), channel_id=1, source_target_pairs={{0,2},{1,3},{2,0},{3,1},{4,6},{5,7},{6,4},{7,5},{8,10},{9,11},{10,... | collective-permute-start | bytes 98312 | tf_op jit(solution)/shard_map/ppermute | solution.py:249

commit v2 on v1

v2 whole, which is shorter than its diff:
```python
import functools

import jax
import jax.numpy as jnp
import numpy as np
from jax import lax
from jax.experimental import pallas as pl
from jax.experimental.pallas import tpu as pltpu
from jax.sharding import PartitionSpec as P

COMP = 5
EDGE = 5
SLOT = 4
LANES = 128
SIB, EVEN, ODD, CROSS = range(4)


def orient_tables(edge_nodes, components):
    node_ids = np.arange(edge_nodes * edge_nodes)
    row_pos = node_ids // edge_nodes
    col_pos = node_ids % edge_nodes
    table_rows = []
    for orient_code in range(8):
        if orient_code & 4:
            first_pos, second_pos = (col_pos, row_pos)
        else:
            first_pos, second_pos = (row_pos, col_pos)
        if orient_code & 1:
            first_pos = edge_nodes - 1 - first_pos
        if orient_code & 2:
            second_pos = edge_nodes - 1 - second_pos
        moved_node = first_pos * edge_nodes + second_pos
        table_rows.append(
            np.concatenate(
                [
                    part_index * edge_nodes * edge_nodes + moved_node
                    for part_index in range(components)
                ]
            )
        )
    forward = np.stack(table_rows).astype(np.int32)
    backward = np.argsort(forward, axis=1).astype(np.int32)
    return (forward, backward)


def window_rows(trace_len):
    dof = 6 * trace_len
    for height in range(trace_len, dof):
        last = dof - height
        starts = [min(trace_len * k // 16 * 16, last) for k in range(6)]
        if last % 16 == 0 and all(
            start + height >= trace_len * (k + 1) for k, start in enumerate(starts)
        ):
            return height, last
    return dof, 0


def lane_tables(trace_len):
    forward, backward = orient_tables(EDGE, COMP)
    gap = LANES - trace_len
    spare = np.arange(trace_len, LANES)
    lanes = np.arange(LANES)
    _, last = window_rows(trace_len)
    into = np.zeros((6 * 8, LANES), np.int32)
    window = np.zeros((6 * 8, LANES), np.int32)
    outof = np.zeros((6 * 8, LANES), np.int32)
    for k in range(6):
        start = min(trace_len * k // 16 * 16, last)
        for code in range(8):
            full = np.concatenate([forward[code], spare])
            into[k * 8 + code] = full[(lanes + gap * k) % LANES]
            window[k * 8 + code] = full[(lanes - (trace_len * k - start)) % LANES]
            full = np.concatenate([backward[code], spare])
            outof[k * 8 + code] = (full - gap * k) % LANES
    return np.stack([into, window, outof])


def swap_routes(devices):
    routes = [[(i, i ^ 1) for i in range(devices)]]
    for shift in (0, 2):
        route = []
        for i in range(devices):
            other = ((i - shift) ^ 3) + shift
            route.append((i, other if i >= shift and other < devices else i ^ 1))
        routes.append(route)
    return routes


def partners(me):
    core = me & 1
    odd_chip = (me >> 1) & 1
    return (
        me ^ 1,
        me + 2 - 4 * odd_chip,
        me - 2 + 4 * odd_chip,
        me - 1 + 2 * core,
    )


def arrivals(me, from_sib, from_even, from_odd):
    shape = from_sib.shape[1:]
    by_even = jnp.broadcast_to(((me ^ (me >> 1)) & 1) == 1, shape)
    return [
        [from_sib[r] for r in range(SLOT)],
        [from_even[SLOT + r] for r in range(SLOT)],
        [from_odd[SLOT + r] for r in range(SLOT)],
        [jnp.where(by_even, from_even[r], from_odd[r]) for r in range(SLOT)],
    ]


def start_all(pairs, sems):
    copies = [
        pltpu.make_async_copy(src, dst, sems.at[i]) for i, (src, dst) in enumerate(pairs)
    ]
    for copy in copies:
        copy.start()
    return copies


def permuted(tile, index):
    index = jnp.broadcast_to(index, tile.shape)
    return jnp.take_along_axis(tile, index, axis=1, mode="promise_in_bounds")


def first_kernel(
    elem_cap,
    devices,
    faces_hbm,
    counts_hbm,
    rhs_hbm,
    blocks_hbm,
    traces,
    rounded,
    swap,
    cross,
    slots,
    faces,
    counts,
    rhs,
    blocks,
    found,
    sems,
):
    me = lax.axis_index("elem")
    face_dev, functionals, trace_len = rhs.shape
    copies = start_all(
        [(faces_hbm, faces), (counts_hbm, counts), (rhs_hbm, rhs), (blocks_hbm, blocks)], sems
    )
    copies[0].wait()
    copies[1].wait()
    for group, device in enumerate(partners(me)):
        valid = (device >= 0) & (device < devices)
        safe = jnp.clip(device, 0, devices - 1)
        live = jnp.where(valid, counts[safe], 0)
        for r in range(SLOT):
            found[group * 8 + r] = 0

        def scan(e, rank):
            for k in range(6):
                local = faces[k, safe * elem_cap + e] - me * face_dev
                hit = (local >= 0) & (local < face_dev)
                found[group * 8 + rank] = local
                rank = rank + hit.astype(jnp.int32)
            return rank

        lax.fori_loop(0, live, scan, jnp.int32(0))
        for r in range(SLOT):
            slots[group * SLOT + r] = jnp.where(valid, found[group * 8 + r], face_dev)
    copies[2].wait()
    copies[3].wait()
    for f in range(face_dev):
        value = jnp.dot(rhs[f], blocks[f], preferred_element_type=jnp.float32)
        traces[f] = jnp.zeros((functionals, LANES), jnp.float32)
        traces[f, :, :trace_len] = value
        rounded[f] = traces[f].astype(jnp.bfloat16)
    for group in range(4):
        for r in range(SLOT):
            slot = slots[group * SLOT + r]
            tile = rounded[jnp.where(slot < face_dev, slot, 0)]
            if group == CROSS:
                cross[r] = tile
            else:
                swap[group * SLOT + r] = tile


def home_kernel(
    elem_cap,
    faces_hbm,
    orient_hbm,
    counts_hbm,
    tables_hbm,
    rounded,
    mats,
    home,
    remote,
    index_in,
    index_out,
    terms,
    faces,
    orient,
    counts,
    tables,
    table,
    rows,
    heads,
    sems,
):
    me = lax.axis_index("elem")
    face_dev, functionals, _ = rounded.shape
    live = elem_cap - elem_cap // 4
    trace_len = mats.shape[1] // 6
    gap = LANES - trace_len
    far = 4 * SLOT
    copies = start_all(
        [(faces_hbm, faces), (orient_hbm, orient), (counts_hbm, counts), (tables_hbm, tables)], sems
    )
    table[:face_dev] = rounded[...]
    table[face_dev] = jnp.zeros((functionals, LANES), jnp.bfloat16)
    for copy in copies:
        copy.wait()
    groups = list(partners(me))
    for group, device in enumerate(groups):
        heads[device - me + 2] = group * SLOT
    heads[2] = 0
    index_in[...] = jnp.zeros_like(index_in)
    for t in range(far):
        remote[t] = live * 8
    count = counts[me]
    magic = (1 << 16) // face_dev + 1
    places = []
    picks = []
    for e in range(live):
        for k in range(6):
            rel = faces[k, me * elem_cap + e] - (me - 2) * face_dev
            used = e < count
            rel = jnp.where(used, rel, 2 * face_dev)
            owner = (rel * magic) >> 16
            head = heads[owner]
            heads[owner] = head + 1
            at_home = owner == 2
            place = jnp.where(at_home & used, rel - 2 * face_dev, face_dev)
            places.append(place)
            home[6 * e + k] = place
            slot = jnp.where(at_home, far, head)
            remote[slot] = e * 8 + k
            pick = k * 8 + orient[k, me * elem_cap + e]
            picks.append(pick)
            index_in[pl.ds(slot, 1), :] = tables[1, pl.ds(pick, 1), :]
            index_out[pl.ds(6 * e + k, 1), :] = tables[2, pl.ds(pick, 1), :]
    lane = lax.broadcasted_iota(jnp.int32, (functionals, LANES), 1)
    for e in range(live):
        parts = [
            permuted(
                table[places[6 * e + k]].astype(jnp.float32),
                tables[0, pl.ds(picks[6 * e + k], 1), :],
            )
            for k in range(6)
        ]
        for k in range(6):
            later = parts[k + 1] if k < 5 else jnp.zeros_like(parts[k])
            merged = jnp.where(lane < trace_len - gap * k, parts[k], later)
            rows[e, :, k * LANES : (k + 1) * LANES] = merged.astype(jnp.bfloat16)
    for e in range(live):
        terms[e, :, : 6 * trace_len] = jnp.dot(
            rows[e, :, : 6 * trace_len], mats[e], preferred_element_type=jnp.float32
        )


def remote_kernel(
    remote,
    index_in,
    index_out,
    from_sib,
    from_even,
    from_odd,
    before,
    mats,
    swap,
    cross,
    terms,
):
    me = lax.axis_index("elem")
    functionals = before.shape[1]
    live = before.shape[0]
    trace_len = mats.shape[1] // 6
    gap = LANES - trace_len
    height, last = window_rows(trace_len)
    terms[:live] = before[...]
    terms[live] = jnp.zeros(terms.shape[1:], jnp.float32)
    lane = lax.broadcasted_iota(jnp.int32, (functionals, LANES), 1)
    arrived = arrivals(me, from_sib, from_even, from_odd)
    where = []
    for group in range(4):
        for r in range(SLOT):
            t = group * SLOT + r
            packed = remote[t]
            e, k = packed >> 3, packed & 7
            where.append((e, k))
            start = jnp.minimum((trace_len * k) >> 4 << 4, last)
            shift = trace_len * k - start
            tile = permuted(arrived[group][r].astype(jnp.float32), index_in[t : t + 1, :])
            zero = jnp.zeros_like(tile)
            wide = jnp.concatenate(
                [
                    jnp.where((lane >= shift) & (lane < shift + trace_len), tile, zero),
                    jnp.where(lane < shift - gap, tile, zero),
                ],
                axis=1,
            ).astype(jnp.bfloat16)
            window = mats[jnp.minimum(e, live - 1), pl.ds(pl.multiple_of(start, 16), height), :]
            terms[e, :, : 6 * trace_len] += jnp.dot(
                wide[:, :height], window, preferred_element_type=jnp.float32
            )
    for group in range(4):
        for r in range(SLOT):
            t = group * SLOT + r
            e, k = where[t]
            tile = terms[e, :, pl.ds(pl.multiple_of(k * LANES, LANES), LANES)]
            ahead = jnp.maximum(k - 1, 0)
            left = terms[e, :, pl.ds(pl.multiple_of(ahead * LANES, LANES), LANES)]
            tile = jnp.where(lane >= LANES - gap * k, left, tile)
            pick = jnp.minimum(6 * e + k, 6 * live - 1)
            tile = permuted(tile, index_out[pl.ds(pick, 1), :]).astype(jnp.bfloat16)
            if group == CROSS:
                cross[r] = tile
            else:
                swap[group * SLOT + r] = tile


def scatter_kernel(home, index_out, terms, summed):
    functionals = summed.shape[1]
    live = terms.shape[0] - 1
    trace_len = COMP * EDGE * EDGE
    gap = LANES - trace_len
    lane = lax.broadcasted_iota(jnp.int32, (functionals, LANES), 1)
    summed[...] = jnp.zeros_like(summed)
    for e in range(live):
        for k in range(6):
            tile = terms[e, :, k * LANES : (k + 1) * LANES]
            if k:
                left = terms[e, :, (k - 1) * LANES : k * LANES]
                tile = jnp.where(lane >= LANES - gap * k, left, tile)
            i = 6 * e + k
            tile = permuted(tile, index_out[i : i + 1, :])
            place = home[i]
            summed[place] += tile.astype(jnp.bfloat16).astype(jnp.float32)


def last_kernel(slots, home, from_sib, from_even, from_odd, rhs, blocks, traces, out, summed):
    me = lax.axis_index("elem")
    face_dev, _, trace_len = rhs.shape
    summed[...] = home[...]
    arrived = arrivals(me, from_sib, from_even, from_odd)
    for group in range(4):
        for r in range(SLOT):
            place = slots[group * SLOT + r]
            summed[place] += arrived[group][r].astype(jnp.float32)
    for f in range(face_dev):
        residual = rhs[f].astype(jnp.float32) - summed[f, :, :trace_len]
        update = jnp.dot(
            residual.astype(jnp.bfloat16), blocks[f], preferred_element_type=jnp.float32
        )
        out[f] = traces[f, :, :trace_len] + update


def exchange(routes, swap, cross):
    sibling, even_chips, odd_chips = routes
    got = lax.ppermute(swap, "elem", sibling)
    even = jnp.concatenate([cross, got[SLOT : 2 * SLOT]])
    odd = jnp.concatenate([cross, got[2 * SLOT :]])
    return got, lax.ppermute(even, "elem", even_chips), lax.ppermute(odd, "elem", odd_chips)


def per_device(devices, elem_mats, face_blocks, rhs, elem_faces, orient, counts):
    elem_cap, dof, _ = elem_mats.shape
    face_dev, functionals, trace_len = rhs.shape
    live = elem_cap - elem_cap // 4
    far = 4 * SLOT
    routes = swap_routes(devices)

    def in_hbm(array):
        return pltpu.with_memory_space_constraint(array, pltpu.HBM)

    def in_vmem(array):
        return pltpu.with_memory_space_constraint(array, pltpu.VMEM)

    faces = in_hbm(elem_faces.T)
    codes = in_hbm(orient.T)
    counts = in_hbm(counts)
    tables = lane_tables(trace_len)
    vmem = pl.BlockSpec(memory_space=pltpu.VMEM)
    smem = pl.BlockSpec(memory_space=pltpu.SMEM)
    hbm = pl.BlockSpec(memory_space=pltpu.HBM)

    def tiles(count, kind, width=LANES):
        return jax.ShapeDtypeStruct((count, functionals, width), kind)

    def integers(*shape):
        return jax.ShapeDtypeStruct(shape, jnp.int32)

    params = pltpu.CompilerParams(vmem_limit_bytes=4 << 20)
    faces_smem = pltpu.SMEM(faces.shape, jnp.int32)
    counts_smem = pltpu.SMEM(counts.shape, jnp.int32)
    traces, rounded, swap, cross, slots = pl.pallas_call(
        functools.partial(first_kernel, elem_cap, devices),
        out_shape=(
            tiles(face_dev, jnp.float32),
            tiles(face_dev, jnp.bfloat16),
            tiles(3 * SLOT, jnp.bfloat16),
            tiles(SLOT, jnp.bfloat16),
            integers(far),
        ),
        in_specs=[hbm] * 4,
        out_specs=(vmem, vmem, vmem, vmem, smem),
        scratch_shapes=[
            faces_smem,
            counts_smem,
            pltpu.VMEM(rhs.shape, rhs.dtype),
            pltpu.VMEM(face_blocks.shape, face_blocks.dtype),
            pltpu.SMEM((32,), jnp.int32),
            pltpu.SemaphoreType.DMA((4,)),
        ],
        compiler_params=params,
        cost_estimate=pl.CostEstimate(
            flops=10**11, bytes_accessed=10**8, transcendentals=0
        ),
        name="first_sweep",
    )(faces, counts, in_hbm(rhs), in_hbm(face_blocks))
    from_sib, from_even, from_odd = exchange(routes, swap, cross)
    home, remote, index_in, index_out, terms = pl.pallas_call(
        functools.partial(home_kernel, elem_cap),
        out_shape=(
            integers(6 * live),
            integers(far + 1),
            integers(far + 1, LANES),
            integers(6 * live, LANES),
            tiles(live, jnp.float32, 6 * LANES),
        ),
        in_specs=[hbm] * 4 + [vmem] * 2,
        out_specs=(smem, smem, vmem, vmem, vmem),
        scratch_shapes=[
            faces_smem,
            faces_smem,
            counts_smem,
            pltpu.VMEM(tables.shape, jnp.int32),
            pltpu.VMEM((face_dev + 1, functionals, LANES), jnp.bfloat16),
            pltpu.VMEM((live, functionals, 6 * LANES), jnp.bfloat16),
            pltpu.SMEM((8,), jnp.int32),
            pltpu.SemaphoreType.DMA((4,)),
        ],
        compiler_params=params,
        cost_estimate=pl.CostEstimate(
            flops=2 * live * functionals * dof * dof,
            bytes_accessed=2 * live * dof * dof,
            transcendentals=0,
        ),
        name="home_terms",
    )(faces, codes, counts, in_hbm(jnp.asarray(tables)), rounded, in_vmem(elem_mats))
    swap, cross, terms = pl.pallas_call(
        remote_kernel,
        out_shape=(
            tiles(3 * SLOT, jnp.bfloat16),
            tiles(SLOT, jnp.bfloat16),
            tiles(live + 1, jnp.float32, 6 * LANES),
        ),
        in_specs=[smem] + [vmem] * 7,
        out_specs=(vmem,) * 3,
        compiler_params=params,
        name="remote_terms",
    )(remote, index_in, index_out, from_sib, from_even, from_odd, terms, in_vmem(elem_mats))
    from_sib, from_even, from_odd = exchange(routes, swap, cross)
    summed = pl.pallas_call(
        scatter_kernel,
        out_shape=tiles(face_dev + 1, jnp.float32),
        in_specs=[smem] + [vmem] * 2,
        out_specs=vmem,
        compiler_params=params,
        name="home_sum",
    )(home, index_out, terms)
    return pl.pallas_call(
        last_kernel,
        out_shape=jax.ShapeDtypeStruct(rhs.shape, jnp.float32),
        in_specs=[smem] + [vmem] * 7,
        out_specs=vmem,
        scratch_shapes=[pltpu.VMEM((face_dev + 1, functionals, LANES), jnp.float32)],
        compiler_params=params,
        name="last_update",
    )(slots, summed, from_sib, from_even, from_odd, rhs, face_blocks, traces)


def solution(mesh):
    in_specs = (P("elem", None, None), P("elem", None, None), P("elem", None, None), P(), P(), P())
    out_specs = P("elem", None, None)
    return jax.shard_map(
        functools.partial(per_device, mesh.shape["elem"]),
        mesh=mesh,
        in_specs=in_specs,
        out_specs=out_specs,
        check_vma=False,
    )
```

time: 31.5 us -> 20.4 us (0.65)
  the two profiles are of different devices: /device:TPU:16 before, /device:TPU:0 now
where the time goes in v2:
time: 20.4 us; the launch traced here: 20.2 us
  Pallas kernels  8.84 us (43%)
  starting transfers between devices  7.89 us (39%)
  waiting for transfers between devices  3.41 us (17%)
    ppermute x2, starting transfers between devices, exchange(): lax.ppermute(even, 'elem', even_chips)  6.25 us
    pallas_call x1, Pallas kernels, per_device(): pl.pallas_call(functools.partial(home_kernel, elem_cap), out_shape=(integ...  3.02 us
    pallas_call x1, Pallas kernels, per_device(): pl.pallas_call(functools.partial(first_kernel, elem_cap, devices), out_sh...  2 us
    ppermute x2, waiting for transfers between devices, exchange(): got = lax.ppermute(swap, 'elem', sibling)  1.95 us
    pallas_call x1, Pallas kernels, per_device(): pl.pallas_call(last_kernel, out_shape=jax.ShapeDtypeStruct(rhs.shape, jnp...  1.67 us
    ppermute x2, waiting for transfers between devices, exchange(): lax.ppermute(even, 'elem', even_chips)  1.45 us
    pallas_call x1, Pallas kernels, per_device(): pl.pallas_call(remote_kernel, out_shape=(tiles(3 * SLOT, jnp.bfloat16), t...  1.3 us
    ppermute x2, starting transfers between devices, exchange(): got = lax.ppermute(swap, 'elem', sibling)  0.99 us
  transfers between devices with their start and end apart: 6, of which 3 were waited for; matrix products, arithmetic and copies ran while one was open for 0% of the time, Pallas kernels for 19%

profile of v2, /device:TPU:0, one launch (start us, length us, event | category | flops | bytes accessed | tf_op | source)
XLA Modules:
  0.0 20.2 jit_solution(16436945538580590431)
XLA Ops:
  0.0 0.0 copy-start
  0.0 2.0 %first_sweep.1 = (f32[27,16,128]{2,1,0:T(8,128)S(1)}, bf16[27,16,128]{2,1,0:T(8,128)(2,1)S(1)}, bf16[12,16,128]{2,1,0:T(8,128)(2,1)S(1)}, bf16[4,16,128]{2,1,0:T(8,128)(2,1)S(1)}, s32[16]{0:T(128)S(1)}) custom-call(s32[6,384]{1,0:T(8,128)} %bitcast.2, s32[32]{0:T(128)} %counts_hbm.3, bf16[27,16,125]{2,1,0:T(8,128)(2,1)} %rhs.1, bf16[27,125,125]{2,1,0:T(8,128)(2,1)} %blocks.1), custom_call_target="tpu_custom_call" | custom-call | flops 99999997952 | bytes 100000000 | tf_op jit(solution)/shard_map/first_sweep/pallas_call | solution.py:404
  2.0 0.8 %collective-permute-start = (bf16[12,16,128]{2,1,0:T(8,128)(2,1)S(1)}, bf16[12,16,128]{2,1,0:T(8,128)(2,1)S(1)}, u32[]{:S(2)}, u32[]{:S(2)}) collective-permute-start(bf16[12,16,128]{2,1,0:T(8,128)(2,1)S(1)} %get-tuple-element.24), channel_id=1, source_target_pairs={{0,1},{1,0},{2,3},{3,2},{4,5},{5,4},{6,7},{7,6},{8,9},{9,8},{10,11... | collective-permute-start | bytes 147464 | tf_op jit(solution)/shard_map/ppermute | solution.py:368
  2.8 0.9 %collective-permute-done.from_sib = bf16[12,16,128]{2,1,0:T(8,128)(2,1)S(1)} collective-permute-done((bf16[12,16,128]{2,1,0:T(8,128)(2,1)S(1)}, bf16[12,16,128]{2,1,0:T(8,128)(2,1)S(1)}, u32[]{:S(2)}, u32[]{:S(2)}) %collective-permute-start) | collective-permute-done | bytes 49184 | tf_op jit(solution)/shard_map/ppermute | solution.py:368
  3.7 0.4 %collective-permute-start.2 = (bf16[8,16,128]{2,1,0:T(8,128)(2,1)S(1)}, bf16[8,16,128]{2,1,0:T(8,128)(2,1)S(1)}, u32[]{:S(2)}, u32[]{:S(2)}) collective-permute-start(bf16[8,16,128]{2,1,0:T(8,128)(2,1)S(1)} %get-tuple-element.37), channel_id=1, source_target_pairs={{0,1},{1,0},{2,5},{3,4},{4,3},{5,2},{6,9},{7,8},{8,7},{9,6},{10,13... | collective-permute-start | bytes 98312 | tf_op jit(solution)/shard_map/ppermute | solution.py:371
  4.1 3.8 %collective-permute-start.1 = (bf16[8,16,128]{2,1,0:T(8,128)(2,1)S(1)}, bf16[8,16,128]{2,1,0:T(8,128)(2,1)S(1)}, u32[]{:S(2)}, u32[]{:S(2)}) collective-permute-start(bf16[8,16,128]{2,1,0:T(8,128)(2,1)S(1)} %get-tuple-element.38), channel_id=1, source_target_pairs={{0,3},{1,2},{2,1},{3,0},{4,7},{5,6},{6,5},{7,4},{8,11},{9,10},{10,... | collective-permute-start | bytes 98312 | tf_op jit(solution)/shard_map/ppermute | solution.py:371
  7.9 0.0 copy-done
  7.9 0.0 copy-start.1
  7.9 0.0 copy-start.2
  7.9 3.0 %home_terms.1 = (s32[54]{0:T(128)S(1)}, s32[17]{0:T(128)S(1)}, s32[17,128]{1,0:T(8,128)S(1)}, s32[54,128]{1,0:T(8,128)S(1)}, f32[9,16,768]{2,1,0:T(8,128)S(1)}) custom-call(s32[6,384]{1,0:T(8,128)} %bitcast.3, s32[6,384]{1,0:T(8,128)} %bitcast.4, s32[32]{0:T(128)} %counts_hbm.3, s32[3,48,128]{2,1,0:T(8,128)} %constant.2.clone.tables_hbm, ...), custom_call_target="tpu_custom_call" | custom-call | flops 162000000 | bytes 10125000 | tf_op jit(solution)/shard_map/home_terms/pallas_call | solution.py:430
  10.9 0.0 collective-permute-done.2.from_odd
  10.9 0.0 collective-permute-done.1.from_even
  10.9 1.3 %remote_terms.1 = (bf16[12,16,128]{2,1,0:T(8,128)(2,1)S(1)}, bf16[4,16,128]{2,1,0:T(8,128)(2,1)S(1)}, f32[10,16,768]{2,1,0:T(8,128)S(1)}) custom-call(s32[17]{0:T(128)S(1)} %get-tuple-element.22.remote, s32[17,128]{1,0:T(8,128)S(1)} %get-tuple-element.23.index_in, s32[54,128]{1,0:T(8,128)S(1)} %get-tuple-element.21.index_out, ...), custom_call_target="tpu_custom_call" | custom-call | tf_op jit(solution)/shard_map/remote_terms/pallas_call | solution.py:459
  12.2 0.2 %collective-permute-start.3 = (bf16[12,16,128]{2,1,0:T(8,128)(2,1)S(1)}, bf16[12,16,128]{2,1,0:T(8,128)(2,1)S(1)}, u32[]{:S(2)}, u32[]{:S(2)}) collective-permute-start(bf16[12,16,128]{2,1,0:T(8,128)(2,1)S(1)} %get-tuple-element.28), channel_id=1, source_target_pairs={{0,1},{1,0},{2,3},{3,2},{4,5},{5,4},{6,7},{7,6},{8,9},{9,8},{10,11... | collective-permute-start | bytes 147464 | tf_op jit(solution)/shard_map/ppermute | solution.py:368
  12.5 1.1 %collective-permute-done.3.from_sib = bf16[12,16,128]{2,1,0:T(8,128)(2,1)S(1)} collective-permute-done((bf16[12,16,128]{2,1,0:T(8,128)(2,1)S(1)}, bf16[12,16,128]{2,1,0:T(8,128)(2,1)S(1)}, u32[]{:S(2)}, u32[]{:S(2)}) %collective-permute-start.3) | collective-permute-done | bytes 49184 | tf_op jit(solution)/shard_map/ppermute | solution.py:368
  13.5 0.2 %collective-permute-start.5 = (bf16[8,16,128]{2,1,0:T(8,128)(2,1)S(1)}, bf16[8,16,128]{2,1,0:T(8,128)(2,1)S(1)}, u32[]{:S(2)}, u32[]{:S(2)}) collective-permute-start(bf16[8,16,128]{2,1,0:T(8,128)(2,1)S(1)} %get-tuple-element.35), channel_id=1, source_target_pairs={{0,1},{1,0},{2,5},{3,4},{4,3},{5,2},{6,9},{7,8},{8,7},{9,6},{10,13... | collective-permute-start | bytes 98312 | tf_op jit(solution)/shard_map/ppermute | solution.py:371
  13.8 2.5 %collective-permute-start.4 = (bf16[8,16,128]{2,1,0:T(8,128)(2,1)S(1)}, bf16[8,16,128]{2,1,0:T(8,128)(2,1)S(1)}, u32[]{:S(2)}, u32[]{:S(2)}) collective-permute-start(bf16[8,16,128]{2,1,0:T(8,128)(2,1)S(1)} %get-tuple-element.36), channel_id=1, source_target_pairs={{0,3},{1,2},{2,1},{3,0},{4,7},{5,6},{6,5},{7,4},{8,11},{9,10},{10,... | collective-permute-start | bytes 98312 | tf_op jit(solution)/shard_map/ppermute | solution.py:371
  16.2 0.8 %home_sum.1.home = f32[28,16,128]{2,1,0:T(8,128)S(1)} custom-call(s32[54]{0:T(128)S(1)} %get-tuple-element.20.home, s32[54,128]{1,0:T(8,128)S(1)} %get-tuple-element.21.index_out, f32[10,16,768]{2,1,0:T(8,128)S(1)} %get-tuple-element.27.terms), custom_call_target="tpu_custom_call" | custom-call | tf_op jit(solution)/shard_map/home_sum/pallas_call | solution.py:472
  17.1 0.0 collective-permute-done.5.from_odd
  17.1 1.5 %collective-permute-done.4.from_even = bf16[8,16,128]{2,1,0:T(8,128)(2,1)S(1)} collective-permute-done((bf16[8,16,128]{2,1,0:T(8,128)(2,1)S(1)}, bf16[8,16,128]{2,1,0:T(8,128)(2,1)S(1)}, u32[]{:S(2)}, u32[]{:S(2)}) %collective-permute-start.4) | collective-permute-done | bytes 32800 | tf_op jit(solution)/shard_map/ppermute | solution.py:371
  18.5 0.0 copy-done.1
  18.5 0.0 copy-done.2
  18.5 1.7 %last_update.1 = f32[27,16,125]{2,1,0:T(8,128)} custom-call(s32[16]{0:T(128)S(1)} %get-tuple-element.18.slots, f32[28,16,128]{2,1,0:T(8,128)S(1)} %home_sum.1.home, bf16[12,16,128]{2,1,0:T(8,128)(2,1)S(1)} %collective-permute-done.3.from_sib, bf16[8,16,128]{2,1,0:T(8,128)(2,1)S(1)} %collective-permute-done.4.from_even, ...), custom_call_target="tpu_custom_call" | custom-call | tf_op jit(solution)/shard_map/last_update/pallas_call | solution.py:480
  (4 shorter events, 0.0 us)
Async XLA Ops:
  0.0 7.9 %copy-start = (bf16[12,750,750]{2,1,0:T(8,128)(2,1)S(1)}, bf16[12,750,750]{2,1,0:T(8,128)(2,1)}, u32[]{:S(2)}) copy-start(bf16[12,750,750]{2,1,0:T(8,128)(2,1)} %mats.3) | copy-start | bytes 40500004
  2.0 1.6 %collective-permute-start = (bf16[12,16,128]{2,1,0:T(8,128)(2,1)S(1)}, bf16[12,16,128]{2,1,0:T(8,128)(2,1)S(1)}, u32[]{:S(2)}, u32[]{:S(2)}) collective-permute-start(bf16[12,16,128]{2,1,0:T(8,128)(2,1)S(1)} %get-tuple-element.24), channel_id=1, source_target_pairs={{0,1},{1,0},{2,3},{3,2},{4,5},{5,4},{6,7},{7,6},{8,9},{9,8},{10,11... | collective-permute-start | bytes 147464 | tf_op jit(solution)/shard_map/ppermute | solution.py:368
  3.7 7.2 %collective-permute-start.2 = (bf16[8,16,128]{2,1,0:T(8,128)(2,1)S(1)}, bf16[8,16,128]{2,1,0:T(8,128)(2,1)S(1)}, u32[]{:S(2)}, u32[]{:S(2)}) collective-permute-start(bf16[8,16,128]{2,1,0:T(8,128)(2,1)S(1)} %get-tuple-element.37), channel_id=1, source_target_pairs={{0,1},{1,0},{2,5},{3,4},{4,3},{5,2},{6,9},{7,8},{8,7},{9,6},{10,13... | collective-permute-start | bytes 98312 | tf_op jit(solution)/shard_map/ppermute | solution.py:371
  4.1 6.8 %collective-permute-start.1 = (bf16[8,16,128]{2,1,0:T(8,128)(2,1)S(1)}, bf16[8,16,128]{2,1,0:T(8,128)(2,1)S(1)}, u32[]{:S(2)}, u32[]{:S(2)}) collective-permute-start(bf16[8,16,128]{2,1,0:T(8,128)(2,1)S(1)} %get-tuple-element.38), channel_id=1, source_target_pairs={{0,3},{1,2},{2,1},{3,0},{4,7},{5,6},{6,5},{7,4},{8,11},{9,10},{10,... | collective-permute-start | bytes 98312 | tf_op jit(solution)/shard_map/ppermute | solution.py:371
  7.9 10.7 %copy-start.1 = (bf16[27,125,125]{2,1,0:T(8,128)(2,1)S(1)}, bf16[27,125,125]{2,1,0:T(8,128)(2,1)}, u32[]{:S(2)}) copy-start(bf16[27,125,125]{2,1,0:T(8,128)(2,1)} %blocks.1) | copy-start | bytes 2531254
  7.9 10.7 %copy-start.2 = (bf16[27,16,125]{2,1,0:T(8,128)(2,1)S(1)}, bf16[27,16,125]{2,1,0:T(8,128)(2,1)}, u32[]{:S(2)}) copy-start(bf16[27,16,125]{2,1,0:T(8,128)(2,1)} %rhs.1) | copy-start | bytes 324004
  12.2 1.3 %collective-permute-start.3 = (bf16[12,16,128]{2,1,0:T(8,128)(2,1)S(1)}, bf16[12,16,128]{2,1,0:T(8,128)(2,1)S(1)}, u32[]{:S(2)}, u32[]{:S(2)}) collective-permute-start(bf16[12,16,128]{2,1,0:T(8,128)(2,1)S(1)} %get-tuple-element.28), channel_id=1, source_target_pairs={{0,1},{1,0},{2,3},{3,2},{4,5},{5,4},{6,7},{7,6},{8,9},{9,8},{10,11... | collective-permute-start | bytes 147464 | tf_op jit(solution)/shard_map/ppermute | solution.py:368
  13.5 3.5 %collective-permute-start.5 = (bf16[8,16,128]{2,1,0:T(8,128)(2,1)S(1)}, bf16[8,16,128]{2,1,0:T(8,128)(2,1)S(1)}, u32[]{:S(2)}, u32[]{:S(2)}) collective-permute-start(bf16[8,16,128]{2,1,0:T(8,128)(2,1)S(1)} %get-tuple-element.35), channel_id=1, source_target_pairs={{0,1},{1,0},{2,5},{3,4},{4,3},{5,2},{6,9},{7,8},{8,7},{9,6},{10,13... | collective-permute-start | bytes 98312 | tf_op jit(solution)/shard_map/ppermute | solution.py:371
  13.8 4.8 %collective-permute-start.4 = (bf16[8,16,128]{2,1,0:T(8,128)(2,1)S(1)}, bf16[8,16,128]{2,1,0:T(8,128)(2,1)S(1)}, u32[]{:S(2)}, u32[]{:S(2)}) collective-permute-start(bf16[8,16,128]{2,1,0:T(8,128)(2,1)S(1)} %get-tuple-element.36), channel_id=1, source_target_pairs={{0,3},{1,2},{2,1},{3,0},{4,7},{5,6},{6,5},{7,4},{8,11},{9,10},{10,... | collective-permute-start | bytes 98312 | tf_op jit(solution)/shard_map/ppermute | solution.py:371

commit v3 on v2

--- a/solution.py
+++ b/solution.py
@@ -122,6 +122,50 @@
     return jnp.take_along_axis(tile, index, axis=1, mode="promise_in_bounds")
 
 
+def wanted_faces(me, elem_cap, devices, face_dev, faces, counts):
+    width = 2 * LANES
+    start = (me - 2) * elem_cap
+    block = jnp.clip(start // LANES, 0, faces.shape[1] // LANES - 2)
+    window = faces[:, pl.ds(pl.multiple_of(block * LANES, LANES), width)]
+    shift = block * LANES - start
+    window = pltpu.roll(
+        jnp.concatenate([window, window[:2]]), jnp.where(shift < 0, shift + width, shift), 1
+    )
+    lane = lax.broadcasted_iota(jnp.int32, (1, LANES), 1)
+    span = sum((lane >= elem_cap * q).astype(jnp.int32) for q in range(1, 6))
+    elem = lane - elem_cap * span
+    limit = jnp.zeros_like(lane)
+    for q in (0, 1, 3, 4):
+        device = me + q - 2
+        inside = (device >= 0) & (device < devices)
+        count = jnp.where(inside, counts[jnp.clip(device, 0, devices - 1)], 0)
+        limit = jnp.where(span == q, count, limit)
+    local = [(window[k : k + 1, :LANES] - me * face_dev) for k in range(6)]
+    hits = [(x >= 0) & (x < face_dev) & (elem < limit) for x in local]
+    ones = [hit.astype(jnp.float32) for hit in hits]
+    column = sum(ones)
+    before = jnp.broadcast_to(column, (8, LANES))
+    elems = jnp.broadcast_to(elem, (8, LANES))
+    step = 1
+    while step < elem_cap:
+        before = before + jnp.where(elems >= step, pltpu.roll(before, step, 1), 0.0)
+        step *= 2
+    rank = before[:1] - column
+    found = [jnp.zeros((1, LANES), jnp.float32) for _ in range(SLOT)]
+    for k in range(6):
+        value = jnp.where(hits[k], local[k].astype(jnp.float32), 0.0)
+        for r in range(SLOT):
+            found[r] = found[r] + jnp.where(rank == r, value, 0.0)
+        rank = rank + ones[k]
+    slots = []
+    for device in partners(me):
+        inside = (device >= 0) & (device < devices)
+        for r in range(SLOT):
+            slot = jnp.sum(jnp.where(span == device - me + 2, found[r], 0.0)).astype(jnp.int32)
+            slots.append(jnp.where(inside, slot, face_dev))
+    return slots
+
+
 def first_kernel(
     elem_cap,
     devices,
@@ -138,7 +182,6 @@
     counts,
     rhs,
     blocks,
-    found,
     sems,
 ):
     me = lax.axis_index("elem")
@@ -148,24 +191,9 @@
     )
     copies[0].wait()
     copies[1].wait()
-    for group, device in enumerate(partners(me)):
-        valid = (device >= 0) & (device < devices)
-        safe = jnp.clip(device, 0, devices - 1)
-        live = jnp.where(valid, counts[safe], 0)
-        for r in range(SLOT):
-            found[group * 8 + r] = 0
-
-        def scan(e, rank):
-            for k in range(6):
-                local = faces[k, safe * elem_cap + e] - me * face_dev
-                hit = (local >= 0) & (local < face_dev)
-                found[group * 8 + rank] = local
-                rank = rank + hit.astype(jnp.int32)
-            return rank
-
-        lax.fori_loop(0, live, scan, jnp.int32(0))
-        for r in range(SLOT):
-            slots[group * SLOT + r] = jnp.where(valid, found[group * 8 + r], face_dev)
+    picked = wanted_faces(me, elem_cap, devices, face_dev, faces, counts)
+    for i, slot in enumerate(picked):
+        slots[i : i + 1, :] = jnp.full((1, LANES), slot)
     copies[2].wait()
     copies[3].wait()
     for f in range(face_dev):
@@ -175,7 +203,7 @@
         rounded[f] = traces[f].astype(jnp.bfloat16)
     for group in range(4):
         for r in range(SLOT):
-            slot = slots[group * SLOT + r]
+            slot = picked[group * SLOT + r]
             tile = rounded[jnp.where(slot < face_dev, slot, 0)]
             if group == CROSS:
                 cross[r] = tile
@@ -190,6 +218,7 @@
     counts_hbm,
     tables_hbm,
     rounded,
+    from_sib,
     mats,
     home,
     remote,
@@ -216,6 +245,7 @@
     )
     table[:face_dev] = rounded[...]
     table[face_dev] = jnp.zeros((functionals, LANES), jnp.bfloat16)
+    table[face_dev + 1 :] = from_sib[:SLOT]
     for copy in copies:
         copy.wait()
     groups = list(partners(me))
@@ -223,8 +253,7 @@
         heads[device - me + 2] = group * SLOT
     heads[2] = 0
     index_in[...] = jnp.zeros_like(index_in)
-    for t in range(far):
-        remote[t] = live * 8
+    remote[...] = jnp.full(remote.shape, live * 8)
     count = counts[me]
     magic = (1 << 16) // face_dev + 1
     places = []
@@ -239,10 +268,10 @@
             heads[owner] = head + 1
             at_home = owner == 2
             place = jnp.where(at_home & used, rel - 2 * face_dev, face_dev)
-            places.append(place)
             home[6 * e + k] = place
             slot = jnp.where(at_home, far, head)
-            remote[slot] = e * 8 + k
+            places.append(jnp.where(slot < SLOT, face_dev + 1 + slot, place))
+            remote[pl.ds(slot, 1), :] = jnp.full((1, LANES), e * 8 + k)
             pick = k * 8 + orient[k, me * elem_cap + e]
             picks.append(pick)
             index_in[pl.ds(slot, 1), :] = tables[1, pl.ds(pick, 1), :]
@@ -289,16 +318,23 @@
     terms[live] = jnp.zeros(terms.shape[1:], jnp.float32)
     lane = lax.broadcasted_iota(jnp.int32, (functionals, LANES), 1)
     arrived = arrivals(me, from_sib, from_even, from_odd)
+    turned = [
+        permuted(arrived[t // SLOT][t % SLOT].astype(jnp.float32), index_in[t : t + 1, :])
+        for t in range(4 * SLOT)
+    ]
+    packs = remote[...]
     where = []
     for group in range(4):
         for r in range(SLOT):
             t = group * SLOT + r
-            packed = remote[t]
+            packed = packs[t, 0]
             e, k = packed >> 3, packed & 7
             where.append((e, k))
+            if group == SIB:
+                continue
             start = jnp.minimum((trace_len * k) >> 4 << 4, last)
             shift = trace_len * k - start
-            tile = permuted(arrived[group][r].astype(jnp.float32), index_in[t : t + 1, :])
+            tile = turned[t]
             zero = jnp.zeros_like(tile)
             wide = jnp.concatenate(
                 [
@@ -327,13 +363,13 @@
                 swap[group * SLOT + r] = tile
 
 
-def scatter_kernel(home, index_out, terms, summed):
-    functionals = summed.shape[1]
+def scatter_kernel(home, index_out, terms, rhs, base):
+    face_dev, functionals, trace_len = rhs.shape
     live = terms.shape[0] - 1
-    trace_len = COMP * EDGE * EDGE
     gap = LANES - trace_len
     lane = lax.broadcasted_iota(jnp.int32, (functionals, LANES), 1)
-    summed[...] = jnp.zeros_like(summed)
+    base[:face_dev, :, :trace_len] = rhs[...].astype(jnp.float32)
+    base[face_dev] = jnp.zeros((functionals, LANES), jnp.float32)
     for e in range(live):
         for k in range(6):
             tile = terms[e, :, k * LANES : (k + 1) * LANES]
@@ -343,22 +379,24 @@
             i = 6 * e + k
             tile = permuted(tile, index_out[i : i + 1, :])
             place = home[i]
-            summed[place] += tile.astype(jnp.bfloat16).astype(jnp.float32)
-
-
-def last_kernel(slots, home, from_sib, from_even, from_odd, rhs, blocks, traces, out, summed):
+            base[place] -= tile.astype(jnp.bfloat16).astype(jnp.float32)
+
+
+def last_kernel(slots, base, from_sib, from_even, from_odd, blocks, traces, out, residual):
     me = lax.axis_index("elem")
-    face_dev, _, trace_len = rhs.shape
-    summed[...] = home[...]
+    face_dev, _, trace_len = out.shape
+    residual[...] = base[...]
     arrived = arrivals(me, from_sib, from_even, from_odd)
+    places = slots[...]
     for group in range(4):
         for r in range(SLOT):
-            place = slots[group * SLOT + r]
-            summed[place] += arrived[group][r].astype(jnp.float32)
+            place = places[group * SLOT + r, 0]
+            residual[place] -= arrived[group][r].astype(jnp.float32)
     for f in range(face_dev):
-        residual = rhs[f].astype(jnp.float32) - summed[f, :, :trace_len]
         update = jnp.dot(
-            residual.astype(jnp.bfloat16), blocks[f], preferred_element_type=jnp.float32
+            residual[f, :, :trace_len].astype(jnp.bfloat16),
+            blocks[f],
+            preferred_element_type=jnp.float32,
         )
         out[f] = traces[f, :, :trace_len] + update
 
@@ -408,16 +446,15 @@
             tiles(face_dev, jnp.bfloat16),
             tiles(3 * SLOT, jnp.bfloat16),
             tiles(SLOT, jnp.bfloat16),
-            integers(far),
+            integers(far, LANES),
         ),
         in_specs=[hbm] * 4,
-        out_specs=(vmem, vmem, vmem, vmem, smem),
+        out_specs=(vmem,) * 5,
         scratch_shapes=[
-            faces_smem,
+            pltpu.VMEM(faces.shape, jnp.int32),
             counts_smem,
             pltpu.VMEM(rhs.shape, rhs.dtype),
             pltpu.VMEM(face_blocks.shape, face_blocks.dtype),
-            pltpu.SMEM((32,), jnp.int32),
             pltpu.SemaphoreType.DMA((4,)),
         ],
         compiler_params=params,
@@ -431,19 +468,19 @@
         functools.partial(home_kernel, elem_cap),
         out_shape=(
             integers(6 * live),
-            integers(far + 1),
+            integers(far + 1, LANES),
             integers(far + 1, LANES),
             integers(6 * live, LANES),
             tiles(live, jnp.float32, 6 * LANES),
         ),
-        in_specs=[hbm] * 4 + [vmem] * 2,
-        out_specs=(smem, smem, vmem, vmem, vmem),
+        in_specs=[hbm] * 4 + [vmem] * 3,
+        out_specs=(smem,) + (vmem,) * 4,
         scratch_shapes=[
             faces_smem,
             faces_smem,
             counts_smem,
             pltpu.VMEM(tables.shape, jnp.int32),
-            pltpu.VMEM((face_dev + 1, functionals, LANES), jnp.bfloat16),
+            pltpu.VMEM((face_dev + 1 + SLOT, functionals, LANES), jnp.bfloat16),
             pltpu.VMEM((live, functionals, 6 * LANES), jnp.bfloat16),
             pltpu.SMEM((8,), jnp.int32),
             pltpu.SemaphoreType.DMA((4,)),
@@ -455,7 +492,7 @@
             transcendentals=0,
         ),
         name="home_terms",
-    )(faces, codes, counts, in_hbm(jnp.asarray(tables)), rounded, in_vmem(elem_mats))
+    )(faces, codes, counts, in_hbm(jnp.asarray(tables)), rounded, from_sib, in_vmem(elem_mats))
     swap, cross, terms = pl.pallas_call(
         remote_kernel,
         out_shape=(
@@ -463,29 +500,31 @@
             tiles(SLOT, jnp.bfloat16),
             tiles(live + 1, jnp.float32, 6 * LANES),
         ),
-        in_specs=[smem] + [vmem] * 7,
+        in_specs=[vmem] * 8,
         out_specs=(vmem,) * 3,
         compiler_params=params,
         name="remote_terms",
     )(remote, index_in, index_out, from_sib, from_even, from_odd, terms, in_vmem(elem_mats))
     from_sib, from_even, from_odd = exchange(routes, swap, cross)
-    summed = pl.pallas_call(
+    base = pl.pallas_call(
         scatter_kernel,
         out_shape=tiles(face_dev + 1, jnp.float32),
-        in_specs=[smem] + [vmem] * 2,
+        in_specs=[smem] + [vmem] * 3,
         out_specs=vmem,
         compiler_params=params,
         name="home_sum",
-    )(home, index_out, terms)
+    )(home, index_out, terms, rhs)
     return pl.pallas_call(
         last_kernel,
         out_shape=jax.ShapeDtypeStruct(rhs.shape, jnp.float32),
-        in_specs=[smem] + [vmem] * 7,
+        in_specs=[vmem] * 7,
         out_specs=vmem,
-        scratch_shapes=[pltpu.VMEM((face_dev + 1, functionals, LANES), jnp.float32)],
+        scratch_shapes=[
+            pltpu.VMEM((face_dev + 1, functionals, LANES), jnp.float32),
+        ],
         compiler_params=params,
         name="last_update",
-    )(slots, summed, from_sib, from_even, from_odd, rhs, face_blocks, traces)
+    )(slots, base, from_sib, from_even, from_odd, face_blocks, traces)
 
 
 def solution(mesh):

time: 20.4 us -> 18.7 us (0.917)
  Pallas kernels: 8.84 us -> 7.45 us
  starting transfers between devices: 7.89 us -> 7.63 us
    pallas_call x1, Pallas kernels: 1.3 us -> 0.68 us  [per_device(): pl.pallas_call(remote_kernel, out_shape=(tiles(3 * SLOT, jnp.bfloat16), t...]
    pallas_call x1, Pallas kernels: 1.67 us -> 1.14 us  [per_device(): pl.pallas_call(last_kernel, out_shape=jax.ShapeDtypeStruct(rhs.shape, jnp...]
    ppermute x2, starting transfers between devices: 0.99 us -> 0.74 us  [exchange(): got = lax.ppermute(swap, 'elem', sibling)]
  transfers between devices with their start and end apart: 6 -> 6, of which waited for: 3 -> 3; matrix products, arithmetic and copies ran while one was open for 0% -> 0% of each run, Pallas kernels for 19% -> 21%
where the time goes in v3:
time: 18.7 us; the launch traced here: 18.6 us
  starting transfers between devices  7.63 us (41%)
  Pallas kernels  7.45 us (40%)
  waiting for transfers between devices  3.43 us (18%)
    ppermute x2, starting transfers between devices, exchange(): lax.ppermute(even, 'elem', even_chips)  6.24 us
    pallas_call x1, Pallas kernels, per_device(): pl.pallas_call(functools.partial(home_kernel, elem_cap), out_shape=(integ...  3.01 us
    ppermute x2, waiting for transfers between devices, exchange(): got = lax.ppermute(swap, 'elem', sibling)  1.95 us
    pallas_call x1, Pallas kernels, per_device(): pl.pallas_call(functools.partial(first_kernel, elem_cap, devices), out_sh...  1.81 us
    ppermute x2, waiting for transfers between devices, exchange(): lax.ppermute(even, 'elem', even_chips)  1.48 us
    pallas_call x1, Pallas kernels, per_device(): pl.pallas_call(last_kernel, out_shape=jax.ShapeDtypeStruct(rhs.shape, jnp...  1.14 us
    pallas_call x1, Pallas kernels, per_device(): pl.pallas_call(scatter_kernel, out_shape=tiles(face_dev + 1, jnp.float32)...  0.82 us
    ppermute x2, starting transfers between devices, exchange(): got = lax.ppermute(swap, 'elem', sibling)  0.74 us
  transfers between devices with their start and end apart: 6, of which 3 were waited for; matrix products, arithmetic and copies ran while one was open for 0% of the time, Pallas kernels for 21%

profile of v3, /device:TPU:0, one launch (start us, length us, event | category | flops | bytes accessed | tf_op | source)
XLA Modules:
  0.0 18.6 jit_solution(7286165524036569657)
XLA Ops:
  0.0 0.0 copy-start
  0.0 1.8 %first_sweep.1 = (f32[27,16,128]{2,1,0:T(8,128)S(1)}, bf16[27,16,128]{2,1,0:T(8,128)(2,1)S(1)}, bf16[12,16,128]{2,1,0:T(8,128)(2,1)S(1)}, bf16[4,16,128]{2,1,0:T(8,128)(2,1)S(1)}, s32[16,128]{1,0:T(8,128)S(1)}) custom-call(s32[6,384]{1,0:T(8,128)} %bitcast.2, s32[32]{0:T(128)} %counts_hbm.3, bf16[27,16,125]{2,1,0:T(8,128)(2,1)} %rhs.1, ...), custom_call_target="tpu_custom_call" | custom-call | flops 99999997952 | bytes 100000000 | tf_op jit(solution)/shard_map/first_sweep/pallas_call | solution.py:442
  1.8 0.5 %collective-permute-start = (bf16[12,16,128]{2,1,0:T(8,128)(2,1)S(1)}, bf16[12,16,128]{2,1,0:T(8,128)(2,1)S(1)}, u32[]{:S(2)}, u32[]{:S(2)}) collective-permute-start(bf16[12,16,128]{2,1,0:T(8,128)(2,1)S(1)} %get-tuple-element.20), channel_id=1, source_target_pairs={{0,1},{1,0},{2,3},{3,2},{4,5},{5,4},{6,7},{7,6},{8,9},{9,8},{10,11... | collective-permute-start | bytes 147464 | tf_op jit(solution)/shard_map/ppermute | solution.py:406
  2.3 0.9 %collective-permute-done.from_sib = bf16[12,16,128]{2,1,0:T(8,128)(2,1)S(1)} collective-permute-done((bf16[12,16,128]{2,1,0:T(8,128)(2,1)S(1)}, bf16[12,16,128]{2,1,0:T(8,128)(2,1)S(1)}, u32[]{:S(2)}, u32[]{:S(2)}) %collective-permute-start) | collective-permute-done | bytes 49184 | tf_op jit(solution)/shard_map/ppermute | solution.py:406
  3.2 0.4 %collective-permute-start.2 = (bf16[8,16,128]{2,1,0:T(8,128)(2,1)S(1)}, bf16[8,16,128]{2,1,0:T(8,128)(2,1)S(1)}, u32[]{:S(2)}, u32[]{:S(2)}) collective-permute-start(bf16[8,16,128]{2,1,0:T(8,128)(2,1)S(1)} %get-tuple-element.37), channel_id=1, source_target_pairs={{0,1},{1,0},{2,5},{3,4},{4,3},{5,2},{6,9},{7,8},{8,7},{9,6},{10,13... | collective-permute-start | bytes 98312 | tf_op jit(solution)/shard_map/ppermute | solution.py:409
  3.6 3.7 %collective-permute-start.1 = (bf16[8,16,128]{2,1,0:T(8,128)(2,1)S(1)}, bf16[8,16,128]{2,1,0:T(8,128)(2,1)S(1)}, u32[]{:S(2)}, u32[]{:S(2)}) collective-permute-start(bf16[8,16,128]{2,1,0:T(8,128)(2,1)S(1)} %get-tuple-element.38), channel_id=1, source_target_pairs={{0,3},{1,2},{2,1},{3,0},{4,7},{5,6},{6,5},{7,4},{8,11},{9,10},{10,... | collective-permute-start | bytes 98312 | tf_op jit(solution)/shard_map/ppermute | solution.py:409
  7.3 0.0 copy-done
  7.3 0.0 copy-start.2
  7.4 0.0 copy-start.1
  7.4 3.0 %home_terms.1 = (s32[54]{0:T(128)S(1)}, s32[17,128]{1,0:T(8,128)S(1)}, s32[17,128]{1,0:T(8,128)S(1)}, s32[54,128]{1,0:T(8,128)S(1)}, f32[9,16,768]{2,1,0:T(8,128)S(1)}) custom-call(s32[6,384]{1,0:T(8,128)} %bitcast.3, s32[6,384]{1,0:T(8,128)} %bitcast.4, s32[32]{0:T(128)} %counts_hbm.3, s32[3,48,128]{2,1,0:T(8,128)} %constant.2.clone.tables_hbm, ...), custom_call_target="tpu_custom_call" | custom-call | flops 162000000 | bytes 10125000 | tf_op jit(solution)/shard_map/home_terms/pallas_call | solution.py:467
  10.4 0.0 collective-permute-done.2.from_odd
  10.4 0.0 collective-permute-done.1.from_even
  10.4 0.7 %remote_terms.1 = (bf16[12,16,128]{2,1,0:T(8,128)(2,1)S(1)}, bf16[4,16,128]{2,1,0:T(8,128)(2,1)S(1)}, f32[10,16,768]{2,1,0:T(8,128)S(1)}) custom-call(s32[17,128]{1,0:T(8,128)S(1)} %get-tuple-element.23.remote, s32[17,128]{1,0:T(8,128)S(1)} %get-tuple-element.24.index_in, s32[54,128]{1,0:T(8,128)S(1)} %get-tuple-element.22.index_out, ...), custom_call_target="tpu_custom_call" | custom-call | tf_op jit(solution)/shard_map/remote_terms/pallas_call | solution.py:496
  11.1 0.2 %collective-permute-start.3 = (bf16[12,16,128]{2,1,0:T(8,128)(2,1)S(1)}, bf16[12,16,128]{2,1,0:T(8,128)(2,1)S(1)}, u32[]{:S(2)}, u32[]{:S(2)}) collective-permute-start(bf16[12,16,128]{2,1,0:T(8,128)(2,1)S(1)} %get-tuple-element.28), channel_id=1, source_target_pairs={{0,1},{1,0},{2,3},{3,2},{4,5},{5,4},{6,7},{7,6},{8,9},{9,8},{10,11... | collective-permute-start | bytes 147464 | tf_op jit(solution)/shard_map/ppermute | solution.py:406
  11.3 1.1 %collective-permute-done.3.from_sib = bf16[12,16,128]{2,1,0:T(8,128)(2,1)S(1)} collective-permute-done((bf16[12,16,128]{2,1,0:T(8,128)(2,1)S(1)}, bf16[12,16,128]{2,1,0:T(8,128)(2,1)S(1)}, u32[]{:S(2)}, u32[]{:S(2)}) %collective-permute-start.3) | collective-permute-done | bytes 49184 | tf_op jit(solution)/shard_map/ppermute | solution.py:406
  12.4 0.2 %collective-permute-start.5 = (bf16[8,16,128]{2,1,0:T(8,128)(2,1)S(1)}, bf16[8,16,128]{2,1,0:T(8,128)(2,1)S(1)}, u32[]{:S(2)}, u32[]{:S(2)}) collective-permute-start(bf16[8,16,128]{2,1,0:T(8,128)(2,1)S(1)} %get-tuple-element.35), channel_id=1, source_target_pairs={{0,1},{1,0},{2,5},{3,4},{4,3},{5,2},{6,9},{7,8},{8,7},{9,6},{10,13... | collective-permute-start | bytes 98312 | tf_op jit(solution)/shard_map/ppermute | solution.py:409
  12.6 2.5 %collective-permute-start.4 = (bf16[8,16,128]{2,1,0:T(8,128)(2,1)S(1)}, bf16[8,16,128]{2,1,0:T(8,128)(2,1)S(1)}, u32[]{:S(2)}, u32[]{:S(2)}) collective-permute-start(bf16[8,16,128]{2,1,0:T(8,128)(2,1)S(1)} %get-tuple-element.36), channel_id=1, source_target_pairs={{0,3},{1,2},{2,1},{3,0},{4,7},{5,6},{6,5},{7,4},{8,11},{9,10},{10,... | collective-permute-start | bytes 98312 | tf_op jit(solution)/shard_map/ppermute | solution.py:409
  15.2 0.0 copy-done.2
  15.2 0.8 %home_sum.1.base = f32[28,16,128]{2,1,0:T(8,128)S(1)} custom-call(s32[54]{0:T(128)S(1)} %get-tuple-element.21.home, s32[54,128]{1,0:T(8,128)S(1)} %get-tuple-element.22.index_out, f32[10,16,768]{2,1,0:T(8,128)S(1)} %get-tuple-element.27.terms, bf16[27,16,125]{2,1,0:T(8,128)(2,1)S(1)} %copy-done.2), custom_call_target="tpu_custom_call" | custom-call | tf_op jit(solution)/shard_map/home_sum/pallas_call | solution.py:509
  16.0 0.0 collective-permute-done.5.from_odd
  16.0 1.5 %collective-permute-done.4.from_even = bf16[8,16,128]{2,1,0:T(8,128)(2,1)S(1)} collective-permute-done((bf16[8,16,128]{2,1,0:T(8,128)(2,1)S(1)}, bf16[8,16,128]{2,1,0:T(8,128)(2,1)S(1)}, u32[]{:S(2)}, u32[]{:S(2)}) %collective-permute-start.4) | collective-permute-done | bytes 32800 | tf_op jit(solution)/shard_map/ppermute | solution.py:409
  17.5 0.0 copy-done.1
  17.5 1.1 %last_update.1 = f32[27,16,125]{2,1,0:T(8,128)} custom-call(s32[16,128]{1,0:T(8,128)S(1)} %get-tuple-element.18.slots, f32[28,16,128]{2,1,0:T(8,128)S(1)} %home_sum.1.base, bf16[12,16,128]{2,1,0:T(8,128)(2,1)S(1)} %collective-permute-done.3.from_sib, bf16[8,16,128]{2,1,0:T(8,128)(2,1)S(1)} %collective-permute-done.4.from_even, ...), custom_call_target="tpu_custom_call" | custom-call | tf_op jit(solution)/shard_map/last_update/pallas_call | solution.py:517
  (4 shorter events, 0.0 us)
Async XLA Ops:
  0.0 7.3 %copy-start = (bf16[12,750,750]{2,1,0:T(8,128)(2,1)S(1)}, bf16[12,750,750]{2,1,0:T(8,128)(2,1)}, u32[]{:S(2)}) copy-start(bf16[12,750,750]{2,1,0:T(8,128)(2,1)} %mats.3) | copy-start | bytes 40500004
  1.8 1.4 %collective-permute-start = (bf16[12,16,128]{2,1,0:T(8,128)(2,1)S(1)}, bf16[12,16,128]{2,1,0:T(8,128)(2,1)S(1)}, u32[]{:S(2)}, u32[]{:S(2)}) collective-permute-start(bf16[12,16,128]{2,1,0:T(8,128)(2,1)S(1)} %get-tuple-element.20), channel_id=1, source_target_pairs={{0,1},{1,0},{2,3},{3,2},{4,5},{5,4},{6,7},{7,6},{8,9},{9,8},{10,11... | collective-permute-start | bytes 147464 | tf_op jit(solution)/shard_map/ppermute | solution.py:406
  3.2 7.1 %collective-permute-start.2 = (bf16[8,16,128]{2,1,0:T(8,128)(2,1)S(1)}, bf16[8,16,128]{2,1,0:T(8,128)(2,1)S(1)}, u32[]{:S(2)}, u32[]{:S(2)}) collective-permute-start(bf16[8,16,128]{2,1,0:T(8,128)(2,1)S(1)} %get-tuple-element.37), channel_id=1, source_target_pairs={{0,1},{1,0},{2,5},{3,4},{4,3},{5,2},{6,9},{7,8},{8,7},{9,6},{10,13... | collective-permute-start | bytes 98312 | tf_op jit(solution)/shard_map/ppermute | solution.py:409
  3.6 6.7 %collective-permute-start.1 = (bf16[8,16,128]{2,1,0:T(8,128)(2,1)S(1)}, bf16[8,16,128]{2,1,0:T(8,128)(2,1)S(1)}, u32[]{:S(2)}, u32[]{:S(2)}) collective-permute-start(bf16[8,16,128]{2,1,0:T(8,128)(2,1)S(1)} %get-tuple-element.38), channel_id=1, source_target_pairs={{0,3},{1,2},{2,1},{3,0},{4,7},{5,6},{6,5},{7,4},{8,11},{9,10},{10,... | collective-permute-start | bytes 98312 | tf_op jit(solution)/shard_map/ppermute | solution.py:409
  7.3 7.8 %copy-start.2 = (bf16[27,16,125]{2,1,0:T(8,128)(2,1)S(1)}, bf16[27,16,125]{2,1,0:T(8,128)(2,1)}, u32[]{:S(2)}) copy-start(bf16[27,16,125]{2,1,0:T(8,128)(2,1)} %rhs.1) | copy-start | bytes 324004
  7.4 10.1 %copy-start.1 = (bf16[27,125,125]{2,1,0:T(8,128)(2,1)S(1)}, bf16[27,125,125]{2,1,0:T(8,128)(2,1)}, u32[]{:S(2)}) copy-start(bf16[27,125,125]{2,1,0:T(8,128)(2,1)} %blocks.1) | copy-start | bytes 2531254
  11.1 1.3 %collective-permute-start.3 = (bf16[12,16,128]{2,1,0:T(8,128)(2,1)S(1)}, bf16[12,16,128]{2,1,0:T(8,128)(2,1)S(1)}, u32[]{:S(2)}, u32[]{:S(2)}) collective-permute-start(bf16[12,16,128]{2,1,0:T(8,128)(2,1)S(1)} %get-tuple-element.28), channel_id=1, source_target_pairs={{0,1},{1,0},{2,3},{3,2},{4,5},{5,4},{6,7},{7,6},{8,9},{9,8},{10,11... | collective-permute-start | bytes 147464 | tf_op jit(solution)/shard_map/ppermute | solution.py:406
  12.4 3.6 %collective-permute-start.5 = (bf16[8,16,128]{2,1,0:T(8,128)(2,1)S(1)}, bf16[8,16,128]{2,1,0:T(8,128)(2,1)S(1)}, u32[]{:S(2)}, u32[]{:S(2)}) collective-permute-start(bf16[8,16,128]{2,1,0:T(8,128)(2,1)S(1)} %get-tuple-element.35), channel_id=1, source_target_pairs={{0,1},{1,0},{2,5},{3,4},{4,3},{5,2},{6,9},{7,8},{8,7},{9,6},{10,13... | collective-permute-start | bytes 98312 | tf_op jit(solution)/shard_map/ppermute | solution.py:409
  12.6 4.9 %collective-permute-start.4 = (bf16[8,16,128]{2,1,0:T(8,128)(2,1)S(1)}, bf16[8,16,128]{2,1,0:T(8,128)(2,1)S(1)}, u32[]{:S(2)}, u32[]{:S(2)}) collective-permute-start(bf16[8,16,128]{2,1,0:T(8,128)(2,1)S(1)} %get-tuple-element.36), channel_id=1, source_target_pairs={{0,3},{1,2},{2,1},{3,0},{4,7},{5,6},{6,5},{7,4},{8,11},{9,10},{10,... | collective-permute-start | bytes 98312 | tf_op jit(solution)/shard_map/ppermute | solution.py:409

commit v4 on v3

--- a/solution.py
+++ b/solution.py
@@ -122,15 +122,27 @@
     return jnp.take_along_axis(tile, index, axis=1, mode="promise_in_bounds")
 
 
+def lanes_from(array, start):
+    width = 2 * LANES
+    block = jnp.clip(start // LANES, 0, array.shape[1] // LANES - 2)
+    window = array[:, pl.ds(pl.multiple_of(block * LANES, LANES), width)]
+    shift = block * LANES - start
+    window = jnp.concatenate([window, window[:2]])
+    return pltpu.roll(window, jnp.where(shift < 0, shift + width, shift), 1)[:, :LANES]
+
+
+def sum_before(counts, elem, elem_cap):
+    elem = jnp.broadcast_to(elem, counts.shape)
+    total = counts
+    step = 1
+    while step < elem_cap:
+        total = total + jnp.where(elem >= step, pltpu.roll(total, step, 1), 0.0)
+        step *= 2
+    return total - counts
+
+
 def wanted_faces(me, elem_cap, devices, face_dev, faces, counts):
-    width = 2 * LANES
-    start = (me - 2) * elem_cap
-    block = jnp.clip(start // LANES, 0, faces.shape[1] // LANES - 2)
-    window = faces[:, pl.ds(pl.multiple_of(block * LANES, LANES), width)]
-    shift = block * LANES - start
-    window = pltpu.roll(
-        jnp.concatenate([window, window[:2]]), jnp.where(shift < 0, shift + width, shift), 1
-    )
+    window = lanes_from(faces, (me - 2) * elem_cap)
     lane = lax.broadcasted_iota(jnp.int32, (1, LANES), 1)
     span = sum((lane >= elem_cap * q).astype(jnp.int32) for q in range(1, 6))
     elem = lane - elem_cap * span
@@ -140,17 +152,11 @@
         inside = (device >= 0) & (device < devices)
         count = jnp.where(inside, counts[jnp.clip(device, 0, devices - 1)], 0)
         limit = jnp.where(span == q, count, limit)
-    local = [(window[k : k + 1, :LANES] - me * face_dev) for k in range(6)]
+    local = [(window[k : k + 1] - me * face_dev) for k in range(6)]
     hits = [(x >= 0) & (x < face_dev) & (elem < limit) for x in local]
     ones = [hit.astype(jnp.float32) for hit in hits]
     column = sum(ones)
-    before = jnp.broadcast_to(column, (8, LANES))
-    elems = jnp.broadcast_to(elem, (8, LANES))
-    step = 1
-    while step < elem_cap:
-        before = before + jnp.where(elems >= step, pltpu.roll(before, step, 1), 0.0)
-        step *= 2
-    rank = before[:1] - column
+    rank = sum_before(jnp.broadcast_to(column, (8, LANES)), elem, elem_cap)[:1]
     found = [jnp.zeros((1, LANES), jnp.float32) for _ in range(SLOT)]
     for k in range(6):
         value = jnp.where(hits[k], local[k].astype(jnp.float32), 0.0)
@@ -211,80 +217,77 @@
                 swap[group * SLOT + r] = tile
 
 
+def own_lists(me, elem_cap, face_dev, faces, orient, counts):
+    window = lanes_from(faces, me * elem_cap)
+    codes = lanes_from(orient, me * elem_cap)
+    lane = lax.broadcasted_iota(jnp.int32, (1, LANES), 1)
+    every = lax.broadcasted_iota(jnp.int32, (1, counts.shape[0]), 1)
+    count = jnp.sum(jnp.where(every == me, counts[...].reshape(every.shape), 0).astype(jnp.float32))
+    used = lane.astype(jnp.float32) < count
+    rel = [window[k : k + 1] - (me - 2) * face_dev for k in range(6)]
+    owner = [sum((x >= face_dev * j).astype(jnp.int32) for j in range(1, 5)) for x in rel]
+    owner = [jnp.where(used, x, 2) for x in owner]
+    others = [0, 1, 3, 4]
+    column = [sum((x == j).astype(jnp.float32) for x in owner) for j in others]
+    column = jnp.concatenate(column + [jnp.zeros((4, LANES), jnp.float32)])
+    ranks = sum_before(column, lane, elem_cap).astype(jnp.int32)
+    heads = []
+    for i, j in enumerate(others):
+        base = sum(
+            jnp.where(device == me + j - 2, group * SLOT, 0)
+            for group, device in enumerate(partners(me))
+        )
+        heads.append(ranks[i : i + 1] + base)
+    gather, home, slots, picks = [], [], [], []
+    for k in range(6):
+        slot = jnp.full_like(lane, 4 * SLOT)
+        for i, j in enumerate(others):
+            hit = owner[k] == j
+            slot = jnp.where(hit, heads[i], slot)
+            heads[i] = heads[i] + hit.astype(jnp.int32)
+        place = jnp.where(used & (owner[k] == 2), rel[k] - 2 * face_dev, face_dev)
+        gather.append(jnp.where(slot < SLOT, face_dev + 1 + slot, place))
+        home.append(place)
+        slots.append(slot)
+        picks.append(codes[k : k + 1] + 8 * k)
+    return gather, home, slots, picks
+
+
 def home_kernel(
     elem_cap,
-    faces_hbm,
-    orient_hbm,
-    counts_hbm,
-    tables_hbm,
-    rounded,
-    from_sib,
-    mats,
-    home,
-    remote,
-    index_in,
-    index_out,
-    terms,
     faces,
     orient,
     counts,
     tables,
+    rounded,
+    from_sib,
+    mats,
+    terms,
+    sums,
+    remote,
+    index_in,
     table,
     rows,
-    heads,
-    sems,
 ):
     me = lax.axis_index("elem")
     face_dev, functionals, _ = rounded.shape
-    live = elem_cap - elem_cap // 4
+    live = rows.shape[0]
     trace_len = mats.shape[1] // 6
     gap = LANES - trace_len
-    far = 4 * SLOT
-    copies = start_all(
-        [(faces_hbm, faces), (orient_hbm, orient), (counts_hbm, counts), (tables_hbm, tables)], sems
-    )
     table[:face_dev] = rounded[...]
     table[face_dev] = jnp.zeros((functionals, LANES), jnp.bfloat16)
     table[face_dev + 1 :] = from_sib[:SLOT]
-    for copy in copies:
-        copy.wait()
-    groups = list(partners(me))
-    for group, device in enumerate(groups):
-        heads[device - me + 2] = group * SLOT
-    heads[2] = 0
-    index_in[...] = jnp.zeros_like(index_in)
-    remote[...] = jnp.full(remote.shape, live * 8)
-    count = counts[me]
-    magic = (1 << 16) // face_dev + 1
-    places = []
-    picks = []
-    for e in range(live):
-        for k in range(6):
-            rel = faces[k, me * elem_cap + e] - (me - 2) * face_dev
-            used = e < count
-            rel = jnp.where(used, rel, 2 * face_dev)
-            owner = (rel * magic) >> 16
-            head = heads[owner]
-            heads[owner] = head + 1
-            at_home = owner == 2
-            place = jnp.where(at_home & used, rel - 2 * face_dev, face_dev)
-            home[6 * e + k] = place
-            slot = jnp.where(at_home, far, head)
-            places.append(jnp.where(slot < SLOT, face_dev + 1 + slot, place))
-            remote[pl.ds(slot, 1), :] = jnp.full((1, LANES), e * 8 + k)
-            pick = k * 8 + orient[k, me * elem_cap + e]
-            picks.append(pick)
-            index_in[pl.ds(slot, 1), :] = tables[1, pl.ds(pick, 1), :]
-            index_out[pl.ds(6 * e + k, 1), :] = tables[2, pl.ds(pick, 1), :]
+    gather, home, slots, picks = own_lists(me, elem_cap, face_dev, faces, orient, counts)
+    packed = [gather[k] * 64 + picks[k] for k in range(6)]
+    for k in range(6):
+        sums[k : k + 1, :] = home[k] * 64 + picks[k]
     lane = lax.broadcasted_iota(jnp.int32, (functionals, LANES), 1)
     for e in range(live):
-        parts = [
-            permuted(
-                table[places[6 * e + k]].astype(jnp.float32),
-                tables[0, pl.ds(picks[6 * e + k], 1), :],
-            )
-            for k in range(6)
-        ]
+        parts = []
+        for k in range(6):
+            code = packed[k][0, e]
+            tile = table[code >> 6].astype(jnp.float32)
+            parts.append(permuted(tile, tables[0, pl.ds(code & 63, 1), :]))
         for k in range(6):
             later = parts[k + 1] if k < 5 else jnp.zeros_like(parts[k])
             merged = jnp.where(lane < trace_len - gap * k, parts[k], later)
@@ -293,12 +296,21 @@
         terms[e, :, : 6 * trace_len] = jnp.dot(
             rows[e, :, : 6 * trace_len], mats[e], preferred_element_type=jnp.float32
         )
+    elem = lax.broadcasted_iota(jnp.int32, (1, LANES), 1)
+    for t in range(4 * SLOT):
+        entry = jnp.zeros((1, LANES), jnp.float32)
+        for k in range(6):
+            code = ((elem - live) * 8 + k) * 64 + picks[k]
+            entry = entry + jnp.where(slots[k] == t, code.astype(jnp.float32), 0.0)
+        code = jnp.sum(entry).astype(jnp.int32) + live * 512
+        remote[t : t + 1, :] = jnp.full((1, LANES), code)
+        index_in[t : t + 1, :] = tables[1, pl.ds(code & 63, 1), :]
 
 
 def remote_kernel(
     remote,
     index_in,
-    index_out,
+    tables,
     from_sib,
     from_even,
     from_odd,
@@ -328,8 +340,8 @@
         for r in range(SLOT):
             t = group * SLOT + r
             packed = packs[t, 0]
-            e, k = packed >> 3, packed & 7
-            where.append((e, k))
+            e, k = packed >> 9, (packed >> 6) & 7
+            where.append((e, k, packed & 63))
             if group == SIB:
                 continue
             start = jnp.minimum((trace_len * k) >> 4 << 4, last)
@@ -350,35 +362,35 @@
     for group in range(4):
         for r in range(SLOT):
             t = group * SLOT + r
-            e, k = where[t]
+            e, k, pick = where[t]
             tile = terms[e, :, pl.ds(pl.multiple_of(k * LANES, LANES), LANES)]
             ahead = jnp.maximum(k - 1, 0)
             left = terms[e, :, pl.ds(pl.multiple_of(ahead * LANES, LANES), LANES)]
             tile = jnp.where(lane >= LANES - gap * k, left, tile)
-            pick = jnp.minimum(6 * e + k, 6 * live - 1)
-            tile = permuted(tile, index_out[pl.ds(pick, 1), :]).astype(jnp.bfloat16)
+            tile = permuted(tile, tables[2, pl.ds(pick, 1), :]).astype(jnp.bfloat16)
             if group == CROSS:
                 cross[r] = tile
             else:
                 swap[group * SLOT + r] = tile
 
 
-def scatter_kernel(home, index_out, terms, rhs, base):
+def scatter_kernel(sums, tables, terms, rhs, base):
     face_dev, functionals, trace_len = rhs.shape
     live = terms.shape[0] - 1
     gap = LANES - trace_len
     lane = lax.broadcasted_iota(jnp.int32, (functionals, LANES), 1)
     base[:face_dev, :, :trace_len] = rhs[...].astype(jnp.float32)
     base[face_dev] = jnp.zeros((functionals, LANES), jnp.float32)
+    codes = sums[...]
     for e in range(live):
         for k in range(6):
             tile = terms[e, :, k * LANES : (k + 1) * LANES]
             if k:
                 left = terms[e, :, (k - 1) * LANES : k * LANES]
                 tile = jnp.where(lane >= LANES - gap * k, left, tile)
-            i = 6 * e + k
-            tile = permuted(tile, index_out[i : i + 1, :])
-            place = home[i]
+            code = codes[k, e]
+            tile = permuted(tile, tables[2, pl.ds(code & 63, 1), :])
+            place = code >> 6
             base[place] -= tile.astype(jnp.bfloat16).astype(jnp.float32)
 
 
@@ -423,9 +435,7 @@
         return pltpu.with_memory_space_constraint(array, pltpu.VMEM)
 
     faces = in_hbm(elem_faces.T)
-    codes = in_hbm(orient.T)
-    counts = in_hbm(counts)
-    tables = lane_tables(trace_len)
+    tables = jnp.asarray(lane_tables(trace_len))
     vmem = pl.BlockSpec(memory_space=pltpu.VMEM)
     smem = pl.BlockSpec(memory_space=pltpu.SMEM)
     hbm = pl.BlockSpec(memory_space=pltpu.HBM)
@@ -437,7 +447,6 @@
         return jax.ShapeDtypeStruct(shape, jnp.int32)
 
     params = pltpu.CompilerParams(vmem_limit_bytes=4 << 20)
-    faces_smem = pltpu.SMEM(faces.shape, jnp.int32)
     counts_smem = pltpu.SMEM(counts.shape, jnp.int32)
     traces, rounded, swap, cross, slots = pl.pallas_call(
         functools.partial(first_kernel, elem_cap, devices),
@@ -462,28 +471,21 @@
             flops=10**11, bytes_accessed=10**8, transcendentals=0
         ),
         name="first_sweep",
-    )(faces, counts, in_hbm(rhs), in_hbm(face_blocks))
+    )(faces, in_hbm(counts), in_hbm(rhs), in_hbm(face_blocks))
     from_sib, from_even, from_odd = exchange(routes, swap, cross)
-    home, remote, index_in, index_out, terms = pl.pallas_call(
+    terms, sums, remote, index_in = pl.pallas_call(
         functools.partial(home_kernel, elem_cap),
         out_shape=(
-            integers(6 * live),
-            integers(far + 1, LANES),
-            integers(far + 1, LANES),
-            integers(6 * live, LANES),
             tiles(live, jnp.float32, 6 * LANES),
+            integers(6, LANES),
+            integers(far, LANES),
+            integers(far, LANES),
         ),
-        in_specs=[hbm] * 4 + [vmem] * 3,
-        out_specs=(smem,) + (vmem,) * 4,
+        in_specs=[vmem] * 7,
+        out_specs=(vmem,) * 4,
         scratch_shapes=[
-            faces_smem,
-            faces_smem,
-            counts_smem,
-            pltpu.VMEM(tables.shape, jnp.int32),
             pltpu.VMEM((face_dev + 1 + SLOT, functionals, LANES), jnp.bfloat16),
             pltpu.VMEM((live, functionals, 6 * LANES), jnp.bfloat16),
-            pltpu.SMEM((8,), jnp.int32),
-            pltpu.SemaphoreType.DMA((4,)),
         ],
         compiler_params=params,
         cost_estimate=pl.CostEstimate(
@@ -492,7 +494,7 @@
             transcendentals=0,
         ),
         name="home_terms",
-    )(faces, codes, counts, in_hbm(jnp.asarray(tables)), rounded, from_sib, in_vmem(elem_mats))
+    )(elem_faces.T, orient.T, counts, tables, rounded, from_sib, in_vmem(elem_mats))
     swap, cross, terms = pl.pallas_call(
         remote_kernel,
         out_shape=(
@@ -504,16 +506,16 @@
         out_specs=(vmem,) * 3,
         compiler_params=params,
         name="remote_terms",
-    )(remote, index_in, index_out, from_sib, from_even, from_odd, terms, in_vmem(elem_mats))
+    )(remote, index_in, tables, from_sib, from_even, from_odd, terms, in_vmem(elem_mats))
     from_sib, from_even, from_odd = exchange(routes, swap, cross)
     base = pl.pallas_call(
         scatter_kernel,
         out_shape=tiles(face_dev + 1, jnp.float32),
-        in_specs=[smem] + [vmem] * 3,
+        in_specs=[vmem] * 4,
         out_specs=vmem,
         compiler_params=params,
         name="home_sum",
-    )(home, index_out, terms, rhs)
+    )(sums, tables, terms, rhs)
     return pl.pallas_call(
         last_kernel,
         out_shape=jax.ShapeDtypeStruct(rhs.shape, jnp.float32),

time: 18.7 us -> 17.9 us (0.957)
  the two profiles are of different devices: /device:TPU:0 before, /device:TPU:25 now
where the time goes in v4:
time: 17.9 us; the launch traced here: 17.6 us
  Pallas kernels  6.16 us (34%)
  starting transfers between devices  5.91 us (33%)
  waiting for transfers between devices  5.4 us (30%)
    ppermute x2, starting transfers between devices, exchange(): lax.ppermute(odd, 'elem', odd_chips)  4.33 us
    ppermute x2, waiting for transfers between devices, exchange(): lax.ppermute(odd, 'elem', odd_chips)  2.92 us
    pallas_call x1, Pallas kernels, per_device(): pl.pallas_call(functools.partial(home_kernel, elem_cap), out_shape=(tiles...  2.08 us
    ppermute x2, waiting for transfers between devices, exchange(): got = lax.ppermute(swap, 'elem', sibling)  1.96 us
    pallas_call x1, Pallas kernels, per_device(): pl.pallas_call(functools.partial(first_kernel, elem_cap, devices), out_sh...  1.81 us
    pallas_call x1, Pallas kernels, per_device(): pl.pallas_call(last_kernel, out_shape=jax.ShapeDtypeStruct(rhs.shape, jnp...  1.12 us
    ppermute x2, starting transfers between devices, exchange(): got = lax.ppermute(swap, 'elem', sibling)  0.96 us
    pallas_call x1, Pallas kernels, per_device(): pl.pallas_call(remote_kernel, out_shape=(tiles(3 * SLOT, jnp.bfloat16), t...  0.67 us
  transfers between devices with their start and end apart: 6, of which 6 were waited for; matrix products, arithmetic and copies ran while one was open for 0% of the time, Pallas kernels for 15%

profile of v4, /device:TPU:25, one launch (start us, length us, event | category | flops | bytes accessed | tf_op | source)
XLA Modules:
  0.0 17.6 jit_solution(3341146709542381948)
XLA Ops:
  0.0 0.0 copy-start.5
  0.0 0.0 copy-start.6
  0.0 1.8 %first_sweep.1 = (f32[27,16,128]{2,1,0:T(8,128)S(1)}, bf16[27,16,128]{2,1,0:T(8,128)(2,1)S(1)}, bf16[12,16,128]{2,1,0:T(8,128)(2,1)S(1)}, bf16[4,16,128]{2,1,0:T(8,128)(2,1)S(1)}, s32[16,128]{1,0:T(8,128)S(1)}) custom-call(s32[6,384]{1,0:T(8,128)} %bitcast.2, s32[32]{0:T(128)} %counts.1, bf16[27,16,125]{2,1,0:T(8,128)(2,1)} %rhs.1, bf16[27,125,125]{2,1,0:T(8,128)(2,1)} %blocks.1), custom_call_target="tpu_custom_call" | custom-call | flops 99999997952 | bytes 100000000 | tf_op jit(solution)/shard_map/first_sweep/pallas_call | solution.py:451
  1.9 0.7 %collective-permute-start = (bf16[12,16,128]{2,1,0:T(8,128)(2,1)S(1)}, bf16[12,16,128]{2,1,0:T(8,128)(2,1)S(1)}, u32[]{:S(2)}, u32[]{:S(2)}) collective-permute-start(bf16[12,16,128]{2,1,0:T(8,128)(2,1)S(1)} %get-tuple-element.19), channel_id=1, source_target_pairs={{0,1},{1,0},{2,3},{3,2},{4,5},{5,4},{6,7},{7,6},{8,9},{9,8},{10,11... | collective-permute-start | bytes 147464 | tf_op jit(solution)/shard_map/ppermute | solution.py:418
  2.6 0.9 %collective-permute-done.from_sib = bf16[12,16,128]{2,1,0:T(8,128)(2,1)S(1)} collective-permute-done((bf16[12,16,128]{2,1,0:T(8,128)(2,1)S(1)}, bf16[12,16,128]{2,1,0:T(8,128)(2,1)S(1)}, u32[]{:S(2)}, u32[]{:S(2)}) %collective-permute-start) | collective-permute-done | bytes 49184 | tf_op jit(solution)/shard_map/ppermute | solution.py:418
  3.5 2.4 %collective-permute-start.2 = (bf16[8,16,128]{2,1,0:T(8,128)(2,1)S(1)}, bf16[8,16,128]{2,1,0:T(8,128)(2,1)S(1)}, u32[]{:S(2)}, u32[]{:S(2)}) collective-permute-start(bf16[8,16,128]{2,1,0:T(8,128)(2,1)S(1)} %get-tuple-element.35), channel_id=1, source_target_pairs={{0,1},{1,0},{2,5},{3,4},{4,3},{5,2},{6,9},{7,8},{8,7},{9,6},{10,13... | collective-permute-start | bytes 98312 | tf_op jit(solution)/shard_map/ppermute | solution.py:421
  5.8 0.4 %collective-permute-start.1 = (bf16[8,16,128]{2,1,0:T(8,128)(2,1)S(1)}, bf16[8,16,128]{2,1,0:T(8,128)(2,1)S(1)}, u32[]{:S(2)}, u32[]{:S(2)}) collective-permute-start(bf16[8,16,128]{2,1,0:T(8,128)(2,1)S(1)} %get-tuple-element.36), channel_id=1, source_target_pairs={{0,3},{1,2},{2,1},{3,0},{4,7},{5,6},{6,5},{7,4},{8,11},{9,10},{10,... | collective-permute-start | bytes 98312 | tf_op jit(solution)/shard_map/ppermute | solution.py:421
  6.3 0.0 copy-done
  6.3 0.0 copy-done.2
  6.3 0.0 copy-done.6
  6.3 0.0 copy-start.3
  6.3 0.0 copy-start.1
  6.3 2.1 %home_terms.1 = (f32[9,16,768]{2,1,0:T(8,128)S(1)}, s32[6,128]{1,0:T(8,128)S(1)}, s32[16,128]{1,0:T(8,128)S(1)}, s32[16,128]{1,0:T(8,128)S(1)}) custom-call(s32[6,384]{1,0:T(8,128)S(1)} %bitcast.3, s32[6,384]{1,0:T(8,128)S(1)} %bitcast.4, s32[32]{0:T(128)S(1)} %copy-done.6, s32[3,48,128]{2,1,0:T(8,128)S(1)} %copy-done.2, ...), custom_call_target="tpu_custom_call" | custom-call | flops 162000000 | bytes 10125000 | tf_op jit(solution)/shard_map/home_terms/pallas_call | solution.py:476
  8.4 0.4 %collective-permute-done.2.from_odd = bf16[8,16,128]{2,1,0:T(8,128)(2,1)S(1)} collective-permute-done((bf16[8,16,128]{2,1,0:T(8,128)(2,1)S(1)}, bf16[8,16,128]{2,1,0:T(8,128)(2,1)S(1)}, u32[]{:S(2)}, u32[]{:S(2)}) %collective-permute-start.2) | collective-permute-done | bytes 32800 | tf_op jit(solution)/shard_map/ppermute | solution.py:421
  8.7 0.4 %collective-permute-done.1.from_even = bf16[8,16,128]{2,1,0:T(8,128)(2,1)S(1)} collective-permute-done((bf16[8,16,128]{2,1,0:T(8,128)(2,1)S(1)}, bf16[8,16,128]{2,1,0:T(8,128)(2,1)S(1)}, u32[]{:S(2)}, u32[]{:S(2)}) %collective-permute-start.1) | collective-permute-done | bytes 32800 | tf_op jit(solution)/shard_map/ppermute | solution.py:421
  9.2 0.7 %remote_terms.1 = (bf16[12,16,128]{2,1,0:T(8,128)(2,1)S(1)}, bf16[4,16,128]{2,1,0:T(8,128)(2,1)S(1)}, f32[10,16,768]{2,1,0:T(8,128)S(1)}) custom-call(s32[16,128]{1,0:T(8,128)S(1)} %get-tuple-element.21.remote, s32[16,128]{1,0:T(8,128)S(1)} %get-tuple-element.22.index_in, s32[3,48,128]{2,1,0:T(8,128)S(1)} %copy-done.2, ...), custom_call_target="tpu_custom_call" | custom-call | tf_op jit(solution)/shard_map/remote_terms/pallas_call | solution.py:498
  9.9 0.2 %collective-permute-start.3 = (bf16[12,16,128]{2,1,0:T(8,128)(2,1)S(1)}, bf16[12,16,128]{2,1,0:T(8,128)(2,1)S(1)}, u32[]{:S(2)}, u32[]{:S(2)}) collective-permute-start(bf16[12,16,128]{2,1,0:T(8,128)(2,1)S(1)} %get-tuple-element.26), channel_id=1, source_target_pairs={{0,1},{1,0},{2,3},{3,2},{4,5},{5,4},{6,7},{7,6},{8,9},{9,8},{10,11... | collective-permute-start | bytes 147464 | tf_op jit(solution)/shard_map/ppermute | solution.py:418
  10.1 1.1 %collective-permute-done.3.from_sib = bf16[12,16,128]{2,1,0:T(8,128)(2,1)S(1)} collective-permute-done((bf16[12,16,128]{2,1,0:T(8,128)(2,1)S(1)}, bf16[12,16,128]{2,1,0:T(8,128)(2,1)S(1)}, u32[]{:S(2)}, u32[]{:S(2)}) %collective-permute-start.3) | collective-permute-done | bytes 49184 | tf_op jit(solution)/shard_map/ppermute | solution.py:418
  11.2 2.0 %collective-permute-start.5 = (bf16[8,16,128]{2,1,0:T(8,128)(2,1)S(1)}, bf16[8,16,128]{2,1,0:T(8,128)(2,1)S(1)}, u32[]{:S(2)}, u32[]{:S(2)}) collective-permute-start(bf16[8,16,128]{2,1,0:T(8,128)(2,1)S(1)} %get-tuple-element.33), channel_id=1, source_target_pairs={{0,1},{1,0},{2,5},{3,4},{4,3},{5,2},{6,9},{7,8},{8,7},{9,6},{10,13... | collective-permute-start | bytes 98312 | tf_op jit(solution)/shard_map/ppermute | solution.py:421
  13.1 0.2 %collective-permute-start.4 = (bf16[8,16,128]{2,1,0:T(8,128)(2,1)S(1)}, bf16[8,16,128]{2,1,0:T(8,128)(2,1)S(1)}, u32[]{:S(2)}, u32[]{:S(2)}) collective-permute-start(bf16[8,16,128]{2,1,0:T(8,128)(2,1)S(1)} %get-tuple-element.34), channel_id=1, source_target_pairs={{0,3},{1,2},{2,1},{3,0},{4,7},{5,6},{6,5},{7,4},{8,11},{9,10},{10,... | collective-permute-start | bytes 98312 | tf_op jit(solution)/shard_map/ppermute | solution.py:421
  13.3 0.5 %home_sum.1.base = f32[28,16,128]{2,1,0:T(8,128)S(1)} custom-call(s32[6,128]{1,0:T(8,128)S(1)} %get-tuple-element.20.sums, s32[3,48,128]{2,1,0:T(8,128)S(1)} %copy-done.2, f32[10,16,768]{2,1,0:T(8,128)S(1)} %get-tuple-element.25.terms, bf16[27,16,125]{2,1,0:T(8,128)(2,1)S(1)} %copy-done.3), custom_call_target="tpu_custom_call" | custom-call | tf_op jit(solution)/shard_map/home_sum/pallas_call | solution.py:511
  13.8 2.6 %collective-permute-done.5.from_odd = bf16[8,16,128]{2,1,0:T(8,128)(2,1)S(1)} collective-permute-done((bf16[8,16,128]{2,1,0:T(8,128)(2,1)S(1)}, bf16[8,16,128]{2,1,0:T(8,128)(2,1)S(1)}, u32[]{:S(2)}, u32[]{:S(2)}) %collective-permute-start.5) | collective-permute-done | bytes 32800 | tf_op jit(solution)/shard_map/ppermute | solution.py:421
  16.4 0.1 collective-permute-done.4.from_even
  16.5 1.1 %last_update.1 = f32[27,16,125]{2,1,0:T(8,128)} custom-call(s32[16,128]{1,0:T(8,128)S(1)} %get-tuple-element.17.slots, f32[28,16,128]{2,1,0:T(8,128)S(1)} %home_sum.1.base, bf16[12,16,128]{2,1,0:T(8,128)(2,1)S(1)} %collective-permute-done.3.from_sib, bf16[8,16,128]{2,1,0:T(8,128)(2,1)S(1)} %collective-permute-done.4.from_even, ...), custom_call_target="tpu_custom_call" | custom-call | tf_op jit(solution)/shard_map/last_update/pallas_call | solution.py:519
  (11 shorter events, 0.0 us)
Async XLA Ops:
  0.0 6.3 %copy-start = (bf16[12,750,750]{2,1,0:T(8,128)(2,1)S(1)}, bf16[12,750,750]{2,1,0:T(8,128)(2,1)}, u32[]{:S(2)}) copy-start(bf16[12,750,750]{2,1,0:T(8,128)(2,1)} %mats.3) | copy-start | bytes 40500004
  0.0 6.3 %copy-start.2 = (s32[3,48,128]{2,1,0:T(8,128)S(1)}, s32[3,48,128]{2,1,0:T(8,128)}, u32[]{:S(2)}) copy-start(s32[3,48,128]{2,1,0:T(8,128)} %constant.2.clone.tables) | copy-start | bytes 221188
  0.0 6.3 %copy-start.4 = (s32[384,6]{0,1:T(8,128)S(1)}, s32[384,6]{0,1:T(8,128)}, u32[]{:S(2)}) copy-start(s32[384,6]{0,1:T(8,128)} %param.10) | copy-start | bytes 27652
  0.0 6.3 %copy-start.5 = (s32[384,6]{0,1:T(8,128)S(1)}, s32[384,6]{0,1:T(8,128)}, u32[]{:S(2)}) copy-start(s32[384,6]{0,1:T(8,128)} %param.11) | copy-start | bytes 27652
  0.0 6.3 %copy-start.6 = (s32[32]{0:T(128)S(1)}, s32[32]{0:T(128)}, u32[]{:S(2)}) copy-start(s32[32]{0:T(128)} %counts.1) | copy-start | bytes 388
  1.9 1.6 %collective-permute-start = (bf16[12,16,128]{2,1,0:T(8,128)(2,1)S(1)}, bf16[12,16,128]{2,1,0:T(8,128)(2,1)S(1)}, u32[]{:S(2)}, u32[]{:S(2)}) collective-permute-start(bf16[12,16,128]{2,1,0:T(8,128)(2,1)S(1)} %get-tuple-element.19), channel_id=1, source_target_pairs={{0,1},{1,0},{2,3},{3,2},{4,5},{5,4},{6,7},{7,6},{8,9},{9,8},{10,11... | collective-permute-start | bytes 147464 | tf_op jit(solution)/shard_map/ppermute | solution.py:418
  3.5 5.2 %collective-permute-start.2 = (bf16[8,16,128]{2,1,0:T(8,128)(2,1)S(1)}, bf16[8,16,128]{2,1,0:T(8,128)(2,1)S(1)}, u32[]{:S(2)}, u32[]{:S(2)}) collective-permute-start(bf16[8,16,128]{2,1,0:T(8,128)(2,1)S(1)} %get-tuple-element.35), channel_id=1, source_target_pairs={{0,1},{1,0},{2,5},{3,4},{4,3},{5,2},{6,9},{7,8},{8,7},{9,6},{10,13... | collective-permute-start | bytes 98312 | tf_op jit(solution)/shard_map/ppermute | solution.py:421
  5.8 3.3 %collective-permute-start.1 = (bf16[8,16,128]{2,1,0:T(8,128)(2,1)S(1)}, bf16[8,16,128]{2,1,0:T(8,128)(2,1)S(1)}, u32[]{:S(2)}, u32[]{:S(2)}) collective-permute-start(bf16[8,16,128]{2,1,0:T(8,128)(2,1)S(1)} %get-tuple-element.36), channel_id=1, source_target_pairs={{0,3},{1,2},{2,1},{3,0},{4,7},{5,6},{6,5},{7,4},{8,11},{9,10},{10,... | collective-permute-start | bytes 98312 | tf_op jit(solution)/shard_map/ppermute | solution.py:421
  6.3 7.1 %copy-start.3 = (bf16[27,16,125]{2,1,0:T(8,128)(2,1)S(1)}, bf16[27,16,125]{2,1,0:T(8,128)(2,1)}, u32[]{:S(2)}) copy-start(bf16[27,16,125]{2,1,0:T(8,128)(2,1)} %rhs.1) | copy-start | bytes 324004
  6.3 10.2 %copy-start.1 = (bf16[27,125,125]{2,1,0:T(8,128)(2,1)S(1)}, bf16[27,125,125]{2,1,0:T(8,128)(2,1)}, u32[]{:S(2)}) copy-start(bf16[27,125,125]{2,1,0:T(8,128)(2,1)} %blocks.1) | copy-start | bytes 2531254
  9.9 1.3 %collective-permute-start.3 = (bf16[12,16,128]{2,1,0:T(8,128)(2,1)S(1)}, bf16[12,16,128]{2,1,0:T(8,128)(2,1)S(1)}, u32[]{:S(2)}, u32[]{:S(2)}) collective-permute-start(bf16[12,16,128]{2,1,0:T(8,128)(2,1)S(1)} %get-tuple-element.26), channel_id=1, source_target_pairs={{0,1},{1,0},{2,3},{3,2},{4,5},{5,4},{6,7},{7,6},{8,9},{9,8},{10,11... | collective-permute-start | bytes 147464 | tf_op jit(solution)/shard_map/ppermute | solution.py:418
  11.2 5.2 %collective-permute-start.5 = (bf16[8,16,128]{2,1,0:T(8,128)(2,1)S(1)}, bf16[8,16,128]{2,1,0:T(8,128)(2,1)S(1)}, u32[]{:S(2)}, u32[]{:S(2)}) collective-permute-start(bf16[8,16,128]{2,1,0:T(8,128)(2,1)S(1)} %get-tuple-element.33), channel_id=1, source_target_pairs={{0,1},{1,0},{2,5},{3,4},{4,3},{5,2},{6,9},{7,8},{8,7},{9,6},{10,13... | collective-permute-start | bytes 98312 | tf_op jit(solution)/shard_map/ppermute | solution.py:421
  13.1 3.3 %collective-permute-start.4 = (bf16[8,16,128]{2,1,0:T(8,128)(2,1)S(1)}, bf16[8,16,128]{2,1,0:T(8,128)(2,1)S(1)}, u32[]{:S(2)}, u32[]{:S(2)}) collective-permute-start(bf16[8,16,128]{2,1,0:T(8,128)(2,1)S(1)} %get-tuple-element.34), channel_id=1, source_target_pairs={{0,3},{1,2},{2,1},{3,0},{4,7},{5,6},{6,5},{7,4},{8,11},{9,10},{10,... | collective-permute-start | bytes 98312 | tf_op jit(solution)/shard_map/ppermute | solution.py:421

commit v5 on v4

--- a/solution.py
+++ b/solution.py
@@ -97,15 +97,15 @@
     )
 
 
-def arrivals(me, from_sib, from_even, from_odd):
-    shape = from_sib.shape[1:]
-    by_even = jnp.broadcast_to(((me ^ (me >> 1)) & 1) == 1, shape)
-    return [
-        [from_sib[r] for r in range(SLOT)],
-        [from_even[SLOT + r] for r in range(SLOT)],
-        [from_odd[SLOT + r] for r in range(SLOT)],
-        [jnp.where(by_even, from_even[r], from_odd[r]) for r in range(SLOT)],
-    ]
+def crossing_bucket(from_even, from_odd):
+    me = lax.axis_index("elem")
+    by_even = jnp.broadcast_to(((me ^ (me >> 1)) & 1) == 1, from_even.shape[1:])
+    return [jnp.where(by_even, from_even[r], from_odd[r]) for r in range(SLOT)]
+
+
+def put_bucket(group, r, tile, swap, even):
+    target, first = {SIB: (swap, 0), ODD: (swap, SLOT), CROSS: (even, 0), EVEN: (even, SLOT)}[group]
+    target[first + r] = tile
 
 
 def start_all(pairs, sems):
@@ -182,7 +182,7 @@
     traces,
     rounded,
     swap,
-    cross,
+    even,
     slots,
     faces,
     counts,
@@ -204,17 +204,13 @@
     copies[3].wait()
     for f in range(face_dev):
         value = jnp.dot(rhs[f], blocks[f], preferred_element_type=jnp.float32)
-        traces[f] = jnp.zeros((functionals, LANES), jnp.float32)
         traces[f, :, :trace_len] = value
-        rounded[f] = traces[f].astype(jnp.bfloat16)
+        rounded[f, :, :trace_len] = value.astype(jnp.bfloat16)
     for group in range(4):
         for r in range(SLOT):
             slot = picked[group * SLOT + r]
             tile = rounded[jnp.where(slot < face_dev, slot, 0)]
-            if group == CROSS:
-                cross[r] = tile
-            else:
-                swap[group * SLOT + r] = tile
+            put_bucket(group, r, tile, swap, even)
 
 
 def own_lists(me, elem_cap, face_dev, faces, orient, counts):
@@ -253,7 +249,7 @@
     return gather, home, slots, picks
 
 
-def home_kernel(
+def rows_kernel(
     elem_cap,
     faces,
     orient,
@@ -261,18 +257,16 @@
     tables,
     rounded,
     from_sib,
-    mats,
-    terms,
+    rows,
     sums,
     remote,
     index_in,
     table,
-    rows,
 ):
     me = lax.axis_index("elem")
     face_dev, functionals, _ = rounded.shape
     live = rows.shape[0]
-    trace_len = mats.shape[1] // 6
+    trace_len = COMP * EDGE * EDGE
     gap = LANES - trace_len
     table[:face_dev] = rounded[...]
     table[face_dev] = jnp.zeros((functionals, LANES), jnp.bfloat16)
@@ -292,10 +286,6 @@
             later = parts[k + 1] if k < 5 else jnp.zeros_like(parts[k])
             merged = jnp.where(lane < trace_len - gap * k, parts[k], later)
             rows[e, :, k * LANES : (k + 1) * LANES] = merged.astype(jnp.bfloat16)
-    for e in range(live):
-        terms[e, :, : 6 * trace_len] = jnp.dot(
-            rows[e, :, : 6 * trace_len], mats[e], preferred_element_type=jnp.float32
-        )
     elem = lax.broadcasted_iota(jnp.int32, (1, LANES), 1)
     for t in range(4 * SLOT):
         entry = jnp.zeros((1, LANES), jnp.float32)
@@ -307,71 +297,68 @@
         index_in[t : t + 1, :] = tables[1, pl.ds(code & 63, 1), :]
 
 
-def remote_kernel(
-    remote,
-    index_in,
-    tables,
-    from_sib,
-    from_even,
-    from_odd,
-    before,
-    mats,
-    swap,
-    cross,
-    terms,
-):
-    me = lax.axis_index("elem")
-    functionals = before.shape[1]
-    live = before.shape[0]
+def home_kernel(rows, mats, terms):
+    live = rows.shape[0]
+    dof = mats.shape[1]
+    for e in range(live):
+        terms[e, :, :dof] = jnp.dot(rows[e, :, :dof], mats[e], preferred_element_type=jnp.float32)
+    terms[live] = jnp.zeros(terms.shape[1:], jnp.float32)
+
+
+def unpacked(packs, t):
+    packed = packs[t, 0]
+    return packed >> 9, (packed >> 6) & 7, packed & 63
+
+
+def add_remote(group, arrived, first, packs, index_in, mats, terms):
+    live = terms.shape[0] - 1
     trace_len = mats.shape[1] // 6
     gap = LANES - trace_len
     height, last = window_rows(trace_len)
-    terms[:live] = before[...]
-    terms[live] = jnp.zeros(terms.shape[1:], jnp.float32)
-    lane = lax.broadcasted_iota(jnp.int32, (functionals, LANES), 1)
-    arrived = arrivals(me, from_sib, from_even, from_odd)
-    turned = [
-        permuted(arrived[t // SLOT][t % SLOT].astype(jnp.float32), index_in[t : t + 1, :])
-        for t in range(4 * SLOT)
-    ]
+    lane = lax.broadcasted_iota(jnp.int32, arrived[first].shape, 1)
+    for r in range(SLOT):
+        t = group * SLOT + r
+        e, k, _ = unpacked(packs, t)
+        start = jnp.minimum((trace_len * k) >> 4 << 4, last)
+        shift = trace_len * k - start
+        tile = permuted(arrived[first + r].astype(jnp.float32), index_in[t : t + 1, :])
+        zero = jnp.zeros_like(tile)
+        wide = jnp.concatenate(
+            [
+                jnp.where((lane >= shift) & (lane < shift + trace_len), tile, zero),
+                jnp.where(lane < shift - gap, tile, zero),
+            ],
+            axis=1,
+        ).astype(jnp.bfloat16)
+        window = mats[jnp.minimum(e, live - 1), pl.ds(pl.multiple_of(start, 16), height), :]
+        terms[e, :, : 6 * trace_len] += jnp.dot(
+            wide[:, :height], window, preferred_element_type=jnp.float32
+        )
+
+
+def relay_kernel(from_even, _, out):
+    out[...] = from_even[SLOT:]
+
+
+def remote_kernel(
+    remote, index_in, tables, from_even, from_odd, relayed, mats, _, swap, even, terms
+):
+    trace_len = mats.shape[1] // 6
+    gap = LANES - trace_len
     packs = remote[...]
-    where = []
+    add_remote(EVEN, relayed, 0, packs, index_in, mats, terms)
+    add_remote(CROSS, crossing_bucket(from_even, from_odd), 0, packs, index_in, mats, terms)
+    add_remote(ODD, from_odd, SLOT, packs, index_in, mats, terms)
+    lane = lax.broadcasted_iota(jnp.int32, relayed.shape[1:], 1)
     for group in range(4):
         for r in range(SLOT):
-            t = group * SLOT + r
-            packed = packs[t, 0]
-            e, k = packed >> 9, (packed >> 6) & 7
-            where.append((e, k, packed & 63))
-            if group == SIB:
-                continue
-            start = jnp.minimum((trace_len * k) >> 4 << 4, last)
-            shift = trace_len * k - start
-            tile = turned[t]
-            zero = jnp.zeros_like(tile)
-            wide = jnp.concatenate(
-                [
-                    jnp.where((lane >= shift) & (lane < shift + trace_len), tile, zero),
-                    jnp.where(lane < shift - gap, tile, zero),
-                ],
-                axis=1,
-            ).astype(jnp.bfloat16)
-            window = mats[jnp.minimum(e, live - 1), pl.ds(pl.multiple_of(start, 16), height), :]
-            terms[e, :, : 6 * trace_len] += jnp.dot(
-                wide[:, :height], window, preferred_element_type=jnp.float32
-            )
-    for group in range(4):
-        for r in range(SLOT):
-            t = group * SLOT + r
-            e, k, pick = where[t]
+            e, k, pick = unpacked(packs, group * SLOT + r)
             tile = terms[e, :, pl.ds(pl.multiple_of(k * LANES, LANES), LANES)]
             ahead = jnp.maximum(k - 1, 0)
             left = terms[e, :, pl.ds(pl.multiple_of(ahead * LANES, LANES), LANES)]
             tile = jnp.where(lane >= LANES - gap * k, left, tile)
             tile = permuted(tile, tables[2, pl.ds(pick, 1), :]).astype(jnp.bfloat16)
-            if group == CROSS:
-                cross[r] = tile
-            else:
-                swap[group * SLOT + r] = tile
+            put_bucket(group, r, tile, swap, even)
 
 
 def scatter_kernel(sums, tables, terms, rhs, base):
@@ -394,16 +381,18 @@
             base[place] -= tile.astype(jnp.bfloat16).astype(jnp.float32)
 
 
-def last_kernel(slots, base, from_sib, from_even, from_odd, blocks, traces, out, residual):
-    me = lax.axis_index("elem")
+def last_kernel(
+    slots, base, from_sib, from_even, from_odd, relayed, blocks, traces, out, residual
+):
     face_dev, _, trace_len = out.shape
     residual[...] = base[...]
-    arrived = arrivals(me, from_sib, from_even, from_odd)
+    crossing = crossing_bucket(from_even, from_odd)
     places = slots[...]
-    for group in range(4):
-        for r in range(SLOT):
+    for r in range(SLOT):
+        arrived = {SIB: from_sib[r], EVEN: relayed[r], ODD: from_odd[SLOT + r], CROSS: crossing[r]}
+        for group, tile in arrived.items():
             place = places[group * SLOT + r, 0]
-            residual[place] -= arrived[group][r].astype(jnp.float32)
+            residual[place] -= tile.astype(jnp.float32)
     for f in range(face_dev):
         update = jnp.dot(
             residual[f, :, :trace_len].astype(jnp.bfloat16),
@@ -413,12 +402,12 @@
         out[f] = traces[f, :, :trace_len] + update
 
 
-def exchange(routes, swap, cross):
+def exchange(routes, swap, even):
     sibling, even_chips, odd_chips = routes
-    got = lax.ppermute(swap, "elem", sibling)
-    even = jnp.concatenate([cross, got[SLOT : 2 * SLOT]])
-    odd = jnp.concatenate([cross, got[2 * SLOT :]])
-    return got, lax.ppermute(even, "elem", even_chips), lax.ppermute(odd, "elem", odd_chips)
+    from_even = lax.ppermute(even, "elem", even_chips)
+    from_sib = lax.ppermute(swap, "elem", sibling)
+    odd = jnp.concatenate([even[:SLOT], from_sib[SLOT:]])
+    return from_sib, from_even, lax.ppermute(odd, "elem", odd_chips)
 
 
 def per_device(devices, elem_mats, face_blocks, rhs, elem_faces, orient, counts):
@@ -448,13 +437,13 @@
 
     params = pltpu.CompilerParams(vmem_limit_bytes=4 << 20)
     counts_smem = pltpu.SMEM(counts.shape, jnp.int32)
-    traces, rounded, swap, cross, slots = pl.pallas_call(
+    traces, rounded, swap, even, slots = pl.pallas_call(
         functools.partial(first_kernel, elem_cap, devices),
         out_shape=(
             tiles(face_dev, jnp.float32),
             tiles(face_dev, jnp.bfloat16),
-            tiles(3 * SLOT, jnp.bfloat16),
-            tiles(SLOT, jnp.bfloat16),
+            tiles(2 * SLOT, jnp.bfloat16),
+            tiles(2 * SLOT, jnp.bfloat16),
             integers(far, LANES),
         ),
         in_specs=[hbm] * 4,
@@ -472,21 +461,38 @@
         ),
         name="first_sweep",
     )(faces, in_hbm(counts), in_hbm(rhs), in_hbm(face_blocks))
-    from_sib, from_even, from_odd = exchange(routes, swap, cross)
-    terms, sums, remote, index_in = pl.pallas_call(
-        functools.partial(home_kernel, elem_cap),
+    def passed_on(from_even, after):
+        relay = pl.pallas_call(
+            relay_kernel,
+            out_shape=tiles(SLOT, jnp.bfloat16),
+            in_specs=[vmem, pl.BlockSpec(memory_space=pl.ANY)],
+            out_specs=vmem,
+            compiler_params=params,
+            name="relay",
+        )(from_even, after)
+        return lax.ppermute(relay, "elem", routes[0])
+
+    from_sib, from_even, from_odd = exchange(routes, swap, even)
+    all_terms = pltpu.VMEM((live + 1, functionals, 6 * LANES), jnp.float32)
+    rows, sums, remote, index_in = pl.pallas_call(
+        functools.partial(rows_kernel, elem_cap),
         out_shape=(
-            tiles(live, jnp.float32, 6 * LANES),
+            tiles(live, jnp.bfloat16, 6 * LANES),
             integers(6, LANES),
             integers(far, LANES),
             integers(far, LANES),
         ),
-        in_specs=[vmem] * 7,
+        in_specs=[vmem] * 6,
         out_specs=(vmem,) * 4,
-        scratch_shapes=[
-            pltpu.VMEM((face_dev + 1 + SLOT, functionals, LANES), jnp.bfloat16),
-            pltpu.VMEM((live, functionals, 6 * LANES), jnp.bfloat16),
-        ],
+        scratch_shapes=[pltpu.VMEM((face_dev + 1 + SLOT, functionals, LANES), jnp.bfloat16)],
+        compiler_params=params,
+        name="home_rows",
+    )(elem_faces.T, orient.T, counts, tables, rounded, from_sib)
+    terms = pl.pallas_call(
+        home_kernel,
+        out_shape=all_terms,
+        in_specs=[vmem] * 2,
+        out_specs=vmem,
         compiler_params=params,
         cost_estimate=pl.CostEstimate(
             flops=2 * live * functionals * dof * dof,
@@ -494,20 +500,27 @@
             transcendentals=0,
         ),
         name="home_terms",
-    )(elem_faces.T, orient.T, counts, tables, rounded, from_sib, in_vmem(elem_mats))
-    swap, cross, terms = pl.pallas_call(
+    )(rows, in_vmem(elem_mats))
+    relayed = passed_on(from_even, sums)
+    swap, even, terms = pl.pallas_call(
         remote_kernel,
-        out_shape=(
-            tiles(3 * SLOT, jnp.bfloat16),
-            tiles(SLOT, jnp.bfloat16),
-            tiles(live + 1, jnp.float32, 6 * LANES),
-        ),
+        out_shape=(tiles(2 * SLOT, jnp.bfloat16), tiles(2 * SLOT, jnp.bfloat16), all_terms),
         in_specs=[vmem] * 8,
         out_specs=(vmem,) * 3,
+        input_output_aliases={7: 2},
         compiler_params=params,
         name="remote_terms",
-    )(remote, index_in, tables, from_sib, from_even, from_odd, terms, in_vmem(elem_mats))
-    from_sib, from_even, from_odd = exchange(routes, swap, cross)
+    )(
+        remote,
+        index_in,
+        tables,
+        from_even,
+        from_odd,
+        relayed,
+        in_vmem(elem_mats),
+        in_vmem(terms),
+    )
+    from_sib, from_even, from_odd = exchange(routes, swap, even)
     base = pl.pallas_call(
         scatter_kernel,
         out_shape=tiles(face_dev + 1, jnp.float32),
@@ -516,17 +529,18 @@
         compiler_params=params,
         name="home_sum",
     )(sums, tables, terms, rhs)
+    relayed = passed_on(from_even, base)
     return pl.pallas_call(
         last_kernel,
         out_shape=jax.ShapeDtypeStruct(rhs.shape, jnp.float32),
-        in_specs=[vmem] * 7,
+        in_specs=[vmem] * 8,
         out_specs=vmem,
         scratch_shapes=[
             pltpu.VMEM((face_dev + 1, functionals, LANES), jnp.float32),
         ],
         compiler_params=params,
         name="last_update",
-    )(slots, base, from_sib, from_even, from_odd, face_blocks, traces)
+    )(slots, base, from_sib, from_even, from_odd, relayed, face_blocks, traces)
 
 
 def solution(mesh):

time: 17.9 us -> 17.6 us (0.983)
  waiting for transfers between devices: 5.4 us -> 4.3 us
  starting transfers between devices: 5.91 us -> 6.64 us
  Pallas kernels: 6.16 us -> 6.39 us
    ppermute x6 -> x8, waiting for transfers between devices: 5.4 us -> 4.3 us  [the longest x2 2.3 us: exchange(): return (from_sib, from_even, lax.ppermute(odd, 'elem', odd_chips))]
    ppermute x6 -> x8, starting transfers between devices: 5.91 us -> 6.64 us  [the longest x2 3.89 us: exchange(): return (from_sib, from_even, lax.ppermute(odd, 'elem', odd_chips))]
    pallas_call x2 -> x5, Pallas kernels: 2.75 us -> 3.04 us  [the longest x1 1.47 us: per_device(): pl.pallas_call(home_kernel, out_shape=all_terms, in_specs=[vmem] * 2, out...]
  transfers between devices with their start and end apart: 6 -> 8, of which waited for: 6 -> 5; matrix products, arithmetic and copies ran while one was open for 0% -> 0% of each run, Pallas kernels for 15% -> 16%
where the time goes in v5:
time: 17.6 us; the launch traced here: 17.5 us
  starting transfers between devices  6.64 us (38%)
  Pallas kernels  6.39 us (36%)
  waiting for transfers between devices  4.3 us (24%)
    ppermute x2, starting transfers between devices, exchange(): return (from_sib, from_even, lax.ppermute(odd, 'elem', odd_chips))  3.89 us
    ppermute x2, waiting for transfers between devices, exchange(): return (from_sib, from_even, lax.ppermute(odd, 'elem', odd_chips))  2.3 us
    pallas_call x1, Pallas kernels, per_device(): pl.pallas_call(functools.partial(first_kernel, elem_cap, devices), out_sh...  1.8 us
    pallas_call x1, Pallas kernels, per_device(): pl.pallas_call(home_kernel, out_shape=all_terms, in_specs=[vmem] * 2, out...  1.47 us
    ppermute x2, starting transfers between devices, exchange(): from_even = lax.ppermute(even, 'elem', even_chips)  1.22 us
    ppermute x2, starting transfers between devices, exchange(): from_sib = lax.ppermute(swap, 'elem', sibling)  1.2 us
    pallas_call x1, Pallas kernels, per_device(): pl.pallas_call(last_kernel, out_shape=jax.ShapeDtypeStruct(rhs.shape, jnp...  1.11 us
    ppermute x2, waiting for transfers between devices, passed_on(): return lax.ppermute(relay, 'elem', routes[0])  1.04 us
  transfers between devices with their start and end apart: 8, of which 5 were waited for; matrix products, arithmetic and copies ran while one was open for 0% of the time, Pallas kernels for 16%

profile of v5, /device:TPU:25, one launch (start us, length us, event | category | flops | bytes accessed | tf_op | source)
XLA Modules:
  0.0 17.5 jit_solution(6959198725034360302)
XLA Ops:
  0.0 0.0 copy-start.6
  0.0 0.0 copy-start
  0.0 1.8 %first_sweep.1 = (f32[27,16,128]{2,1,0:T(8,128)S(1)}, bf16[27,16,128]{2,1,0:T(8,128)(2,1)S(1)}, bf16[8,16,128]{2,1,0:T(8,128)(2,1)S(1)}, bf16[8,16,128]{2,1,0:T(8,128)(2,1)S(1)}, s32[16,128]{1,0:T(8,128)S(1)}) custom-call(s32[6,384]{1,0:T(8,128)} %bitcast.2, s32[32]{0:T(128)} %counts.1, bf16[27,16,125]{2,1,0:T(8,128)(2,1)} %rhs.1, bf16[27,125,125]{2,1,0:T(8,128)(2,1)} %blocks.1), custom_call_target="tpu_custom_call" | custom-call | flops 99999997952 | bytes 100000000 | tf_op jit(solution)/shard_map/first_sweep/pallas_call | solution.py:440
  1.8 0.7 %collective-permute-start = (bf16[8,16,128]{2,1,0:T(8,128)(2,1)S(1)}, bf16[8,16,128]{2,1,0:T(8,128)(2,1)S(1)}, u32[]{:S(2)}, u32[]{:S(2)}) collective-permute-start(bf16[8,16,128]{2,1,0:T(8,128)(2,1)S(1)} %get-tuple-element.19), channel_id=1, source_target_pairs={{0,1},{1,0},{2,3},{3,2},{4,5},{5,4},{6,7},{7,6},{8,9},{9,8},{10,11... | collective-permute-start | bytes 98312 | tf_op jit(solution)/shard_map/ppermute | solution.py:408
  2.6 1.2 %collective-permute-start.1 = (bf16[8,16,128]{2,1,0:T(8,128)(2,1)S(1)}, bf16[8,16,128]{2,1,0:T(8,128)(2,1)S(1)}, u32[]{:S(2)}, u32[]{:S(2)}) collective-permute-start(bf16[8,16,128]{2,1,0:T(8,128)(2,1)S(1)} %get-tuple-element.23), channel_id=1, source_target_pairs={{0,3},{1,2},{2,1},{3,0},{4,7},{5,6},{6,5},{7,4},{8,11},{9,10},{10,... | collective-permute-start | bytes 98312 | tf_op jit(solution)/shard_map/ppermute | solution.py:407
  3.8 0.0 collective-permute-done.from_sib
  3.8 2.0 %collective-permute-start.2 = (bf16[8,16,128]{2,1,0:T(8,128)(2,1)S(1)}, bf16[8,16,128]{2,1,0:T(8,128)(2,1)S(1)}, u32[]{:S(2)}, u32[]{:S(2)}) collective-permute-start(bf16[8,16,128]{2,1,0:T(8,128)(2,1)S(1)} %pad_maximum_fusion), channel_id=1, source_target_pairs={{0,1},{1,0},{2,5},{3,4},{4,3},{5,2},{6,9},{7,8},{8,7},{9,6},{10,13... | collective-permute-start | bytes 98312 | tf_op jit(solution)/shard_map/ppermute | solution.py:410
  5.8 0.9 %home_rows.1 = (bf16[9,16,768]{2,1,0:T(8,128)(2,1)S(1)}, s32[6,128]{1,0:T(8,128)S(1)}, s32[16,128]{1,0:T(8,128)S(1)}, s32[16,128]{1,0:T(8,128)S(1)}) custom-call(s32[6,384]{1,0:T(8,128)S(1)} %bitcast.3, s32[6,384]{1,0:T(8,128)S(1)} %bitcast.4, s32[32]{0:T(128)S(1)} %copy-done.6, s32[3,48,128]{2,1,0:T(8,128)S(1)} %copy-done.2, ...), custom_call_target="tpu_custom_call" | custom-call | tf_op jit(solution)/shard_map/home_rows/pallas_call | solution.py:477
  6.7 0.0 collective-permute-done.1.from_even
  6.7 0.2 %collective-permute-start.3 = (bf16[4,16,128]{2,1,0:T(8,128)(2,1)S(1)}, bf16[4,16,128]{2,1,0:T(8,128)(2,1)S(1)}, u32[]{:S(2)}, u32[]{:S(2)}) collective-permute-start(bf16[4,16,128]{2,1,0:T(8,128)(2,1)S(1)} %relay.2), channel_id=1, source_target_pairs={{0,1},{1,0},{2,3},{3,2},{4,5},{5,4},{6,7},{7,6},{8,9},{9,8},{10,11... | collective-permute-start | bytes 49160 | tf_op jit(solution)/shard_map/ppermute | solution.py:473
  6.9 1.5 %home_terms.1._ = f32[10,16,768]{2,1,0:T(8,128)S(1)} custom-call(bf16[9,16,768]{2,1,0:T(8,128)(2,1)S(1)} %get-tuple-element.24.rows, bf16[12,750,750]{2,1,0:T(8,128)(2,1)S(1)} %copy-done), custom_call_target="tpu_custom_call" | custom-call | flops 162000000 | bytes 10125000 | tf_op jit(solution)/shard_map/home_terms/pallas_call | solution.py:491
  8.4 0.0 collective-permute-done.3.relayed
  8.4 0.7 %collective-permute-done.2.from_odd = bf16[8,16,128]{2,1,0:T(8,128)(2,1)S(1)} collective-permute-done((bf16[8,16,128]{2,1,0:T(8,128)(2,1)S(1)}, bf16[8,16,128]{2,1,0:T(8,128)(2,1)S(1)}, u32[]{:S(2)}, u32[]{:S(2)}) %collective-permute-start.2) | collective-permute-done | bytes 32800 | tf_op jit(solution)/shard_map/ppermute | solution.py:410
  9.1 0.7 %remote_terms.1 = (bf16[8,16,128]{2,1,0:T(8,128)(2,1)S(1)}, bf16[8,16,128]{2,1,0:T(8,128)(2,1)S(1)}, f32[10,16,768]{2,1,0:T(8,128)S(1)}) custom-call(s32[16,128]{1,0:T(8,128)S(1)} %get-tuple-element.21.remote, s32[16,128]{1,0:T(8,128)S(1)} %get-tuple-element.22.index_in, s32[3,48,128]{2,1,0:T(8,128)S(1)} %copy-done.2, ...), custom_call_target="tpu_custom_call", output_to_operand_aliasing={{2}: (7, {})} | custom-call | tf_op jit(solution)/shard_map/remote_terms/pallas_call | solution.py:505
  9.8 0.5 %collective-permute-start.4 = (bf16[8,16,128]{2,1,0:T(8,128)(2,1)S(1)}, bf16[8,16,128]{2,1,0:T(8,128)(2,1)S(1)}, u32[]{:S(2)}, u32[]{:S(2)}) collective-permute-start(bf16[8,16,128]{2,1,0:T(8,128)(2,1)S(1)} %get-tuple-element.26), channel_id=1, source_target_pairs={{0,1},{1,0},{2,3},{3,2},{4,5},{5,4},{6,7},{7,6},{8,9},{9,8},{10,11... | collective-permute-start | bytes 98312 | tf_op jit(solution)/shard_map/ppermute | solution.py:408
  10.3 0.0 collective-permute-start.5
  10.3 0.8 %collective-permute-done.4.from_sib = bf16[8,16,128]{2,1,0:T(8,128)(2,1)S(1)} collective-permute-done((bf16[8,16,128]{2,1,0:T(8,128)(2,1)S(1)}, bf16[8,16,128]{2,1,0:T(8,128)(2,1)S(1)}, u32[]{:S(2)}, u32[]{:S(2)}) %collective-permute-start.4) | collective-permute-done | bytes 32800 | tf_op jit(solution)/shard_map/ppermute | solution.py:408
  11.1 1.9 %collective-permute-start.6 = (bf16[8,16,128]{2,1,0:T(8,128)(2,1)S(1)}, bf16[8,16,128]{2,1,0:T(8,128)(2,1)S(1)}, u32[]{:S(2)}, u32[]{:S(2)}) collective-permute-start(bf16[8,16,128]{2,1,0:T(8,128)(2,1)S(1)} %pad_maximum_fusion.1), channel_id=1, source_target_pairs={{0,1},{1,0},{2,5},{3,4},{4,3},{5,2},{6,9},{7,8},{8,7},{9,6},{10,13... | collective-permute-start | bytes 98312 | tf_op jit(solution)/shard_map/ppermute | solution.py:410
  13.0 0.4 %home_sum.1._.base = f32[28,16,128]{2,1,0:T(8,128)S(1)} custom-call(s32[6,128]{1,0:T(8,128)S(1)} %get-tuple-element.20._.sums, s32[3,48,128]{2,1,0:T(8,128)S(1)} %copy-done.2, f32[10,16,768]{2,1,0:T(8,128)S(1)} %get-tuple-element.25.terms, bf16[27,16,125]{2,1,0:T(8,128)(2,1)S(1)} %copy-done.3), custom_call_target="tpu_custom_call" | custom-call | tf_op jit(solution)/shard_map/home_sum/pallas_call | solution.py:524
  13.5 0.1 collective-permute-done.5.from_even
  13.6 0.1 collective-permute-start.7
  13.8 1.0 %collective-permute-done.7.relayed = bf16[4,16,128]{2,1,0:T(8,128)(2,1)S(1)} collective-permute-done((bf16[4,16,128]{2,1,0:T(8,128)(2,1)S(1)}, bf16[4,16,128]{2,1,0:T(8,128)(2,1)S(1)}, u32[]{:S(2)}, u32[]{:S(2)}) %collective-permute-start.7) | collective-permute-done | bytes 16416 | tf_op jit(solution)/shard_map/ppermute | solution.py:473
  14.8 1.6 %collective-permute-done.6.from_odd = bf16[8,16,128]{2,1,0:T(8,128)(2,1)S(1)} collective-permute-done((bf16[8,16,128]{2,1,0:T(8,128)(2,1)S(1)}, bf16[8,16,128]{2,1,0:T(8,128)(2,1)S(1)}, u32[]{:S(2)}, u32[]{:S(2)}) %collective-permute-start.6) | collective-permute-done | bytes 32800 | tf_op jit(solution)/shard_map/ppermute | solution.py:410
  16.4 1.1 %last_update.1 = f32[27,16,125]{2,1,0:T(8,128)} custom-call(s32[16,128]{1,0:T(8,128)S(1)} %get-tuple-element.17.slots, f32[28,16,128]{2,1,0:T(8,128)S(1)} %home_sum.1._.base, bf16[8,16,128]{2,1,0:T(8,128)(2,1)S(1)} %collective-permute-done.4.from_sib, bf16[8,16,128]{2,1,0:T(8,128)(2,1)S(1)} %collective-permute-done.5.from_even, ...), custom_call_target="tpu_custom_call" | custom-call | tf_op jit(solution)/shard_map/last_update/pallas_call | solution.py:533
  (20 shorter events, 0.1 us)
Async XLA Ops:
  0.0 5.8 %copy-start.2 = (s32[3,48,128]{2,1,0:T(8,128)S(1)}, s32[3,48,128]{2,1,0:T(8,128)}, u32[]{:S(2)}) copy-start(s32[3,48,128]{2,1,0:T(8,128)} %constant.2.clone.tables) | copy-start | bytes 221188
  0.0 5.8 %copy-start.4 = (s32[384,6]{0,1:T(8,128)S(1)}, s32[384,6]{0,1:T(8,128)}, u32[]{:S(2)}) copy-start(s32[384,6]{0,1:T(8,128)} %param.10) | copy-start | bytes 27652
  0.0 5.8 %copy-start.5 = (s32[384,6]{0,1:T(8,128)S(1)}, s32[384,6]{0,1:T(8,128)}, u32[]{:S(2)}) copy-start(s32[384,6]{0,1:T(8,128)} %param.11) | copy-start | bytes 27652
  0.0 5.8 %copy-start.6 = (s32[32]{0:T(128)S(1)}, s32[32]{0:T(128)}, u32[]{:S(2)}) copy-start(s32[32]{0:T(128)} %counts.1) | copy-start | bytes 388
  0.0 6.9 %copy-start = (bf16[12,750,750]{2,1,0:T(8,128)(2,1)S(1)}, bf16[12,750,750]{2,1,0:T(8,128)(2,1)}, u32[]{:S(2)}) copy-start(bf16[12,750,750]{2,1,0:T(8,128)(2,1)} %mats.3) | copy-start | bytes 40500004
  1.8 1.9 %collective-permute-start = (bf16[8,16,128]{2,1,0:T(8,128)(2,1)S(1)}, bf16[8,16,128]{2,1,0:T(8,128)(2,1)S(1)}, u32[]{:S(2)}, u32[]{:S(2)}) collective-permute-start(bf16[8,16,128]{2,1,0:T(8,128)(2,1)S(1)} %get-tuple-element.19), channel_id=1, source_target_pairs={{0,1},{1,0},{2,3},{3,2},{4,5},{5,4},{6,7},{7,6},{8,9},{9,8},{10,11... | collective-permute-start | bytes 98312 | tf_op jit(solution)/shard_map/ppermute | solution.py:408
  2.6 4.1 %collective-permute-start.1 = (bf16[8,16,128]{2,1,0:T(8,128)(2,1)S(1)}, bf16[8,16,128]{2,1,0:T(8,128)(2,1)S(1)}, u32[]{:S(2)}, u32[]{:S(2)}) collective-permute-start(bf16[8,16,128]{2,1,0:T(8,128)(2,1)S(1)} %get-tuple-element.23), channel_id=1, source_target_pairs={{0,3},{1,2},{2,1},{3,0},{4,7},{5,6},{6,5},{7,4},{8,11},{9,10},{10,... | collective-permute-start | bytes 98312 | tf_op jit(solution)/shard_map/ppermute | solution.py:407
  3.8 5.4 %collective-permute-start.2 = (bf16[8,16,128]{2,1,0:T(8,128)(2,1)S(1)}, bf16[8,16,128]{2,1,0:T(8,128)(2,1)S(1)}, u32[]{:S(2)}, u32[]{:S(2)}) collective-permute-start(bf16[8,16,128]{2,1,0:T(8,128)(2,1)S(1)} %pad_maximum_fusion), channel_id=1, source_target_pairs={{0,1},{1,0},{2,5},{3,4},{4,3},{5,2},{6,9},{7,8},{8,7},{9,6},{10,13... | collective-permute-start | bytes 98312 | tf_op jit(solution)/shard_map/ppermute | solution.py:410
  6.7 1.7 %collective-permute-start.3 = (bf16[4,16,128]{2,1,0:T(8,128)(2,1)S(1)}, bf16[4,16,128]{2,1,0:T(8,128)(2,1)S(1)}, u32[]{:S(2)}, u32[]{:S(2)}) collective-permute-start(bf16[4,16,128]{2,1,0:T(8,128)(2,1)S(1)} %relay.2), channel_id=1, source_target_pairs={{0,1},{1,0},{2,3},{3,2},{4,5},{5,4},{6,7},{7,6},{8,9},{9,8},{10,11... | collective-permute-start | bytes 49160 | tf_op jit(solution)/shard_map/ppermute | solution.py:473
  6.9 6.1 %copy-start.3 = (bf16[27,16,125]{2,1,0:T(8,128)(2,1)S(1)}, bf16[27,16,125]{2,1,0:T(8,128)(2,1)}, u32[]{:S(2)}) copy-start(bf16[27,16,125]{2,1,0:T(8,128)(2,1)} %rhs.1) | copy-start | bytes 324004
  6.9 9.4 %copy-start.1 = (bf16[27,125,125]{2,1,0:T(8,128)(2,1)S(1)}, bf16[27,125,125]{2,1,0:T(8,128)(2,1)}, u32[]{:S(2)}) copy-start(bf16[27,125,125]{2,1,0:T(8,128)(2,1)} %blocks.1) | copy-start | bytes 2531254
  9.8 1.3 %collective-permute-start.4 = (bf16[8,16,128]{2,1,0:T(8,128)(2,1)S(1)}, bf16[8,16,128]{2,1,0:T(8,128)(2,1)S(1)}, u32[]{:S(2)}, u32[]{:S(2)}) collective-permute-start(bf16[8,16,128]{2,1,0:T(8,128)(2,1)S(1)} %get-tuple-element.26), channel_id=1, source_target_pairs={{0,1},{1,0},{2,3},{3,2},{4,5},{5,4},{6,7},{7,6},{8,9},{9,8},{10,11... | collective-permute-start | bytes 98312 | tf_op jit(solution)/shard_map/ppermute | solution.py:408
  10.3 3.3 %collective-permute-start.5 = (bf16[8,16,128]{2,1,0:T(8,128)(2,1)S(1)}, bf16[8,16,128]{2,1,0:T(8,128)(2,1)S(1)}, u32[]{:S(2)}, u32[]{:S(2)}) collective-permute-start(bf16[8,16,128]{2,1,0:T(8,128)(2,1)S(1)} %get-tuple-element.27), channel_id=1, source_target_pairs={{0,3},{1,2},{2,1},{3,0},{4,7},{5,6},{6,5},{7,4},{8,11},{9,10},{10,... | collective-permute-start | bytes 98312 | tf_op jit(solution)/shard_map/ppermute | solution.py:407
  11.1 5.2 %collective-permute-start.6 = (bf16[8,16,128]{2,1,0:T(8,128)(2,1)S(1)}, bf16[8,16,128]{2,1,0:T(8,128)(2,1)S(1)}, u32[]{:S(2)}, u32[]{:S(2)}) collective-permute-start(bf16[8,16,128]{2,1,0:T(8,128)(2,1)S(1)} %pad_maximum_fusion.1), channel_id=1, source_target_pairs={{0,1},{1,0},{2,5},{3,4},{4,3},{5,2},{6,9},{7,8},{8,7},{9,6},{10,13... | collective-permute-start | bytes 98312 | tf_op jit(solution)/shard_map/ppermute | solution.py:410
  13.6 1.2 %collective-permute-start.7 = (bf16[4,16,128]{2,1,0:T(8,128)(2,1)S(1)}, bf16[4,16,128]{2,1,0:T(8,128)(2,1)S(1)}, u32[]{:S(2)}, u32[]{:S(2)}) collective-permute-start(bf16[4,16,128]{2,1,0:T(8,128)(2,1)S(1)} %relay.3), channel_id=1, source_target_pairs={{0,1},{1,0},{2,3},{3,2},{4,5},{5,4},{6,7},{7,6},{8,9},{9,8},{10,11... | collective-permute-start | bytes 49160 | tf_op jit(solution)/shard_map/ppermute | solution.py:473

commit v6 on v5

--- a/solution.py
+++ b/solution.py
@@ -340,16 +340,19 @@
     out[...] = from_even[SLOT:]
 
 
+def even_kernel(remote, index_in, relayed, mats, _, terms):
+    add_remote(EVEN, relayed, 0, remote[...], index_in, mats, terms)
+
+
 def remote_kernel(
-    remote, index_in, tables, from_even, from_odd, relayed, mats, _, swap, even, terms
+    remote, index_in, tables, from_even, from_odd, mats, _, swap, even, terms
 ):
     trace_len = mats.shape[1] // 6
     gap = LANES - trace_len
     packs = remote[...]
-    add_remote(EVEN, relayed, 0, packs, index_in, mats, terms)
     add_remote(CROSS, crossing_bucket(from_even, from_odd), 0, packs, index_in, mats, terms)
     add_remote(ODD, from_odd, SLOT, packs, index_in, mats, terms)
-    lane = lax.broadcasted_iota(jnp.int32, relayed.shape[1:], 1)
+    lane = lax.broadcasted_iota(jnp.int32, from_odd.shape[1:], 1)
     for group in range(4):
         for r in range(SLOT):
             e, k, pick = unpacked(packs, group * SLOT + r)
@@ -502,12 +505,21 @@
         name="home_terms",
     )(rows, in_vmem(elem_mats))
     relayed = passed_on(from_even, sums)
+    terms = pl.pallas_call(
+        even_kernel,
+        out_shape=all_terms,
+        in_specs=[vmem] * 5,
+        out_specs=vmem,
+        input_output_aliases={4: 0},
+        compiler_params=params,
+        name="even_terms",
+    )(remote, index_in, relayed, in_vmem(elem_mats), in_vmem(terms))
     swap, even, terms = pl.pallas_call(
         remote_kernel,
         out_shape=(tiles(2 * SLOT, jnp.bfloat16), tiles(2 * SLOT, jnp.bfloat16), all_terms),
-        in_specs=[vmem] * 8,
+        in_specs=[vmem] * 7,
         out_specs=(vmem,) * 3,
-        input_output_aliases={7: 2},
+        input_output_aliases={6: 2},
         compiler_params=params,
         name="remote_terms",
     )(
@@ -516,7 +528,6 @@
         tables,
         from_even,
         from_odd,
-        relayed,
         in_vmem(elem_mats),
         in_vmem(terms),
     )

time: 17.6 us -> 17.5 us (level)
  waiting for transfers between devices: 4.3 us -> 3.64 us
  starting transfers between devices: 6.64 us -> 6.93 us
  Pallas kernels: 6.39 us -> 6.63 us
    ppermute x2, waiting for transfers between devices: 2.3 us -> 2 us  [exchange(): return (from_sib, from_even, lax.ppermute(odd, 'elem', odd_chips))]
    ppermute x2, waiting for transfers between devices: 0.82 us -> 0.53 us  [exchange(): from_sib = lax.ppermute(swap, 'elem', sibling)]
    ppermute x2, starting transfers between devices: 1.22 us -> 1.51 us  [exchange(): from_even = lax.ppermute(even, 'elem', even_chips)]
    pallas_call x0 -> x1, Pallas kernels: none -> 0.28 us  [per_device(): pl.pallas_call(even_kernel, out_shape=all_terms, in_specs=[vmem] * 5, out...]
  transfers between devices with their start and end apart: 8 -> 8, of which waited for: 5 -> 5; matrix products, arithmetic and copies ran while one was open for 0% -> 0% of each run, Pallas kernels for 16% -> 18%
where the time goes in v6:
time: 17.5 us; the launch traced here: 17.3 us
  starting transfers between devices  6.93 us (40%)
  Pallas kernels  6.63 us (38%)
  waiting for transfers between devices  3.64 us (21%)
    ppermute x2, starting transfers between devices, exchange(): return (from_sib, from_even, lax.ppermute(odd, 'elem', odd_chips))  3.9 us
    ppermute x2, waiting for transfers between devices, exchange(): return (from_sib, from_even, lax.ppermute(odd, 'elem', odd_chips))  2 us
    pallas_call x1, Pallas kernels, per_device(): pl.pallas_call(functools.partial(first_kernel, elem_cap, devices), out_sh...  1.8 us
    ppermute x2, starting transfers between devices, exchange(): from_even = lax.ppermute(even, 'elem', even_chips)  1.51 us
    pallas_call x1, Pallas kernels, per_device(): pl.pallas_call(home_kernel, out_shape=all_terms, in_specs=[vmem] * 2, out...  1.47 us
    ppermute x2, starting transfers between devices, exchange(): from_sib = lax.ppermute(swap, 'elem', sibling)  1.2 us
    pallas_call x1, Pallas kernels, per_device(): pl.pallas_call(last_kernel, out_shape=jax.ShapeDtypeStruct(rhs.shape, jnp...  1.11 us
    ppermute x2, waiting for transfers between devices, passed_on(): return lax.ppermute(relay, 'elem', routes[0])  1.04 us
  transfers between devices with their start and end apart: 8, of which 5 were waited for; matrix products, arithmetic and copies ran while one was open for 0% of the time, Pallas kernels for 18%

profile of v6, /device:TPU:25, one launch (start us, length us, event | category | flops | bytes accessed | tf_op | source)
XLA Modules:
  0.0 17.3 jit_solution(14039132108049118615)
XLA Ops:
  0.0 1.8 %first_sweep.1 = (f32[27,16,128]{2,1,0:T(8,128)S(1)}, bf16[27,16,128]{2,1,0:T(8,128)(2,1)S(1)}, bf16[8,16,128]{2,1,0:T(8,128)(2,1)S(1)}, bf16[8,16,128]{2,1,0:T(8,128)(2,1)S(1)}, s32[16,128]{1,0:T(8,128)S(1)}) custom-call(s32[6,384]{1,0:T(8,128)} %bitcast.2, s32[32]{0:T(128)} %counts.1, bf16[27,16,125]{2,1,0:T(8,128)(2,1)} %rhs.1, bf16[27,125,125]{2,1,0:T(8,128)(2,1)} %blocks.1), custom_call_target="tpu_custom_call" | custom-call | flops 99999997952 | bytes 100000000 | tf_op jit(solution)/shard_map/first_sweep/pallas_call | solution.py:443
  1.8 0.7 %collective-permute-start = (bf16[8,16,128]{2,1,0:T(8,128)(2,1)S(1)}, bf16[8,16,128]{2,1,0:T(8,128)(2,1)S(1)}, u32[]{:S(2)}, u32[]{:S(2)}) collective-permute-start(bf16[8,16,128]{2,1,0:T(8,128)(2,1)S(1)} %get-tuple-element.19), channel_id=1, source_target_pairs={{0,1},{1,0},{2,3},{3,2},{4,5},{5,4},{6,7},{7,6},{8,9},{9,8},{10,11... | collective-permute-start | bytes 98312 | tf_op jit(solution)/shard_map/ppermute | solution.py:411
  2.6 1.2 %collective-permute-start.1 = (bf16[8,16,128]{2,1,0:T(8,128)(2,1)S(1)}, bf16[8,16,128]{2,1,0:T(8,128)(2,1)S(1)}, u32[]{:S(2)}, u32[]{:S(2)}) collective-permute-start(bf16[8,16,128]{2,1,0:T(8,128)(2,1)S(1)} %get-tuple-element.23), channel_id=1, source_target_pairs={{0,3},{1,2},{2,1},{3,0},{4,7},{5,6},{6,5},{7,4},{8,11},{9,10},{10,... | collective-permute-start | bytes 98312 | tf_op jit(solution)/shard_map/ppermute | solution.py:410
  3.8 0.0 collective-permute-done.from_sib
  3.8 2.0 %collective-permute-start.2 = (bf16[8,16,128]{2,1,0:T(8,128)(2,1)S(1)}, bf16[8,16,128]{2,1,0:T(8,128)(2,1)S(1)}, u32[]{:S(2)}, u32[]{:S(2)}) collective-permute-start(bf16[8,16,128]{2,1,0:T(8,128)(2,1)S(1)} %pad_maximum_fusion), channel_id=1, source_target_pairs={{0,1},{1,0},{2,5},{3,4},{4,3},{5,2},{6,9},{7,8},{8,7},{9,6},{10,13... | collective-permute-start | bytes 98312 | tf_op jit(solution)/shard_map/ppermute | solution.py:413
  5.8 0.9 %home_rows.1 = (bf16[9,16,768]{2,1,0:T(8,128)(2,1)S(1)}, s32[6,128]{1,0:T(8,128)S(1)}, s32[16,128]{1,0:T(8,128)S(1)}, s32[16,128]{1,0:T(8,128)S(1)}) custom-call(s32[6,384]{1,0:T(8,128)S(1)} %bitcast.3, s32[6,384]{1,0:T(8,128)S(1)} %bitcast.4, s32[32]{0:T(128)S(1)} %copy-done.6, s32[3,48,128]{2,1,0:T(8,128)S(1)} %copy-done.2, ...), custom_call_target="tpu_custom_call" | custom-call | tf_op jit(solution)/shard_map/home_rows/pallas_call | solution.py:480
  6.7 0.0 collective-permute-done.1.from_even
  6.7 0.2 %collective-permute-start.3 = (bf16[4,16,128]{2,1,0:T(8,128)(2,1)S(1)}, bf16[4,16,128]{2,1,0:T(8,128)(2,1)S(1)}, u32[]{:S(2)}, u32[]{:S(2)}) collective-permute-start(bf16[4,16,128]{2,1,0:T(8,128)(2,1)S(1)} %relay.2), channel_id=1, source_target_pairs={{0,1},{1,0},{2,3},{3,2},{4,5},{5,4},{6,7},{7,6},{8,9},{9,8},{10,11... | collective-permute-start | bytes 49160 | tf_op jit(solution)/shard_map/ppermute | solution.py:476
  6.9 1.5 %home_terms.1._ = f32[10,16,768]{2,1,0:T(8,128)S(1)} custom-call(bf16[9,16,768]{2,1,0:T(8,128)(2,1)S(1)} %get-tuple-element.24.rows, bf16[12,750,750]{2,1,0:T(8,128)(2,1)S(1)} %copy-done), custom_call_target="tpu_custom_call" | custom-call | flops 162000000 | bytes 10125000 | tf_op jit(solution)/shard_map/home_terms/pallas_call | solution.py:494
  8.4 0.0 collective-permute-done.3.relayed
  8.4 0.0 copy-start.1
  8.4 0.3 %even_terms.1._ = f32[10,16,768]{2,1,0:T(8,128)S(1)} custom-call(s32[16,128]{1,0:T(8,128)S(1)} %get-tuple-element.21.remote, s32[16,128]{1,0:T(8,128)S(1)} %get-tuple-element.22.index_in, bf16[4,16,128]{2,1,0:T(8,128)(2,1)S(1)} %collective-permute-done.3.relayed, bf16[12,750,750]{2,1,0:T(8,128)(2,1)S(1)} %copy-done, ...), custom_call_target="tpu_custom_call", output_to_operand_aliasing={{}: (4, {})} | custom-call | tf_op jit(solution)/shard_map/even_terms/pallas_call | solution.py:508
  8.7 0.4 %collective-permute-done.2.from_odd = bf16[8,16,128]{2,1,0:T(8,128)(2,1)S(1)} collective-permute-done((bf16[8,16,128]{2,1,0:T(8,128)(2,1)S(1)}, bf16[8,16,128]{2,1,0:T(8,128)(2,1)S(1)}, u32[]{:S(2)}, u32[]{:S(2)}) %collective-permute-start.2) | collective-permute-done | bytes 32800 | tf_op jit(solution)/shard_map/ppermute | solution.py:413
  9.1 0.5 %remote_terms.1 = (bf16[8,16,128]{2,1,0:T(8,128)(2,1)S(1)}, bf16[8,16,128]{2,1,0:T(8,128)(2,1)S(1)}, f32[10,16,768]{2,1,0:T(8,128)S(1)}) custom-call(s32[16,128]{1,0:T(8,128)S(1)} %get-tuple-element.21.remote, s32[16,128]{1,0:T(8,128)S(1)} %get-tuple-element.22.index_in, s32[3,48,128]{2,1,0:T(8,128)S(1)} %copy-done.2, ...), custom_call_target="tpu_custom_call", output_to_operand_aliasing={{2}: (6, {})} | custom-call | tf_op jit(solution)/shard_map/remote_terms/pallas_call | solution.py:517
  9.7 0.5 %collective-permute-start.4 = (bf16[8,16,128]{2,1,0:T(8,128)(2,1)S(1)}, bf16[8,16,128]{2,1,0:T(8,128)(2,1)S(1)}, u32[]{:S(2)}, u32[]{:S(2)}) collective-permute-start(bf16[8,16,128]{2,1,0:T(8,128)(2,1)S(1)} %get-tuple-element.26), channel_id=1, source_target_pairs={{0,1},{1,0},{2,3},{3,2},{4,5},{5,4},{6,7},{7,6},{8,9},{9,8},{10,11... | collective-permute-start | bytes 98312 | tf_op jit(solution)/shard_map/ppermute | solution.py:411
  10.1 0.3 %collective-permute-start.5 = (bf16[8,16,128]{2,1,0:T(8,128)(2,1)S(1)}, bf16[8,16,128]{2,1,0:T(8,128)(2,1)S(1)}, u32[]{:S(2)}, u32[]{:S(2)}) collective-permute-start(bf16[8,16,128]{2,1,0:T(8,128)(2,1)S(1)} %get-tuple-element.27), channel_id=1, source_target_pairs={{0,3},{1,2},{2,1},{3,0},{4,7},{5,6},{6,5},{7,4},{8,11},{9,10},{10,... | collective-permute-start | bytes 98312 | tf_op jit(solution)/shard_map/ppermute | solution.py:410
  10.5 0.5 %collective-permute-done.4.from_sib = bf16[8,16,128]{2,1,0:T(8,128)(2,1)S(1)} collective-permute-done((bf16[8,16,128]{2,1,0:T(8,128)(2,1)S(1)}, bf16[8,16,128]{2,1,0:T(8,128)(2,1)S(1)}, u32[]{:S(2)}, u32[]{:S(2)}) %collective-permute-start.4) | collective-permute-done | bytes 32800 | tf_op jit(solution)/shard_map/ppermute | solution.py:411
  11.0 1.9 %collective-permute-start.6 = (bf16[8,16,128]{2,1,0:T(8,128)(2,1)S(1)}, bf16[8,16,128]{2,1,0:T(8,128)(2,1)S(1)}, u32[]{:S(2)}, u32[]{:S(2)}) collective-permute-start(bf16[8,16,128]{2,1,0:T(8,128)(2,1)S(1)} %pad_maximum_fusion.1), channel_id=1, source_target_pairs={{0,1},{1,0},{2,5},{3,4},{4,3},{5,2},{6,9},{7,8},{8,7},{9,6},{10,13... | collective-permute-start | bytes 98312 | tf_op jit(solution)/shard_map/ppermute | solution.py:413
  12.9 0.5 %home_sum.1._.base = f32[28,16,128]{2,1,0:T(8,128)S(1)} custom-call(s32[6,128]{1,0:T(8,128)S(1)} %get-tuple-element.20._.sums, s32[3,48,128]{2,1,0:T(8,128)S(1)} %copy-done.2, f32[10,16,768]{2,1,0:T(8,128)S(1)} %get-tuple-element.25.terms, bf16[27,16,125]{2,1,0:T(8,128)(2,1)S(1)} %copy-done.3), custom_call_target="tpu_custom_call" | custom-call | tf_op jit(solution)/shard_map/home_sum/pallas_call | solution.py:535
  13.4 0.1 collective-permute-done.5.from_even
  13.5 0.1 collective-permute-start.7
  13.6 1.0 %collective-permute-done.7.relayed = bf16[4,16,128]{2,1,0:T(8,128)(2,1)S(1)} collective-permute-done((bf16[4,16,128]{2,1,0:T(8,128)(2,1)S(1)}, bf16[4,16,128]{2,1,0:T(8,128)(2,1)S(1)}, u32[]{:S(2)}, u32[]{:S(2)}) %collective-permute-start.7) | collective-permute-done | bytes 16416 | tf_op jit(solution)/shard_map/ppermute | solution.py:476
  14.7 1.6 %collective-permute-done.6.from_odd = bf16[8,16,128]{2,1,0:T(8,128)(2,1)S(1)} collective-permute-done((bf16[8,16,128]{2,1,0:T(8,128)(2,1)S(1)}, bf16[8,16,128]{2,1,0:T(8,128)(2,1)S(1)}, u32[]{:S(2)}, u32[]{:S(2)}) %collective-permute-start.6) | collective-permute-done | bytes 32800 | tf_op jit(solution)/shard_map/ppermute | solution.py:413
  16.2 1.1 %last_update.1 = f32[27,16,125]{2,1,0:T(8,128)} custom-call(s32[16,128]{1,0:T(8,128)S(1)} %get-tuple-element.17.slots, f32[28,16,128]{2,1,0:T(8,128)S(1)} %home_sum.1._.base, bf16[8,16,128]{2,1,0:T(8,128)(2,1)S(1)} %collective-permute-done.4.from_sib, bf16[8,16,128]{2,1,0:T(8,128)(2,1)S(1)} %collective-permute-done.5.from_even, ...), custom_call_target="tpu_custom_call" | custom-call | tf_op jit(solution)/shard_map/last_update/pallas_call | solution.py:544
  (21 shorter events, 0.1 us)
Async XLA Ops:
  0.0 5.8 %copy-start.2 = (s32[3,48,128]{2,1,0:T(8,128)S(1)}, s32[3,48,128]{2,1,0:T(8,128)}, u32[]{:S(2)}) copy-start(s32[3,48,128]{2,1,0:T(8,128)} %constant.2.clone.tables) | copy-start | bytes 221188
  0.0 5.8 %copy-start.4 = (s32[384,6]{0,1:T(8,128)S(1)}, s32[384,6]{0,1:T(8,128)}, u32[]{:S(2)}) copy-start(s32[384,6]{0,1:T(8,128)} %param.10) | copy-start | bytes 27652
  0.0 5.8 %copy-start.5 = (s32[384,6]{0,1:T(8,128)S(1)}, s32[384,6]{0,1:T(8,128)}, u32[]{:S(2)}) copy-start(s32[384,6]{0,1:T(8,128)} %param.11) | copy-start | bytes 27652
  0.0 5.8 %copy-start.6 = (s32[32]{0:T(128)S(1)}, s32[32]{0:T(128)}, u32[]{:S(2)}) copy-start(s32[32]{0:T(128)} %counts.1) | copy-start | bytes 388
  0.0 6.9 %copy-start = (bf16[12,750,750]{2,1,0:T(8,128)(2,1)S(1)}, bf16[12,750,750]{2,1,0:T(8,128)(2,1)}, u32[]{:S(2)}) copy-start(bf16[12,750,750]{2,1,0:T(8,128)(2,1)} %mats.5) | copy-start | bytes 40500004
  1.8 1.9 %collective-permute-start = (bf16[8,16,128]{2,1,0:T(8,128)(2,1)S(1)}, bf16[8,16,128]{2,1,0:T(8,128)(2,1)S(1)}, u32[]{:S(2)}, u32[]{:S(2)}) collective-permute-start(bf16[8,16,128]{2,1,0:T(8,128)(2,1)S(1)} %get-tuple-element.19), channel_id=1, source_target_pairs={{0,1},{1,0},{2,3},{3,2},{4,5},{5,4},{6,7},{7,6},{8,9},{9,8},{10,11... | collective-permute-start | bytes 98312 | tf_op jit(solution)/shard_map/ppermute | solution.py:411
  2.6 4.1 %collective-permute-start.1 = (bf16[8,16,128]{2,1,0:T(8,128)(2,1)S(1)}, bf16[8,16,128]{2,1,0:T(8,128)(2,1)S(1)}, u32[]{:S(2)}, u32[]{:S(2)}) collective-permute-start(bf16[8,16,128]{2,1,0:T(8,128)(2,1)S(1)} %get-tuple-element.23), channel_id=1, source_target_pairs={{0,3},{1,2},{2,1},{3,0},{4,7},{5,6},{6,5},{7,4},{8,11},{9,10},{10,... | collective-permute-start | bytes 98312 | tf_op jit(solution)/shard_map/ppermute | solution.py:410
  3.8 5.4 %collective-permute-start.2 = (bf16[8,16,128]{2,1,0:T(8,128)(2,1)S(1)}, bf16[8,16,128]{2,1,0:T(8,128)(2,1)S(1)}, u32[]{:S(2)}, u32[]{:S(2)}) collective-permute-start(bf16[8,16,128]{2,1,0:T(8,128)(2,1)S(1)} %pad_maximum_fusion), channel_id=1, source_target_pairs={{0,1},{1,0},{2,5},{3,4},{4,3},{5,2},{6,9},{7,8},{8,7},{9,6},{10,13... | collective-permute-start | bytes 98312 | tf_op jit(solution)/shard_map/ppermute | solution.py:413
  6.7 1.7 %collective-permute-start.3 = (bf16[4,16,128]{2,1,0:T(8,128)(2,1)S(1)}, bf16[4,16,128]{2,1,0:T(8,128)(2,1)S(1)}, u32[]{:S(2)}, u32[]{:S(2)}) collective-permute-start(bf16[4,16,128]{2,1,0:T(8,128)(2,1)S(1)} %relay.2), channel_id=1, source_target_pairs={{0,1},{1,0},{2,3},{3,2},{4,5},{5,4},{6,7},{7,6},{8,9},{9,8},{10,11... | collective-permute-start | bytes 49160 | tf_op jit(solution)/shard_map/ppermute | solution.py:476
  8.4 4.5 %copy-start.3 = (bf16[27,16,125]{2,1,0:T(8,128)(2,1)S(1)}, bf16[27,16,125]{2,1,0:T(8,128)(2,1)}, u32[]{:S(2)}) copy-start(bf16[27,16,125]{2,1,0:T(8,128)(2,1)} %rhs.1) | copy-start | bytes 324004
  8.4 7.8 %copy-start.1 = (bf16[27,125,125]{2,1,0:T(8,128)(2,1)S(1)}, bf16[27,125,125]{2,1,0:T(8,128)(2,1)}, u32[]{:S(2)}) copy-start(bf16[27,125,125]{2,1,0:T(8,128)(2,1)} %blocks.1) | copy-start | bytes 2531254
  9.7 1.3 %collective-permute-start.4 = (bf16[8,16,128]{2,1,0:T(8,128)(2,1)S(1)}, bf16[8,16,128]{2,1,0:T(8,128)(2,1)S(1)}, u32[]{:S(2)}, u32[]{:S(2)}) collective-permute-start(bf16[8,16,128]{2,1,0:T(8,128)(2,1)S(1)} %get-tuple-element.26), channel_id=1, source_target_pairs={{0,1},{1,0},{2,3},{3,2},{4,5},{5,4},{6,7},{7,6},{8,9},{9,8},{10,11... | collective-permute-start | bytes 98312 | tf_op jit(solution)/shard_map/ppermute | solution.py:411
  10.1 3.3 %collective-permute-start.5 = (bf16[8,16,128]{2,1,0:T(8,128)(2,1)S(1)}, bf16[8,16,128]{2,1,0:T(8,128)(2,1)S(1)}, u32[]{:S(2)}, u32[]{:S(2)}) collective-permute-start(bf16[8,16,128]{2,1,0:T(8,128)(2,1)S(1)} %get-tuple-element.27), channel_id=1, source_target_pairs={{0,3},{1,2},{2,1},{3,0},{4,7},{5,6},{6,5},{7,4},{8,11},{9,10},{10,... | collective-permute-start | bytes 98312 | tf_op jit(solution)/shard_map/ppermute | solution.py:410
  11.0 5.2 %collective-permute-start.6 = (bf16[8,16,128]{2,1,0:T(8,128)(2,1)S(1)}, bf16[8,16,128]{2,1,0:T(8,128)(2,1)S(1)}, u32[]{:S(2)}, u32[]{:S(2)}) collective-permute-start(bf16[8,16,128]{2,1,0:T(8,128)(2,1)S(1)} %pad_maximum_fusion.1), channel_id=1, source_target_pairs={{0,1},{1,0},{2,5},{3,4},{4,3},{5,2},{6,9},{7,8},{8,7},{9,6},{10,13... | collective-permute-start | bytes 98312 | tf_op jit(solution)/shard_map/ppermute | solution.py:413
  13.5 1.2 %collective-permute-start.7 = (bf16[4,16,128]{2,1,0:T(8,128)(2,1)S(1)}, bf16[4,16,128]{2,1,0:T(8,128)(2,1)S(1)}, u32[]{:S(2)}, u32[]{:S(2)}) collective-permute-start(bf16[4,16,128]{2,1,0:T(8,128)(2,1)S(1)} %relay.3), channel_id=1, source_target_pairs={{0,1},{1,0},{2,3},{3,2},{4,5},{5,4},{6,7},{7,6},{8,9},{9,8},{10,11... | collective-permute-start | bytes 49160 | tf_op jit(solution)/shard_map/ppermute | solution.py:476

commit v7 on v6

--- a/solution.py
+++ b/solution.py
@@ -384,25 +384,48 @@
             base[place] -= tile.astype(jnp.bfloat16).astype(jnp.float32)
 
 
-def last_kernel(
-    slots, base, from_sib, from_even, from_odd, relayed, blocks, traces, out, residual
-):
-    face_dev, _, trace_len = out.shape
+def updated(residual, block, trace):
+    trace_len = block.shape[0]
+    update = jnp.dot(
+        residual[:, :trace_len].astype(jnp.bfloat16), block, preferred_element_type=jnp.float32
+    )
+    return trace[:, :trace_len] + update
+
+
+def crossing_part(arrived, by_even):
+    me = lax.axis_index("elem")
+    here = (((me ^ (me >> 1)) & 1) == 1) == by_even
+    here = jnp.broadcast_to(here, arrived.shape[1:])
+    return [jnp.where(here, arrived[r].astype(jnp.float32), 0.0) for r in range(SLOT)]
+
+
+def early_kernel(slots, base, from_sib, from_even, relayed, blocks, traces, residual, early):
+    face_dev = early.shape[0]
     residual[...] = base[...]
-    crossing = crossing_bucket(from_even, from_odd)
+    crossing = crossing_part(from_even, True)
     places = slots[...]
     for r in range(SLOT):
-        arrived = {SIB: from_sib[r], EVEN: relayed[r], ODD: from_odd[SLOT + r], CROSS: crossing[r]}
+        arrived = {SIB: from_sib[r], EVEN: relayed[r], CROSS: crossing[r]}
         for group, tile in arrived.items():
             place = places[group * SLOT + r, 0]
             residual[place] -= tile.astype(jnp.float32)
     for f in range(face_dev):
-        update = jnp.dot(
-            residual[f, :, :trace_len].astype(jnp.bfloat16),
-            blocks[f],
-            preferred_element_type=jnp.float32,
-        )
-        out[f] = traces[f, :, :trace_len] + update
+        early[f] = updated(residual[f], blocks[f], traces[f])
+
+
+def last_kernel(slots, before, early, from_odd, blocks, traces, out, residual):
+    face_dev = out.shape[0]
+    residual[...] = before[...]
+    out[...] = early[...]
+    crossing = crossing_part(from_odd, False)
+    codes = slots[...]
+    places = {(g, r): codes[g * SLOT + r, 0] for g in (ODD, CROSS) for r in range(SLOT)}
+    for (group, r), place in places.items():
+        tile = crossing[r] if group == CROSS else from_odd[SLOT + r].astype(jnp.float32)
+        residual[place] -= tile
+    for place in places.values():
+        f = jnp.minimum(place, face_dev - 1)
+        out[f] = updated(residual[f], blocks[f], traces[f])
 
 
 def exchange(routes, swap, even):
@@ -541,17 +564,26 @@
         name="home_sum",
     )(sums, tables, terms, rhs)
     relayed = passed_on(from_even, base)
+    residual, early = pl.pallas_call(
+        early_kernel,
+        out_shape=(
+            tiles(face_dev + 1, jnp.float32),
+            jax.ShapeDtypeStruct(rhs.shape, jnp.float32),
+        ),
+        in_specs=[vmem] * 7,
+        out_specs=(vmem,) * 2,
+        compiler_params=params,
+        name="early_update",
+    )(slots, base, from_sib, from_even, relayed, face_blocks, traces)
     return pl.pallas_call(
         last_kernel,
         out_shape=jax.ShapeDtypeStruct(rhs.shape, jnp.float32),
-        in_specs=[vmem] * 8,
+        in_specs=[vmem] * 6,
         out_specs=vmem,
-        scratch_shapes=[
-            pltpu.VMEM((face_dev + 1, functionals, LANES), jnp.float32),
-        ],
+        scratch_shapes=[pltpu.VMEM((face_dev + 1, functionals, LANES), jnp.float32)],
         compiler_params=params,
         name="last_update",
-    )(slots, base, from_sib, from_even, from_odd, relayed, face_blocks, traces)
+    )(slots, residual, early, from_odd, face_blocks, traces)
 
 
 def solution(mesh):

time: 17.5 us -> 17.3 us (0.989)
  waiting for transfers between devices: 3.64 us -> 3.27 us
  Pallas kernels: 6.63 us -> 6.81 us
    ppermute x2, waiting for transfers between devices: 2 us -> 1.6 us  [exchange(): return (from_sib, from_even, lax.ppermute(odd, 'elem', odd_chips))]
    pallas_call x0 -> x1, Pallas kernels: none -> 0.4 us  [per_device(): pl.pallas_call(early_kernel, out_shape=(tiles(face_dev + 1, jnp.float32),...]
    pallas_call x1, Pallas kernels: 1.11 us -> 0.92 us  [per_device(): pl.pallas_call(last_kernel, out_shape=jax.ShapeDtypeStruct(rhs.shape, jnp...]
  transfers between devices with their start and end apart: 8 -> 8, of which waited for: 5 -> 5; matrix products, arithmetic and copies ran while one was open for 0% -> 0% of each run, Pallas kernels for 18% -> 21%
where the time goes in v7:
time: 17.3 us; the launch traced here: 17.2 us
  starting transfers between devices  6.93 us (40%)
  Pallas kernels  6.81 us (39%)
  waiting for transfers between devices  3.27 us (19%)
    ppermute x2, starting transfers between devices, exchange(): return (from_sib, from_even, lax.ppermute(odd, 'elem', odd_chips))  3.9 us
    pallas_call x1, Pallas kernels, per_device(): pl.pallas_call(functools.partial(first_kernel, elem_cap, devices), out_sh...  1.8 us
    ppermute x2, waiting for transfers between devices, exchange(): return (from_sib, from_even, lax.ppermute(odd, 'elem', odd_chips))  1.6 us
    ppermute x2, starting transfers between devices, exchange(): from_even = lax.ppermute(even, 'elem', even_chips)  1.51 us
    pallas_call x1, Pallas kernels, per_device(): pl.pallas_call(home_kernel, out_shape=all_terms, in_specs=[vmem] * 2, out...  1.47 us
    ppermute x2, starting transfers between devices, exchange(): from_sib = lax.ppermute(swap, 'elem', sibling)  1.2 us
    ppermute x2, waiting for transfers between devices, passed_on(): return lax.ppermute(relay, 'elem', routes[0])  1.04 us
    pallas_call x1, Pallas kernels, per_device(): pl.pallas_call(last_kernel, out_shape=jax.ShapeDtypeStruct(rhs.shape, jnp...  0.92 us
  transfers between devices with their start and end apart: 8, of which 5 were waited for; matrix products, arithmetic and copies ran while one was open for 0% of the time, Pallas kernels for 21%

profile of v7, /device:TPU:25, one launch (start us, length us, event | category | flops | bytes accessed | tf_op | source)
XLA Modules:
  0.0 17.2 jit_solution(15568738449615769822)
XLA Ops:
  0.0 1.8 %first_sweep.1 = (f32[27,16,128]{2,1,0:T(8,128)S(1)}, bf16[27,16,128]{2,1,0:T(8,128)(2,1)S(1)}, bf16[8,16,128]{2,1,0:T(8,128)(2,1)S(1)}, bf16[8,16,128]{2,1,0:T(8,128)(2,1)S(1)}, s32[16,128]{1,0:T(8,128)S(1)}) custom-call(s32[6,384]{1,0:T(8,128)} %bitcast.2, s32[32]{0:T(128)} %counts.1, bf16[27,16,125]{2,1,0:T(8,128)(2,1)} %rhs.1, bf16[27,125,125]{2,1,0:T(8,128)(2,1)} %blocks.3), custom_call_target="tpu_custom_call" | custom-call | flops 99999997952 | bytes 100000000 | tf_op jit(solution)/shard_map/first_sweep/pallas_call | solution.py:466
  1.8 0.7 %collective-permute-start = (bf16[8,16,128]{2,1,0:T(8,128)(2,1)S(1)}, bf16[8,16,128]{2,1,0:T(8,128)(2,1)S(1)}, u32[]{:S(2)}, u32[]{:S(2)}) collective-permute-start(bf16[8,16,128]{2,1,0:T(8,128)(2,1)S(1)} %get-tuple-element.21), channel_id=1, source_target_pairs={{0,1},{1,0},{2,3},{3,2},{4,5},{5,4},{6,7},{7,6},{8,9},{9,8},{10,11... | collective-permute-start | bytes 98312 | tf_op jit(solution)/shard_map/ppermute | solution.py:434
  2.6 1.2 %collective-permute-start.1 = (bf16[8,16,128]{2,1,0:T(8,128)(2,1)S(1)}, bf16[8,16,128]{2,1,0:T(8,128)(2,1)S(1)}, u32[]{:S(2)}, u32[]{:S(2)}) collective-permute-start(bf16[8,16,128]{2,1,0:T(8,128)(2,1)S(1)} %get-tuple-element.25), channel_id=1, source_target_pairs={{0,3},{1,2},{2,1},{3,0},{4,7},{5,6},{6,5},{7,4},{8,11},{9,10},{10,... | collective-permute-start | bytes 98312 | tf_op jit(solution)/shard_map/ppermute | solution.py:433
  3.8 0.0 collective-permute-done.from_sib
  3.8 2.0 %collective-permute-start.2 = (bf16[8,16,128]{2,1,0:T(8,128)(2,1)S(1)}, bf16[8,16,128]{2,1,0:T(8,128)(2,1)S(1)}, u32[]{:S(2)}, u32[]{:S(2)}) collective-permute-start(bf16[8,16,128]{2,1,0:T(8,128)(2,1)S(1)} %pad_maximum_fusion), channel_id=1, source_target_pairs={{0,1},{1,0},{2,5},{3,4},{4,3},{5,2},{6,9},{7,8},{8,7},{9,6},{10,13... | collective-permute-start | bytes 98312 | tf_op jit(solution)/shard_map/ppermute | solution.py:436
  5.8 0.9 %home_rows.1 = (bf16[9,16,768]{2,1,0:T(8,128)(2,1)S(1)}, s32[6,128]{1,0:T(8,128)S(1)}, s32[16,128]{1,0:T(8,128)S(1)}, s32[16,128]{1,0:T(8,128)S(1)}) custom-call(s32[6,384]{1,0:T(8,128)S(1)} %bitcast.3, s32[6,384]{1,0:T(8,128)S(1)} %bitcast.4, s32[32]{0:T(128)S(1)} %copy-done.6, s32[3,48,128]{2,1,0:T(8,128)S(1)} %copy-done.2, ...), custom_call_target="tpu_custom_call" | custom-call | tf_op jit(solution)/shard_map/home_rows/pallas_call | solution.py:503
  6.7 0.0 collective-permute-done.1.from_even
  6.7 0.2 %collective-permute-start.3 = (bf16[4,16,128]{2,1,0:T(8,128)(2,1)S(1)}, bf16[4,16,128]{2,1,0:T(8,128)(2,1)S(1)}, u32[]{:S(2)}, u32[]{:S(2)}) collective-permute-start(bf16[4,16,128]{2,1,0:T(8,128)(2,1)S(1)} %relay.2), channel_id=1, source_target_pairs={{0,1},{1,0},{2,3},{3,2},{4,5},{5,4},{6,7},{7,6},{8,9},{9,8},{10,11... | collective-permute-start | bytes 49160 | tf_op jit(solution)/shard_map/ppermute | solution.py:499
  6.9 1.5 %home_terms.1._ = f32[10,16,768]{2,1,0:T(8,128)S(1)} custom-call(bf16[9,16,768]{2,1,0:T(8,128)(2,1)S(1)} %get-tuple-element.26.rows, bf16[12,750,750]{2,1,0:T(8,128)(2,1)S(1)} %copy-done), custom_call_target="tpu_custom_call" | custom-call | flops 162000000 | bytes 10125000 | tf_op jit(solution)/shard_map/home_terms/pallas_call | solution.py:517
  8.4 0.0 copy-start.1
  8.4 0.3 %even_terms.1._ = f32[10,16,768]{2,1,0:T(8,128)S(1)} custom-call(s32[16,128]{1,0:T(8,128)S(1)} %get-tuple-element.23.remote, s32[16,128]{1,0:T(8,128)S(1)} %get-tuple-element.24.index_in, bf16[4,16,128]{2,1,0:T(8,128)(2,1)S(1)} %collective-permute-done.3.relayed, bf16[12,750,750]{2,1,0:T(8,128)(2,1)S(1)} %copy-done, ...), custom_call_target="tpu_custom_call", output_to_operand_aliasing={{}: (4, {})} | custom-call | tf_op jit(solution)/shard_map/even_terms/pallas_call | solution.py:531
  8.7 0.4 %collective-permute-done.2.from_odd = bf16[8,16,128]{2,1,0:T(8,128)(2,1)S(1)} collective-permute-done((bf16[8,16,128]{2,1,0:T(8,128)(2,1)S(1)}, bf16[8,16,128]{2,1,0:T(8,128)(2,1)S(1)}, u32[]{:S(2)}, u32[]{:S(2)}) %collective-permute-start.2) | collective-permute-done | bytes 32800 | tf_op jit(solution)/shard_map/ppermute | solution.py:436
  9.1 0.5 %remote_terms.1 = (bf16[8,16,128]{2,1,0:T(8,128)(2,1)S(1)}, bf16[8,16,128]{2,1,0:T(8,128)(2,1)S(1)}, f32[10,16,768]{2,1,0:T(8,128)S(1)}) custom-call(s32[16,128]{1,0:T(8,128)S(1)} %get-tuple-element.23.remote, s32[16,128]{1,0:T(8,128)S(1)} %get-tuple-element.24.index_in, s32[3,48,128]{2,1,0:T(8,128)S(1)} %copy-done.2, ...), custom_call_target="tpu_custom_call", output_to_operand_aliasing={{2}: (6, {})} | custom-call | tf_op jit(solution)/shard_map/remote_terms/pallas_call | solution.py:540
  9.7 0.5 %collective-permute-start.4 = (bf16[8,16,128]{2,1,0:T(8,128)(2,1)S(1)}, bf16[8,16,128]{2,1,0:T(8,128)(2,1)S(1)}, u32[]{:S(2)}, u32[]{:S(2)}) collective-permute-start(bf16[8,16,128]{2,1,0:T(8,128)(2,1)S(1)} %get-tuple-element.28), channel_id=1, source_target_pairs={{0,1},{1,0},{2,3},{3,2},{4,5},{5,4},{6,7},{7,6},{8,9},{9,8},{10,11... | collective-permute-start | bytes 98312 | tf_op jit(solution)/shard_map/ppermute | solution.py:434
  10.1 0.3 %collective-permute-start.5 = (bf16[8,16,128]{2,1,0:T(8,128)(2,1)S(1)}, bf16[8,16,128]{2,1,0:T(8,128)(2,1)S(1)}, u32[]{:S(2)}, u32[]{:S(2)}) collective-permute-start(bf16[8,16,128]{2,1,0:T(8,128)(2,1)S(1)} %get-tuple-element.29), channel_id=1, source_target_pairs={{0,3},{1,2},{2,1},{3,0},{4,7},{5,6},{6,5},{7,4},{8,11},{9,10},{10,... | collective-permute-start | bytes 98312 | tf_op jit(solution)/shard_map/ppermute | solution.py:433
  10.5 0.5 %collective-permute-done.4.from_sib = bf16[8,16,128]{2,1,0:T(8,128)(2,1)S(1)} collective-permute-done((bf16[8,16,128]{2,1,0:T(8,128)(2,1)S(1)}, bf16[8,16,128]{2,1,0:T(8,128)(2,1)S(1)}, u32[]{:S(2)}, u32[]{:S(2)}) %collective-permute-start.4) | collective-permute-done | bytes 32800 | tf_op jit(solution)/shard_map/ppermute | solution.py:434
  11.0 1.9 %collective-permute-start.7 = (bf16[8,16,128]{2,1,0:T(8,128)(2,1)S(1)}, bf16[8,16,128]{2,1,0:T(8,128)(2,1)S(1)}, u32[]{:S(2)}, u32[]{:S(2)}) collective-permute-start(bf16[8,16,128]{2,1,0:T(8,128)(2,1)S(1)} %pad_maximum_fusion.1), channel_id=1, source_target_pairs={{0,1},{1,0},{2,5},{3,4},{4,3},{5,2},{6,9},{7,8},{8,7},{9,6},{10,13... | collective-permute-start | bytes 98312 | tf_op jit(solution)/shard_map/ppermute | solution.py:436
  12.9 0.5 %home_sum.1._.base = f32[28,16,128]{2,1,0:T(8,128)S(1)} custom-call(s32[6,128]{1,0:T(8,128)S(1)} %get-tuple-element.22._.sums, s32[3,48,128]{2,1,0:T(8,128)S(1)} %copy-done.2, f32[10,16,768]{2,1,0:T(8,128)S(1)} %get-tuple-element.27.terms, bf16[27,16,125]{2,1,0:T(8,128)(2,1)S(1)} %copy-done.3), custom_call_target="tpu_custom_call" | custom-call | tf_op jit(solution)/shard_map/home_sum/pallas_call | solution.py:558
  13.4 0.1 collective-permute-done.5.from_even
  13.5 0.1 collective-permute-start.6
  13.6 1.0 %collective-permute-done.6.relayed = bf16[4,16,128]{2,1,0:T(8,128)(2,1)S(1)} collective-permute-done((bf16[4,16,128]{2,1,0:T(8,128)(2,1)S(1)}, bf16[4,16,128]{2,1,0:T(8,128)(2,1)S(1)}, u32[]{:S(2)}, u32[]{:S(2)}) %collective-permute-start.6) | collective-permute-done | bytes 16416 | tf_op jit(solution)/shard_map/ppermute | solution.py:499
  14.7 0.4 %early_update.1 = (f32[28,16,128]{2,1,0:T(8,128)S(1)}, f32[27,16,125]{2,1,0:T(8,128)S(1)}) custom-call(s32[16,128]{1,0:T(8,128)S(1)} %get-tuple-element.19.slots, f32[28,16,128]{2,1,0:T(8,128)S(1)} %home_sum.1._.base, bf16[8,16,128]{2,1,0:T(8,128)(2,1)S(1)} %collective-permute-done.4.from_sib, bf16[8,16,128]{2,1,0:T(8,128)(2,1)S(1)} %collective-permute-done.5.from_even, ...), custom_call_target="tpu_custom_call" | custom-call | tf_op jit(solution)/shard_map/early_update/pallas_call | solution.py:567
  15.1 1.2 %collective-permute-done.7.from_odd = bf16[8,16,128]{2,1,0:T(8,128)(2,1)S(1)} collective-permute-done((bf16[8,16,128]{2,1,0:T(8,128)(2,1)S(1)}, bf16[8,16,128]{2,1,0:T(8,128)(2,1)S(1)}, u32[]{:S(2)}, u32[]{:S(2)}) %collective-permute-start.7) | collective-permute-done | bytes 32800 | tf_op jit(solution)/shard_map/ppermute | solution.py:436
  16.2 0.9 %last_update.1 = f32[27,16,125]{2,1,0:T(8,128)} custom-call(s32[16,128]{1,0:T(8,128)S(1)} %get-tuple-element.19.slots, f32[28,16,128]{2,1,0:T(8,128)S(1)} %get-tuple-element.31.before, f32[27,16,125]{2,1,0:T(8,128)S(1)} %get-tuple-element.32.early, bf16[8,16,128]{2,1,0:T(8,128)(2,1)S(1)} %collective-permute-done.7.from_odd, ...), custom_call_target="tpu_custom_call" | custom-call | tf_op jit(solution)/shard_map/last_update/pallas_call | solution.py:578
  (22 shorter events, 0.1 us)
Async XLA Ops:
  0.0 5.8 %copy-start.2 = (s32[3,48,128]{2,1,0:T(8,128)S(1)}, s32[3,48,128]{2,1,0:T(8,128)}, u32[]{:S(2)}) copy-start(s32[3,48,128]{2,1,0:T(8,128)} %constant.2.clone.tables) | copy-start | bytes 221188
  0.0 5.8 %copy-start.4 = (s32[384,6]{0,1:T(8,128)S(1)}, s32[384,6]{0,1:T(8,128)}, u32[]{:S(2)}) copy-start(s32[384,6]{0,1:T(8,128)} %param.10) | copy-start | bytes 27652
  0.0 5.8 %copy-start.5 = (s32[384,6]{0,1:T(8,128)S(1)}, s32[384,6]{0,1:T(8,128)}, u32[]{:S(2)}) copy-start(s32[384,6]{0,1:T(8,128)} %param.11) | copy-start | bytes 27652
  0.0 5.8 %copy-start.6 = (s32[32]{0:T(128)S(1)}, s32[32]{0:T(128)}, u32[]{:S(2)}) copy-start(s32[32]{0:T(128)} %counts.1) | copy-start | bytes 388
  0.0 6.9 %copy-start = (bf16[12,750,750]{2,1,0:T(8,128)(2,1)S(1)}, bf16[12,750,750]{2,1,0:T(8,128)(2,1)}, u32[]{:S(2)}) copy-start(bf16[12,750,750]{2,1,0:T(8,128)(2,1)} %mats.5) | copy-start | bytes 40500004
  1.8 1.9 %collective-permute-start = (bf16[8,16,128]{2,1,0:T(8,128)(2,1)S(1)}, bf16[8,16,128]{2,1,0:T(8,128)(2,1)S(1)}, u32[]{:S(2)}, u32[]{:S(2)}) collective-permute-start(bf16[8,16,128]{2,1,0:T(8,128)(2,1)S(1)} %get-tuple-element.21), channel_id=1, source_target_pairs={{0,1},{1,0},{2,3},{3,2},{4,5},{5,4},{6,7},{7,6},{8,9},{9,8},{10,11... | collective-permute-start | bytes 98312 | tf_op jit(solution)/shard_map/ppermute | solution.py:434
  2.6 4.1 %collective-permute-start.1 = (bf16[8,16,128]{2,1,0:T(8,128)(2,1)S(1)}, bf16[8,16,128]{2,1,0:T(8,128)(2,1)S(1)}, u32[]{:S(2)}, u32[]{:S(2)}) collective-permute-start(bf16[8,16,128]{2,1,0:T(8,128)(2,1)S(1)} %get-tuple-element.25), channel_id=1, source_target_pairs={{0,3},{1,2},{2,1},{3,0},{4,7},{5,6},{6,5},{7,4},{8,11},{9,10},{10,... | collective-permute-start | bytes 98312 | tf_op jit(solution)/shard_map/ppermute | solution.py:433
  3.8 5.4 %collective-permute-start.2 = (bf16[8,16,128]{2,1,0:T(8,128)(2,1)S(1)}, bf16[8,16,128]{2,1,0:T(8,128)(2,1)S(1)}, u32[]{:S(2)}, u32[]{:S(2)}) collective-permute-start(bf16[8,16,128]{2,1,0:T(8,128)(2,1)S(1)} %pad_maximum_fusion), channel_id=1, source_target_pairs={{0,1},{1,0},{2,5},{3,4},{4,3},{5,2},{6,9},{7,8},{8,7},{9,6},{10,13... | collective-permute-start | bytes 98312 | tf_op jit(solution)/shard_map/ppermute | solution.py:436
  6.7 1.7 %collective-permute-start.3 = (bf16[4,16,128]{2,1,0:T(8,128)(2,1)S(1)}, bf16[4,16,128]{2,1,0:T(8,128)(2,1)S(1)}, u32[]{:S(2)}, u32[]{:S(2)}) collective-permute-start(bf16[4,16,128]{2,1,0:T(8,128)(2,1)S(1)} %relay.2), channel_id=1, source_target_pairs={{0,1},{1,0},{2,3},{3,2},{4,5},{5,4},{6,7},{7,6},{8,9},{9,8},{10,11... | collective-permute-start | bytes 49160 | tf_op jit(solution)/shard_map/ppermute | solution.py:499
  8.4 4.5 %copy-start.3 = (bf16[27,16,125]{2,1,0:T(8,128)(2,1)S(1)}, bf16[27,16,125]{2,1,0:T(8,128)(2,1)}, u32[]{:S(2)}) copy-start(bf16[27,16,125]{2,1,0:T(8,128)(2,1)} %rhs.1) | copy-start | bytes 324004
  8.4 6.3 %copy-start.1 = (bf16[27,125,125]{2,1,0:T(8,128)(2,1)S(1)}, bf16[27,125,125]{2,1,0:T(8,128)(2,1)}, u32[]{:S(2)}) copy-start(bf16[27,125,125]{2,1,0:T(8,128)(2,1)} %blocks.3) | copy-start | bytes 2531254
  9.7 1.3 %collective-permute-start.4 = (bf16[8,16,128]{2,1,0:T(8,128)(2,1)S(1)}, bf16[8,16,128]{2,1,0:T(8,128)(2,1)S(1)}, u32[]{:S(2)}, u32[]{:S(2)}) collective-permute-start(bf16[8,16,128]{2,1,0:T(8,128)(2,1)S(1)} %get-tuple-element.28), channel_id=1, source_target_pairs={{0,1},{1,0},{2,3},{3,2},{4,5},{5,4},{6,7},{7,6},{8,9},{9,8},{10,11... | collective-permute-start | bytes 98312 | tf_op jit(solution)/shard_map/ppermute | solution.py:434
  10.1 3.3 %collective-permute-start.5 = (bf16[8,16,128]{2,1,0:T(8,128)(2,1)S(1)}, bf16[8,16,128]{2,1,0:T(8,128)(2,1)S(1)}, u32[]{:S(2)}, u32[]{:S(2)}) collective-permute-start(bf16[8,16,128]{2,1,0:T(8,128)(2,1)S(1)} %get-tuple-element.29), channel_id=1, source_target_pairs={{0,3},{1,2},{2,1},{3,0},{4,7},{5,6},{6,5},{7,4},{8,11},{9,10},{10,... | collective-permute-start | bytes 98312 | tf_op jit(solution)/shard_map/ppermute | solution.py:433
  11.0 5.2 %collective-permute-start.7 = (bf16[8,16,128]{2,1,0:T(8,128)(2,1)S(1)}, bf16[8,16,128]{2,1,0:T(8,128)(2,1)S(1)}, u32[]{:S(2)}, u32[]{:S(2)}) collective-permute-start(bf16[8,16,128]{2,1,0:T(8,128)(2,1)S(1)} %pad_maximum_fusion.1), channel_id=1, source_target_pairs={{0,1},{1,0},{2,5},{3,4},{4,3},{5,2},{6,9},{7,8},{8,7},{9,6},{10,13... | collective-permute-start | bytes 98312 | tf_op jit(solution)/shard_map/ppermute | solution.py:436
  13.5 1.2 %collective-permute-start.6 = (bf16[4,16,128]{2,1,0:T(8,128)(2,1)S(1)}, bf16[4,16,128]{2,1,0:T(8,128)(2,1)S(1)}, u32[]{:S(2)}, u32[]{:S(2)}) collective-permute-start(bf16[4,16,128]{2,1,0:T(8,128)(2,1)S(1)} %relay.3), channel_id=1, source_target_pairs={{0,1},{1,0},{2,3},{3,2},{4,5},{5,4},{6,7},{7,6},{8,9},{9,8},{10,11... | collective-permute-start | bytes 49160 | tf_op jit(solution)/shard_map/ppermute | solution.py:499

commit v8 on v7

--- a/solution.py
+++ b/solution.py
@@ -172,6 +172,19 @@
     return slots
 
 
+def first_traces(rhs, block):
+    value = jnp.dot(rhs, block, preferred_element_type=jnp.float32)
+    spare = jnp.zeros((value.shape[0], LANES - value.shape[1]), jnp.float32)
+    return jnp.concatenate([value, spare], axis=1)
+
+
+def traces_kernel(rhs, blocks, traces, rounded):
+    for f in range(rhs.shape[0]):
+        value = first_traces(rhs[f], blocks[f])
+        traces[f] = value
+        rounded[f] = value.astype(jnp.bfloat16)
+
+
 def first_kernel(
     elem_cap,
     devices,
@@ -179,8 +192,6 @@
     counts_hbm,
     rhs_hbm,
     blocks_hbm,
-    traces,
-    rounded,
     swap,
     even,
     slots,
@@ -191,7 +202,7 @@
     sems,
 ):
     me = lax.axis_index("elem")
-    face_dev, functionals, trace_len = rhs.shape
+    face_dev = rhs.shape[0]
     copies = start_all(
         [(faces_hbm, faces), (counts_hbm, counts), (rhs_hbm, rhs), (blocks_hbm, blocks)], sems
     )
@@ -202,14 +213,10 @@
         slots[i : i + 1, :] = jnp.full((1, LANES), slot)
     copies[2].wait()
     copies[3].wait()
-    for f in range(face_dev):
-        value = jnp.dot(rhs[f], blocks[f], preferred_element_type=jnp.float32)
-        traces[f, :, :trace_len] = value
-        rounded[f, :, :trace_len] = value.astype(jnp.bfloat16)
     for group in range(4):
         for r in range(SLOT):
-            slot = picked[group * SLOT + r]
-            tile = rounded[jnp.where(slot < face_dev, slot, 0)]
+            f = jnp.minimum(picked[group * SLOT + r], face_dev - 1)
+            tile = first_traces(rhs[f], blocks[f]).astype(jnp.bfloat16)
             put_bucket(group, r, tile, swap, even)
 
 
@@ -463,17 +470,15 @@
 
     params = pltpu.CompilerParams(vmem_limit_bytes=4 << 20)
     counts_smem = pltpu.SMEM(counts.shape, jnp.int32)
-    traces, rounded, swap, even, slots = pl.pallas_call(
+    swap, even, slots = pl.pallas_call(
         functools.partial(first_kernel, elem_cap, devices),
         out_shape=(
-            tiles(face_dev, jnp.float32),
-            tiles(face_dev, jnp.bfloat16),
             tiles(2 * SLOT, jnp.bfloat16),
             tiles(2 * SLOT, jnp.bfloat16),
             integers(far, LANES),
         ),
         in_specs=[hbm] * 4,
-        out_specs=(vmem,) * 5,
+        out_specs=(vmem,) * 3,
         scratch_shapes=[
             pltpu.VMEM(faces.shape, jnp.int32),
             counts_smem,
@@ -500,6 +505,14 @@
 
     from_sib, from_even, from_odd = exchange(routes, swap, even)
     all_terms = pltpu.VMEM((live + 1, functionals, 6 * LANES), jnp.float32)
+    traces, rounded = pl.pallas_call(
+        traces_kernel,
+        out_shape=(tiles(face_dev, jnp.float32), tiles(face_dev, jnp.bfloat16)),
+        in_specs=[vmem] * 2,
+        out_specs=(vmem,) * 2,
+        compiler_params=params,
+        name="all_traces",
+    )(rhs, face_blocks)
     rows, sums, remote, index_in = pl.pallas_call(
         functools.partial(rows_kernel, elem_cap),
         out_shape=(

time: 17.3 us -> 17.2 us (level)
  waiting for transfers between devices: 3.27 us -> 2.51 us
  starting transfers between devices: 6.93 us -> 7.3 us
  Pallas kernels: 6.81 us -> 7.1 us
    ppermute x2, starting transfers between devices: 1.51 us -> 1.88 us  [exchange(): from_even = lax.ppermute(even, 'elem', even_chips)]
    ppermute x2, waiting for transfers between devices: 0.53 us -> 0.16 us  [exchange(): from_sib = lax.ppermute(swap, 'elem', sibling)]
    ppermute x2, waiting for transfers between devices: 1.6 us -> 1.24 us  [exchange(): return (from_sib, from_even, lax.ppermute(odd, 'elem', odd_chips))]
    pallas_call x0 -> x1, Pallas kernels: none -> 0.35 us  [per_device(): pl.pallas_call(traces_kernel, out_shape=(tiles(face_dev, jnp.float32), ti...]
  transfers between devices with their start and end apart: 8 -> 8, of which waited for: 5 -> 5; matrix products, arithmetic and copies ran while one was open for 0% -> 0% of each run, Pallas kernels for 21% -> 23%
where the time goes in v8:
time: 17.2 us; the launch traced here: 17.1 us
  starting transfers between devices  7.3 us (42%)
  Pallas kernels  7.1 us (41%)
  waiting for transfers between devices  2.51 us (15%)
    ppermute x2, starting transfers between devices, exchange(): return (from_sib, from_even, lax.ppermute(odd, 'elem', odd_chips))  3.9 us
    ppermute x2, starting transfers between devices, exchange(): from_even = lax.ppermute(even, 'elem', even_chips)  1.88 us
    pallas_call x1, Pallas kernels, per_device(): pl.pallas_call(functools.partial(first_kernel, elem_cap, devices), out_sh...  1.69 us
    pallas_call x1, Pallas kernels, per_device(): pl.pallas_call(home_kernel, out_shape=all_terms, in_specs=[vmem] * 2, out...  1.47 us
    ppermute x2, waiting for transfers between devices, exchange(): return (from_sib, from_even, lax.ppermute(odd, 'elem', odd_chips))  1.24 us
    ppermute x2, starting transfers between devices, exchange(): from_sib = lax.ppermute(swap, 'elem', sibling)  1.19 us
    ppermute x2, waiting for transfers between devices, passed_on(): return lax.ppermute(relay, 'elem', routes[0])  1.04 us
    pallas_call x1, Pallas kernels, per_device(): pl.pallas_call(last_kernel, out_shape=jax.ShapeDtypeStruct(rhs.shape, jnp...  0.92 us
  transfers between devices with their start and end apart: 8, of which 5 were waited for; matrix products, arithmetic and copies ran while one was open for 0% of the time, Pallas kernels for 23%

profile of v8, /device:TPU:25, one launch (start us, length us, event | category | flops | bytes accessed | tf_op | source)
XLA Modules:
  0.0 17.1 jit_solution(1277552530783307529)
XLA Ops:
  0.0 1.7 %first_sweep.1 = (bf16[8,16,128]{2,1,0:T(8,128)(2,1)S(1)}, bf16[8,16,128]{2,1,0:T(8,128)(2,1)S(1)}, s32[16,128]{1,0:T(8,128)S(1)}) custom-call(s32[6,384]{1,0:T(8,128)} %bitcast.2, s32[32]{0:T(128)} %counts.1, bf16[27,16,125]{2,1,0:T(8,128)(2,1)} %rhs.3, bf16[27,125,125]{2,1,0:T(8,128)(2,1)} %blocks.5), custom_call_target="tpu_custom_call" | custom-call | flops 99999997952 | bytes 100000000 | tf_op jit(solution)/shard_map/first_sweep/pallas_call | solution.py:473
  1.7 0.7 %collective-permute-start = (bf16[8,16,128]{2,1,0:T(8,128)(2,1)S(1)}, bf16[8,16,128]{2,1,0:T(8,128)(2,1)S(1)}, u32[]{:S(2)}, u32[]{:S(2)}) collective-permute-start(bf16[8,16,128]{2,1,0:T(8,128)(2,1)S(1)} %get-tuple-element.21), channel_id=1, source_target_pairs={{0,1},{1,0},{2,3},{3,2},{4,5},{5,4},{6,7},{7,6},{8,9},{9,8},{10,11... | collective-permute-start | bytes 98312 | tf_op jit(solution)/shard_map/ppermute | solution.py:441
  2.5 1.2 %collective-permute-start.1 = (bf16[8,16,128]{2,1,0:T(8,128)(2,1)S(1)}, bf16[8,16,128]{2,1,0:T(8,128)(2,1)S(1)}, u32[]{:S(2)}, u32[]{:S(2)}) collective-permute-start(bf16[8,16,128]{2,1,0:T(8,128)(2,1)S(1)} %get-tuple-element.25), channel_id=1, source_target_pairs={{0,3},{1,2},{2,1},{3,0},{4,7},{5,6},{6,5},{7,4},{8,11},{9,10},{10,... | collective-permute-start | bytes 98312 | tf_op jit(solution)/shard_map/ppermute | solution.py:440
  3.7 0.0 collective-permute-done.from_sib
  3.7 2.0 %collective-permute-start.2 = (bf16[8,16,128]{2,1,0:T(8,128)(2,1)S(1)}, bf16[8,16,128]{2,1,0:T(8,128)(2,1)S(1)}, u32[]{:S(2)}, u32[]{:S(2)}) collective-permute-start(bf16[8,16,128]{2,1,0:T(8,128)(2,1)S(1)} %pad_maximum_fusion), channel_id=1, source_target_pairs={{0,1},{1,0},{2,5},{3,4},{4,3},{5,2},{6,9},{7,8},{8,7},{9,6},{10,13... | collective-permute-start | bytes 98312 | tf_op jit(solution)/shard_map/ppermute | solution.py:443
  5.7 0.4 %all_traces.1 = (f32[27,16,128]{2,1,0:T(8,128)S(1)}, bf16[27,16,128]{2,1,0:T(8,128)(2,1)S(1)}) custom-call(bf16[27,16,125]{2,1,0:T(8,128)(2,1)S(1)} %copy-done.3, bf16[27,125,125]{2,1,0:T(8,128)(2,1)S(1)} %copy-done.1), custom_call_target="tpu_custom_call" | custom-call | tf_op jit(solution)/shard_map/all_traces/pallas_call | solution.py:508
  6.1 0.9 %home_rows.1 = (bf16[9,16,768]{2,1,0:T(8,128)(2,1)S(1)}, s32[6,128]{1,0:T(8,128)S(1)}, s32[16,128]{1,0:T(8,128)S(1)}, s32[16,128]{1,0:T(8,128)S(1)}) custom-call(s32[6,384]{1,0:T(8,128)S(1)} %bitcast.3, s32[6,384]{1,0:T(8,128)S(1)} %bitcast.4, s32[32]{0:T(128)S(1)} %copy-done.6, s32[3,48,128]{2,1,0:T(8,128)S(1)} %copy-done.2, ...), custom_call_target="tpu_custom_call" | custom-call | tf_op jit(solution)/shard_map/home_rows/pallas_call | solution.py:516
  7.0 0.2 %collective-permute-start.3 = (bf16[4,16,128]{2,1,0:T(8,128)(2,1)S(1)}, bf16[4,16,128]{2,1,0:T(8,128)(2,1)S(1)}, u32[]{:S(2)}, u32[]{:S(2)}) collective-permute-start(bf16[4,16,128]{2,1,0:T(8,128)(2,1)S(1)} %relay.2), channel_id=1, source_target_pairs={{0,1},{1,0},{2,3},{3,2},{4,5},{5,4},{6,7},{7,6},{8,9},{9,8},{10,11... | collective-permute-start | bytes 49160 | tf_op jit(solution)/shard_map/ppermute | solution.py:504
  7.2 1.5 %home_terms.1._ = f32[10,16,768]{2,1,0:T(8,128)S(1)} custom-call(bf16[9,16,768]{2,1,0:T(8,128)(2,1)S(1)} %get-tuple-element.26.rows, bf16[12,750,750]{2,1,0:T(8,128)(2,1)S(1)} %copy-done), custom_call_target="tpu_custom_call" | custom-call | flops 162000000 | bytes 10125000 | tf_op jit(solution)/shard_map/home_terms/pallas_call | solution.py:530
  8.7 0.0 collective-permute-done.3.relayed
  8.7 0.3 %even_terms.1._ = f32[10,16,768]{2,1,0:T(8,128)S(1)} custom-call(s32[16,128]{1,0:T(8,128)S(1)} %get-tuple-element.23.remote, s32[16,128]{1,0:T(8,128)S(1)} %get-tuple-element.24.index_in, bf16[4,16,128]{2,1,0:T(8,128)(2,1)S(1)} %collective-permute-done.3.relayed, bf16[12,750,750]{2,1,0:T(8,128)(2,1)S(1)} %copy-done, ...), custom_call_target="tpu_custom_call", output_to_operand_aliasing={{}: (4, {})} | custom-call | tf_op jit(solution)/shard_map/even_terms/pallas_call | solution.py:544
  9.0 0.1 collective-permute-done.2.from_odd
  9.0 0.5 %remote_terms.1 = (bf16[8,16,128]{2,1,0:T(8,128)(2,1)S(1)}, bf16[8,16,128]{2,1,0:T(8,128)(2,1)S(1)}, f32[10,16,768]{2,1,0:T(8,128)S(1)}) custom-call(s32[16,128]{1,0:T(8,128)S(1)} %get-tuple-element.23.remote, s32[16,128]{1,0:T(8,128)S(1)} %get-tuple-element.24.index_in, s32[3,48,128]{2,1,0:T(8,128)S(1)} %copy-done.2, ...), custom_call_target="tpu_custom_call", output_to_operand_aliasing={{2}: (6, {})} | custom-call | tf_op jit(solution)/shard_map/remote_terms/pallas_call | solution.py:553
  9.6 0.5 %collective-permute-start.4 = (bf16[8,16,128]{2,1,0:T(8,128)(2,1)S(1)}, bf16[8,16,128]{2,1,0:T(8,128)(2,1)S(1)}, u32[]{:S(2)}, u32[]{:S(2)}) collective-permute-start(bf16[8,16,128]{2,1,0:T(8,128)(2,1)S(1)} %get-tuple-element.28), channel_id=1, source_target_pairs={{0,1},{1,0},{2,3},{3,2},{4,5},{5,4},{6,7},{7,6},{8,9},{9,8},{10,11... | collective-permute-start | bytes 98312 | tf_op jit(solution)/shard_map/ppermute | solution.py:441
  10.1 0.7 %collective-permute-start.5 = (bf16[8,16,128]{2,1,0:T(8,128)(2,1)S(1)}, bf16[8,16,128]{2,1,0:T(8,128)(2,1)S(1)}, u32[]{:S(2)}, u32[]{:S(2)}) collective-permute-start(bf16[8,16,128]{2,1,0:T(8,128)(2,1)S(1)} %get-tuple-element.29), channel_id=1, source_target_pairs={{0,3},{1,2},{2,1},{3,0},{4,7},{5,6},{6,5},{7,4},{8,11},{9,10},{10,... | collective-permute-start | bytes 98312 | tf_op jit(solution)/shard_map/ppermute | solution.py:440
  10.8 0.2 collective-permute-done.4.from_sib
  10.9 1.9 %collective-permute-start.7 = (bf16[8,16,128]{2,1,0:T(8,128)(2,1)S(1)}, bf16[8,16,128]{2,1,0:T(8,128)(2,1)S(1)}, u32[]{:S(2)}, u32[]{:S(2)}) collective-permute-start(bf16[8,16,128]{2,1,0:T(8,128)(2,1)S(1)} %pad_maximum_fusion.1), channel_id=1, source_target_pairs={{0,1},{1,0},{2,5},{3,4},{4,3},{5,2},{6,9},{7,8},{8,7},{9,6},{10,13... | collective-permute-start | bytes 98312 | tf_op jit(solution)/shard_map/ppermute | solution.py:443
  12.8 0.5 %home_sum.1._.base = f32[28,16,128]{2,1,0:T(8,128)S(1)} custom-call(s32[6,128]{1,0:T(8,128)S(1)} %get-tuple-element.22._.sums, s32[3,48,128]{2,1,0:T(8,128)S(1)} %copy-done.2, f32[10,16,768]{2,1,0:T(8,128)S(1)} %get-tuple-element.27.terms, bf16[27,16,125]{2,1,0:T(8,128)(2,1)S(1)} %copy-done.3), custom_call_target="tpu_custom_call" | custom-call | tf_op jit(solution)/shard_map/home_sum/pallas_call | solution.py:571
  13.3 0.1 collective-permute-done.5.from_even
  13.4 0.1 collective-permute-start.6
  13.5 1.0 %collective-permute-done.6.relayed = bf16[4,16,128]{2,1,0:T(8,128)(2,1)S(1)} collective-permute-done((bf16[4,16,128]{2,1,0:T(8,128)(2,1)S(1)}, bf16[4,16,128]{2,1,0:T(8,128)(2,1)S(1)}, u32[]{:S(2)}, u32[]{:S(2)}) %collective-permute-start.6) | collective-permute-done | bytes 16416 | tf_op jit(solution)/shard_map/ppermute | solution.py:504
  14.6 0.4 %early_update.1 = (f32[28,16,128]{2,1,0:T(8,128)S(1)}, f32[27,16,125]{2,1,0:T(8,128)S(1)}) custom-call(s32[16,128]{1,0:T(8,128)S(1)} %get-tuple-element.19.slots, f32[28,16,128]{2,1,0:T(8,128)S(1)} %home_sum.1._.base, bf16[8,16,128]{2,1,0:T(8,128)(2,1)S(1)} %collective-permute-done.4.from_sib, bf16[8,16,128]{2,1,0:T(8,128)(2,1)S(1)} %collective-permute-done.5.from_even, ...), custom_call_target="tpu_custom_call" | custom-call | tf_op jit(solution)/shard_map/early_update/pallas_call | solution.py:580
  15.0 1.2 %collective-permute-done.7.from_odd = bf16[8,16,128]{2,1,0:T(8,128)(2,1)S(1)} collective-permute-done((bf16[8,16,128]{2,1,0:T(8,128)(2,1)S(1)}, bf16[8,16,128]{2,1,0:T(8,128)(2,1)S(1)}, u32[]{:S(2)}, u32[]{:S(2)}) %collective-permute-start.7) | collective-permute-done | bytes 32800 | tf_op jit(solution)/shard_map/ppermute | solution.py:443
  16.1 0.9 %last_update.1 = f32[27,16,125]{2,1,0:T(8,128)} custom-call(s32[16,128]{1,0:T(8,128)S(1)} %get-tuple-element.19.slots, f32[28,16,128]{2,1,0:T(8,128)S(1)} %get-tuple-element.31.before, f32[27,16,125]{2,1,0:T(8,128)S(1)} %get-tuple-element.32.early, bf16[8,16,128]{2,1,0:T(8,128)(2,1)S(1)} %collective-permute-done.7.from_odd, ...), custom_call_target="tpu_custom_call" | custom-call | tf_op jit(solution)/shard_map/last_update/pallas_call | solution.py:591
  (23 shorter events, 0.1 us)
Async XLA Ops:
  0.0 5.7 %copy-start.1 = (bf16[27,125,125]{2,1,0:T(8,128)(2,1)S(1)}, bf16[27,125,125]{2,1,0:T(8,128)(2,1)}, u32[]{:S(2)}) copy-start(bf16[27,125,125]{2,1,0:T(8,128)(2,1)} %blocks.5) | copy-start | bytes 2531254
  0.0 5.7 %copy-start.3 = (bf16[27,16,125]{2,1,0:T(8,128)(2,1)S(1)}, bf16[27,16,125]{2,1,0:T(8,128)(2,1)}, u32[]{:S(2)}) copy-start(bf16[27,16,125]{2,1,0:T(8,128)(2,1)} %rhs.3) | copy-start | bytes 324004
  0.0 6.1 %copy-start.2 = (s32[3,48,128]{2,1,0:T(8,128)S(1)}, s32[3,48,128]{2,1,0:T(8,128)}, u32[]{:S(2)}) copy-start(s32[3,48,128]{2,1,0:T(8,128)} %constant.2.clone.tables) | copy-start | bytes 221188
  0.0 6.1 %copy-start.4 = (s32[384,6]{0,1:T(8,128)S(1)}, s32[384,6]{0,1:T(8,128)}, u32[]{:S(2)}) copy-start(s32[384,6]{0,1:T(8,128)} %param.10) | copy-start | bytes 27652
  0.0 6.1 %copy-start.5 = (s32[384,6]{0,1:T(8,128)S(1)}, s32[384,6]{0,1:T(8,128)}, u32[]{:S(2)}) copy-start(s32[384,6]{0,1:T(8,128)} %param.11) | copy-start | bytes 27652
  0.0 6.1 %copy-start.6 = (s32[32]{0:T(128)S(1)}, s32[32]{0:T(128)}, u32[]{:S(2)}) copy-start(s32[32]{0:T(128)} %counts.1) | copy-start | bytes 388
  0.0 7.2 %copy-start = (bf16[12,750,750]{2,1,0:T(8,128)(2,1)S(1)}, bf16[12,750,750]{2,1,0:T(8,128)(2,1)}, u32[]{:S(2)}) copy-start(bf16[12,750,750]{2,1,0:T(8,128)(2,1)} %mats.5) | copy-start | bytes 40500004
  1.7 1.9 %collective-permute-start = (bf16[8,16,128]{2,1,0:T(8,128)(2,1)S(1)}, bf16[8,16,128]{2,1,0:T(8,128)(2,1)S(1)}, u32[]{:S(2)}, u32[]{:S(2)}) collective-permute-start(bf16[8,16,128]{2,1,0:T(8,128)(2,1)S(1)} %get-tuple-element.21), channel_id=1, source_target_pairs={{0,1},{1,0},{2,3},{3,2},{4,5},{5,4},{6,7},{7,6},{8,9},{9,8},{10,11... | collective-permute-start | bytes 98312 | tf_op jit(solution)/shard_map/ppermute | solution.py:441
  2.5 4.5 %collective-permute-start.1 = (bf16[8,16,128]{2,1,0:T(8,128)(2,1)S(1)}, bf16[8,16,128]{2,1,0:T(8,128)(2,1)S(1)}, u32[]{:S(2)}, u32[]{:S(2)}) collective-permute-start(bf16[8,16,128]{2,1,0:T(8,128)(2,1)S(1)} %get-tuple-element.25), channel_id=1, source_target_pairs={{0,3},{1,2},{2,1},{3,0},{4,7},{5,6},{6,5},{7,4},{8,11},{9,10},{10,... | collective-permute-start | bytes 98312 | tf_op jit(solution)/shard_map/ppermute | solution.py:440
  3.7 5.4 %collective-permute-start.2 = (bf16[8,16,128]{2,1,0:T(8,128)(2,1)S(1)}, bf16[8,16,128]{2,1,0:T(8,128)(2,1)S(1)}, u32[]{:S(2)}, u32[]{:S(2)}) collective-permute-start(bf16[8,16,128]{2,1,0:T(8,128)(2,1)S(1)} %pad_maximum_fusion), channel_id=1, source_target_pairs={{0,1},{1,0},{2,5},{3,4},{4,3},{5,2},{6,9},{7,8},{8,7},{9,6},{10,13... | collective-permute-start | bytes 98312 | tf_op jit(solution)/shard_map/ppermute | solution.py:443
  7.0 1.7 %collective-permute-start.3 = (bf16[4,16,128]{2,1,0:T(8,128)(2,1)S(1)}, bf16[4,16,128]{2,1,0:T(8,128)(2,1)S(1)}, u32[]{:S(2)}, u32[]{:S(2)}) collective-permute-start(bf16[4,16,128]{2,1,0:T(8,128)(2,1)S(1)} %relay.2), channel_id=1, source_target_pairs={{0,1},{1,0},{2,3},{3,2},{4,5},{5,4},{6,7},{7,6},{8,9},{9,8},{10,11... | collective-permute-start | bytes 49160 | tf_op jit(solution)/shard_map/ppermute | solution.py:504
  9.6 1.3 %collective-permute-start.4 = (bf16[8,16,128]{2,1,0:T(8,128)(2,1)S(1)}, bf16[8,16,128]{2,1,0:T(8,128)(2,1)S(1)}, u32[]{:S(2)}, u32[]{:S(2)}) collective-permute-start(bf16[8,16,128]{2,1,0:T(8,128)(2,1)S(1)} %get-tuple-element.28), channel_id=1, source_target_pairs={{0,1},{1,0},{2,3},{3,2},{4,5},{5,4},{6,7},{7,6},{8,9},{9,8},{10,11... | collective-permute-start | bytes 98312 | tf_op jit(solution)/shard_map/ppermute | solution.py:441
  10.1 3.3 %collective-permute-start.5 = (bf16[8,16,128]{2,1,0:T(8,128)(2,1)S(1)}, bf16[8,16,128]{2,1,0:T(8,128)(2,1)S(1)}, u32[]{:S(2)}, u32[]{:S(2)}) collective-permute-start(bf16[8,16,128]{2,1,0:T(8,128)(2,1)S(1)} %get-tuple-element.29), channel_id=1, source_target_pairs={{0,3},{1,2},{2,1},{3,0},{4,7},{5,6},{6,5},{7,4},{8,11},{9,10},{10,... | collective-permute-start | bytes 98312 | tf_op jit(solution)/shard_map/ppermute | solution.py:440
  10.9 5.2 %collective-permute-start.7 = (bf16[8,16,128]{2,1,0:T(8,128)(2,1)S(1)}, bf16[8,16,128]{2,1,0:T(8,128)(2,1)S(1)}, u32[]{:S(2)}, u32[]{:S(2)}) collective-permute-start(bf16[8,16,128]{2,1,0:T(8,128)(2,1)S(1)} %pad_maximum_fusion.1), channel_id=1, source_target_pairs={{0,1},{1,0},{2,5},{3,4},{4,3},{5,2},{6,9},{7,8},{8,7},{9,6},{10,13... | collective-permute-start | bytes 98312 | tf_op jit(solution)/shard_map/ppermute | solution.py:443
  13.4 1.2 %collective-permute-start.6 = (bf16[4,16,128]{2,1,0:T(8,128)(2,1)S(1)}, bf16[4,16,128]{2,1,0:T(8,128)(2,1)S(1)}, u32[]{:S(2)}, u32[]{:S(2)}) collective-permute-start(bf16[4,16,128]{2,1,0:T(8,128)(2,1)S(1)} %relay.3), channel_id=1, source_target_pairs={{0,1},{1,0},{2,3},{3,2},{4,5},{5,4},{6,7},{7,6},{8,9},{9,8},{10,11... | collective-permute-start | bytes 49160 | tf_op jit(solution)/shard_map/ppermute | solution.py:504

commit v9 on v8

--- a/solution.py
+++ b/solution.py
@@ -176,13 +176,6 @@
     value = jnp.dot(rhs, block, preferred_element_type=jnp.float32)
     spare = jnp.zeros((value.shape[0], LANES - value.shape[1]), jnp.float32)
     return jnp.concatenate([value, spare], axis=1)
-
-
-def traces_kernel(rhs, blocks, traces, rounded):
-    for f in range(rhs.shape[0]):
-        value = first_traces(rhs[f], blocks[f])
-        traces[f] = value
-        rounded[f] = value.astype(jnp.bfloat16)
 
 
 def first_kernel(
@@ -262,8 +255,10 @@
     orient,
     counts,
     tables,
-    rounded,
+    rhs,
+    blocks,
     from_sib,
+    traces,
     rows,
     sums,
     remote,
@@ -271,11 +266,14 @@
     table,
 ):
     me = lax.axis_index("elem")
-    face_dev, functionals, _ = rounded.shape
+    face_dev, functionals, _ = rhs.shape
     live = rows.shape[0]
     trace_len = COMP * EDGE * EDGE
     gap = LANES - trace_len
-    table[:face_dev] = rounded[...]
+    for f in range(face_dev):
+        value = first_traces(rhs[f], blocks[f])
+        traces[f] = value
+        table[f] = value.astype(jnp.bfloat16)
     table[face_dev] = jnp.zeros((functionals, LANES), jnp.bfloat16)
     table[face_dev + 1 :] = from_sib[:SLOT]
     gather, home, slots, picks = own_lists(me, elem_cap, face_dev, faces, orient, counts)
@@ -505,28 +503,21 @@
 
     from_sib, from_even, from_odd = exchange(routes, swap, even)
     all_terms = pltpu.VMEM((live + 1, functionals, 6 * LANES), jnp.float32)
-    traces, rounded = pl.pallas_call(
-        traces_kernel,
-        out_shape=(tiles(face_dev, jnp.float32), tiles(face_dev, jnp.bfloat16)),
-        in_specs=[vmem] * 2,
-        out_specs=(vmem,) * 2,
-        compiler_params=params,
-        name="all_traces",
-    )(rhs, face_blocks)
-    rows, sums, remote, index_in = pl.pallas_call(
+    traces, rows, sums, remote, index_in = pl.pallas_call(
         functools.partial(rows_kernel, elem_cap),
         out_shape=(
+            tiles(face_dev, jnp.float32),
             tiles(live, jnp.bfloat16, 6 * LANES),
             integers(6, LANES),
             integers(far, LANES),
             integers(far, LANES),
         ),
-        in_specs=[vmem] * 6,
-        out_specs=(vmem,) * 4,
+        in_specs=[vmem] * 7,
+        out_specs=(vmem,) * 5,
         scratch_shapes=[pltpu.VMEM((face_dev + 1 + SLOT, functionals, LANES), jnp.bfloat16)],
         compiler_params=params,
         name="home_rows",
-    )(elem_faces.T, orient.T, counts, tables, rounded, from_sib)
+    )(elem_faces.T, orient.T, counts, tables, rhs, face_blocks, from_sib)
     terms = pl.pallas_call(
         home_kernel,
         out_shape=all_terms,

time: 17.2 us -> 17.2 us (level)
  waiting for transfers between devices: 2.51 us -> 3.2 us
  starting transfers between devices: 7.3 us -> 6.95 us
  Pallas kernels: 7.1 us -> 6.76 us
    pallas_call x1 -> x0, Pallas kernels: 0.35 us -> none  [per_device(): pl.pallas_call(traces_kernel, out_shape=(tiles(face_dev, jnp.float32), ti...]
    ppermute x2, starting transfers between devices: 1.88 us -> 1.53 us  [exchange(): from_even = lax.ppermute(even, 'elem', even_chips)]
    ppermute x2, waiting for transfers between devices: 0.16 us -> 0.51 us  [exchange(): from_sib = lax.ppermute(swap, 'elem', sibling)]
    ppermute x2, waiting for transfers between devices: 1.24 us -> 1.58 us  [exchange(): return (from_sib, from_even, lax.ppermute(odd, 'elem', odd_chips))]
  transfers between devices with their start and end apart: 8 -> 8, of which waited for: 5 -> 5; matrix products, arithmetic and copies ran while one was open for 0% -> 0% of each run, Pallas kernels for 23% -> 21%
where the time goes in v9:
time: 17.2 us; the launch traced here: 17.1 us
  starting transfers between devices  6.95 us (40%)
  Pallas kernels  6.76 us (39%)
  waiting for transfers between devices  3.2 us (19%)
    ppermute x2, starting transfers between devices, exchange(): return (from_sib, from_even, lax.ppermute(odd, 'elem', odd_chips))  3.9 us
    pallas_call x1, Pallas kernels, per_device(): pl.pallas_call(functools.partial(first_kernel, elem_cap, devices), out_sh...  1.69 us
    ppermute x2, waiting for transfers between devices, exchange(): return (from_sib, from_even, lax.ppermute(odd, 'elem', odd_chips))  1.58 us
    ppermute x2, starting transfers between devices, exchange(): from_even = lax.ppermute(even, 'elem', even_chips)  1.53 us
    pallas_call x1, Pallas kernels, per_device(): pl.pallas_call(home_kernel, out_shape=all_terms, in_specs=[vmem] * 2, out...  1.47 us
    ppermute x2, starting transfers between devices, exchange(): from_sib = lax.ppermute(swap, 'elem', sibling)  1.2 us
    ppermute x2, waiting for transfers between devices, passed_on(): return lax.ppermute(relay, 'elem', routes[0])  1.04 us
    pallas_call x1, Pallas kernels, per_device(): pl.pallas_call(last_kernel, out_shape=jax.ShapeDtypeStruct(rhs.shape, jnp...  0.92 us
  transfers between devices with their start and end apart: 8, of which 5 were waited for; matrix products, arithmetic and copies ran while one was open for 0% of the time, Pallas kernels for 21%

profile of v9, /device:TPU:25, one launch (start us, length us, event | category | flops | bytes accessed | tf_op | source)
XLA Modules:
  0.0 17.1 jit_solution(1760959577002261374)
XLA Ops:
  0.0 1.7 %first_sweep.1 = (bf16[8,16,128]{2,1,0:T(8,128)(2,1)S(1)}, bf16[8,16,128]{2,1,0:T(8,128)(2,1)S(1)}, s32[16,128]{1,0:T(8,128)S(1)}) custom-call(s32[6,384]{1,0:T(8,128)} %bitcast.2, s32[32]{0:T(128)} %counts.1, bf16[27,16,125]{2,1,0:T(8,128)(2,1)} %rhs.3, bf16[27,125,125]{2,1,0:T(8,128)(2,1)} %blocks.5), custom_call_target="tpu_custom_call" | custom-call | flops 99999997952 | bytes 100000000 | tf_op jit(solution)/shard_map/first_sweep/pallas_call | solution.py:471
  1.7 0.7 %collective-permute-start = (bf16[8,16,128]{2,1,0:T(8,128)(2,1)S(1)}, bf16[8,16,128]{2,1,0:T(8,128)(2,1)S(1)}, u32[]{:S(2)}, u32[]{:S(2)}) collective-permute-start(bf16[8,16,128]{2,1,0:T(8,128)(2,1)S(1)} %get-tuple-element.19), channel_id=1, source_target_pairs={{0,1},{1,0},{2,3},{3,2},{4,5},{5,4},{6,7},{7,6},{8,9},{9,8},{10,11... | collective-permute-start | bytes 98312 | tf_op jit(solution)/shard_map/ppermute | solution.py:439
  2.5 1.2 %collective-permute-start.1 = (bf16[8,16,128]{2,1,0:T(8,128)(2,1)S(1)}, bf16[8,16,128]{2,1,0:T(8,128)(2,1)S(1)}, u32[]{:S(2)}, u32[]{:S(2)}) collective-permute-start(bf16[8,16,128]{2,1,0:T(8,128)(2,1)S(1)} %get-tuple-element.23), channel_id=1, source_target_pairs={{0,3},{1,2},{2,1},{3,0},{4,7},{5,6},{6,5},{7,4},{8,11},{9,10},{10,... | collective-permute-start | bytes 98312 | tf_op jit(solution)/shard_map/ppermute | solution.py:438
  3.7 0.0 collective-permute-done.from_sib
  3.7 2.0 %collective-permute-start.2 = (bf16[8,16,128]{2,1,0:T(8,128)(2,1)S(1)}, bf16[8,16,128]{2,1,0:T(8,128)(2,1)S(1)}, u32[]{:S(2)}, u32[]{:S(2)}) collective-permute-start(bf16[8,16,128]{2,1,0:T(8,128)(2,1)S(1)} %pad_maximum_fusion), channel_id=1, source_target_pairs={{0,1},{1,0},{2,5},{3,4},{4,3},{5,2},{6,9},{7,8},{8,7},{9,6},{10,13... | collective-permute-start | bytes 98312 | tf_op jit(solution)/shard_map/ppermute | solution.py:441
  5.7 0.9 %home_rows.1 = (f32[27,16,128]{2,1,0:T(8,128)S(1)}, bf16[9,16,768]{2,1,0:T(8,128)(2,1)S(1)}, s32[6,128]{1,0:T(8,128)S(1)}, s32[16,128]{1,0:T(8,128)S(1)}, s32[16,128]{1,0:T(8,128)S(1)}) custom-call(s32[6,384]{1,0:T(8,128)S(1)} %bitcast.3, s32[6,384]{1,0:T(8,128)S(1)} %bitcast.4, s32[32]{0:T(128)S(1)} %copy-done.6, s32[3,48,128]{2,1,0:T(8,128)S(1)} %copy-done.2, ...), custom_call_target="tpu_custom_call" | custom-call | tf_op jit(solution)/shard_map/home_rows/pallas_call | solution.py:506
  6.6 0.0 collective-permute-done.1.from_even
  6.7 0.2 %collective-permute-start.3 = (bf16[4,16,128]{2,1,0:T(8,128)(2,1)S(1)}, bf16[4,16,128]{2,1,0:T(8,128)(2,1)S(1)}, u32[]{:S(2)}, u32[]{:S(2)}) collective-permute-start(bf16[4,16,128]{2,1,0:T(8,128)(2,1)S(1)} %relay.2), channel_id=1, source_target_pairs={{0,1},{1,0},{2,3},{3,2},{4,5},{5,4},{6,7},{7,6},{8,9},{9,8},{10,11... | collective-permute-start | bytes 49160 | tf_op jit(solution)/shard_map/ppermute | solution.py:502
  6.8 1.5 %home_terms.1._ = f32[10,16,768]{2,1,0:T(8,128)S(1)} custom-call(bf16[9,16,768]{2,1,0:T(8,128)(2,1)S(1)} %get-tuple-element.24.rows, bf16[12,750,750]{2,1,0:T(8,128)(2,1)S(1)} %copy-done), custom_call_target="tpu_custom_call" | custom-call | flops 162000000 | bytes 10125000 | tf_op jit(solution)/shard_map/home_terms/pallas_call | solution.py:521
  8.3 0.0 collective-permute-done.3.relayed
  8.3 0.3 %even_terms.1._ = f32[10,16,768]{2,1,0:T(8,128)S(1)} custom-call(s32[16,128]{1,0:T(8,128)S(1)} %get-tuple-element.21.remote, s32[16,128]{1,0:T(8,128)S(1)} %get-tuple-element.22.index_in, bf16[4,16,128]{2,1,0:T(8,128)(2,1)S(1)} %collective-permute-done.3.relayed, bf16[12,750,750]{2,1,0:T(8,128)(2,1)S(1)} %copy-done, ...), custom_call_target="tpu_custom_call", output_to_operand_aliasing={{}: (4, {})} | custom-call | tf_op jit(solution)/shard_map/even_terms/pallas_call | solution.py:535
  8.6 0.4 %collective-permute-done.2.from_odd = bf16[8,16,128]{2,1,0:T(8,128)(2,1)S(1)} collective-permute-done((bf16[8,16,128]{2,1,0:T(8,128)(2,1)S(1)}, bf16[8,16,128]{2,1,0:T(8,128)(2,1)S(1)}, u32[]{:S(2)}, u32[]{:S(2)}) %collective-permute-start.2) | collective-permute-done | bytes 32800 | tf_op jit(solution)/shard_map/ppermute | solution.py:441
  9.0 0.5 %remote_terms.1 = (bf16[8,16,128]{2,1,0:T(8,128)(2,1)S(1)}, bf16[8,16,128]{2,1,0:T(8,128)(2,1)S(1)}, f32[10,16,768]{2,1,0:T(8,128)S(1)}) custom-call(s32[16,128]{1,0:T(8,128)S(1)} %get-tuple-element.21.remote, s32[16,128]{1,0:T(8,128)S(1)} %get-tuple-element.22.index_in, s32[3,48,128]{2,1,0:T(8,128)S(1)} %copy-done.2, ...), custom_call_target="tpu_custom_call", output_to_operand_aliasing={{2}: (6, {})} | custom-call | tf_op jit(solution)/shard_map/remote_terms/pallas_call | solution.py:544
  9.6 0.5 %collective-permute-start.4 = (bf16[8,16,128]{2,1,0:T(8,128)(2,1)S(1)}, bf16[8,16,128]{2,1,0:T(8,128)(2,1)S(1)}, u32[]{:S(2)}, u32[]{:S(2)}) collective-permute-start(bf16[8,16,128]{2,1,0:T(8,128)(2,1)S(1)} %get-tuple-element.26), channel_id=1, source_target_pairs={{0,1},{1,0},{2,3},{3,2},{4,5},{5,4},{6,7},{7,6},{8,9},{9,8},{10,11... | collective-permute-start | bytes 98312 | tf_op jit(solution)/shard_map/ppermute | solution.py:439
  10.1 0.4 %collective-permute-start.5 = (bf16[8,16,128]{2,1,0:T(8,128)(2,1)S(1)}, bf16[8,16,128]{2,1,0:T(8,128)(2,1)S(1)}, u32[]{:S(2)}, u32[]{:S(2)}) collective-permute-start(bf16[8,16,128]{2,1,0:T(8,128)(2,1)S(1)} %get-tuple-element.27), channel_id=1, source_target_pairs={{0,3},{1,2},{2,1},{3,0},{4,7},{5,6},{6,5},{7,4},{8,11},{9,10},{10,... | collective-permute-start | bytes 98312 | tf_op jit(solution)/shard_map/ppermute | solution.py:438
  10.4 0.5 %collective-permute-done.4.from_sib = bf16[8,16,128]{2,1,0:T(8,128)(2,1)S(1)} collective-permute-done((bf16[8,16,128]{2,1,0:T(8,128)(2,1)S(1)}, bf16[8,16,128]{2,1,0:T(8,128)(2,1)S(1)}, u32[]{:S(2)}, u32[]{:S(2)}) %collective-permute-start.4) | collective-permute-done | bytes 32800 | tf_op jit(solution)/shard_map/ppermute | solution.py:439
  10.9 1.9 %collective-permute-start.7 = (bf16[8,16,128]{2,1,0:T(8,128)(2,1)S(1)}, bf16[8,16,128]{2,1,0:T(8,128)(2,1)S(1)}, u32[]{:S(2)}, u32[]{:S(2)}) collective-permute-start(bf16[8,16,128]{2,1,0:T(8,128)(2,1)S(1)} %pad_maximum_fusion.1), channel_id=1, source_target_pairs={{0,1},{1,0},{2,5},{3,4},{4,3},{5,2},{6,9},{7,8},{8,7},{9,6},{10,13... | collective-permute-start | bytes 98312 | tf_op jit(solution)/shard_map/ppermute | solution.py:441
  12.8 0.5 %home_sum.1._.base = f32[28,16,128]{2,1,0:T(8,128)S(1)} custom-call(s32[6,128]{1,0:T(8,128)S(1)} %get-tuple-element.20._.sums, s32[3,48,128]{2,1,0:T(8,128)S(1)} %copy-done.2, f32[10,16,768]{2,1,0:T(8,128)S(1)} %get-tuple-element.25.terms, bf16[27,16,125]{2,1,0:T(8,128)(2,1)S(1)} %copy-done.3), custom_call_target="tpu_custom_call" | custom-call | tf_op jit(solution)/shard_map/home_sum/pallas_call | solution.py:562
  13.3 0.1 collective-permute-done.5.from_even
  13.4 0.1 collective-permute-start.6
  13.5 1.0 %collective-permute-done.6.relayed = bf16[4,16,128]{2,1,0:T(8,128)(2,1)S(1)} collective-permute-done((bf16[4,16,128]{2,1,0:T(8,128)(2,1)S(1)}, bf16[4,16,128]{2,1,0:T(8,128)(2,1)S(1)}, u32[]{:S(2)}, u32[]{:S(2)}) %collective-permute-start.6) | collective-permute-done | bytes 16416 | tf_op jit(solution)/shard_map/ppermute | solution.py:502
  14.6 0.4 %early_update.1 = (f32[28,16,128]{2,1,0:T(8,128)S(1)}, f32[27,16,125]{2,1,0:T(8,128)S(1)}) custom-call(s32[16,128]{1,0:T(8,128)S(1)} %get-tuple-element.18.slots, f32[28,16,128]{2,1,0:T(8,128)S(1)} %home_sum.1._.base, bf16[8,16,128]{2,1,0:T(8,128)(2,1)S(1)} %collective-permute-done.4.from_sib, bf16[8,16,128]{2,1,0:T(8,128)(2,1)S(1)} %collective-permute-done.5.from_even, ...), custom_call_target="tpu_custom_call" | custom-call | tf_op jit(solution)/shard_map/early_update/pallas_call | solution.py:571
  15.0 1.1 %collective-permute-done.7.from_odd = bf16[8,16,128]{2,1,0:T(8,128)(2,1)S(1)} collective-permute-done((bf16[8,16,128]{2,1,0:T(8,128)(2,1)S(1)}, bf16[8,16,128]{2,1,0:T(8,128)(2,1)S(1)}, u32[]{:S(2)}, u32[]{:S(2)}) %collective-permute-start.7) | collective-permute-done | bytes 32800 | tf_op jit(solution)/shard_map/ppermute | solution.py:441
  16.1 0.9 %last_update.1 = f32[27,16,125]{2,1,0:T(8,128)} custom-call(s32[16,128]{1,0:T(8,128)S(1)} %get-tuple-element.18.slots, f32[28,16,128]{2,1,0:T(8,128)S(1)} %get-tuple-element.29.before, f32[27,16,125]{2,1,0:T(8,128)S(1)} %get-tuple-element.30.early, bf16[8,16,128]{2,1,0:T(8,128)(2,1)S(1)} %collective-permute-done.7.from_odd, ...), custom_call_target="tpu_custom_call" | custom-call | tf_op jit(solution)/shard_map/last_update/pallas_call | solution.py:582
  (22 shorter events, 0.1 us)
Async XLA Ops:
  0.0 5.7 %copy-start.1 = (bf16[27,125,125]{2,1,0:T(8,128)(2,1)S(1)}, bf16[27,125,125]{2,1,0:T(8,128)(2,1)}, u32[]{:S(2)}) copy-start(bf16[27,125,125]{2,1,0:T(8,128)(2,1)} %blocks.5) | copy-start | bytes 2531254
  0.0 5.7 %copy-start.2 = (s32[3,48,128]{2,1,0:T(8,128)S(1)}, s32[3,48,128]{2,1,0:T(8,128)}, u32[]{:S(2)}) copy-start(s32[3,48,128]{2,1,0:T(8,128)} %constant.2.clone.tables) | copy-start | bytes 221188
  0.0 5.7 %copy-start.3 = (bf16[27,16,125]{2,1,0:T(8,128)(2,1)S(1)}, bf16[27,16,125]{2,1,0:T(8,128)(2,1)}, u32[]{:S(2)}) copy-start(bf16[27,16,125]{2,1,0:T(8,128)(2,1)} %rhs.3) | copy-start | bytes 324004
  0.0 5.7 %copy-start.4 = (s32[384,6]{0,1:T(8,128)S(1)}, s32[384,6]{0,1:T(8,128)}, u32[]{:S(2)}) copy-start(s32[384,6]{0,1:T(8,128)} %param.10) | copy-start | bytes 27652
  0.0 5.7 %copy-start.5 = (s32[384,6]{0,1:T(8,128)S(1)}, s32[384,6]{0,1:T(8,128)}, u32[]{:S(2)}) copy-start(s32[384,6]{0,1:T(8,128)} %param.11) | copy-start | bytes 27652
  0.0 5.7 %copy-start.6 = (s32[32]{0:T(128)S(1)}, s32[32]{0:T(128)}, u32[]{:S(2)}) copy-start(s32[32]{0:T(128)} %counts.1) | copy-start | bytes 388
  0.0 6.8 %copy-start = (bf16[12,750,750]{2,1,0:T(8,128)(2,1)S(1)}, bf16[12,750,750]{2,1,0:T(8,128)(2,1)}, u32[]{:S(2)}) copy-start(bf16[12,750,750]{2,1,0:T(8,128)(2,1)} %mats.5) | copy-start | bytes 40500004
  1.7 1.9 %collective-permute-start = (bf16[8,16,128]{2,1,0:T(8,128)(2,1)S(1)}, bf16[8,16,128]{2,1,0:T(8,128)(2,1)S(1)}, u32[]{:S(2)}, u32[]{:S(2)}) collective-permute-start(bf16[8,16,128]{2,1,0:T(8,128)(2,1)S(1)} %get-tuple-element.19), channel_id=1, source_target_pairs={{0,1},{1,0},{2,3},{3,2},{4,5},{5,4},{6,7},{7,6},{8,9},{9,8},{10,11... | collective-permute-start | bytes 98312 | tf_op jit(solution)/shard_map/ppermute | solution.py:439
  2.5 4.2 %collective-permute-start.1 = (bf16[8,16,128]{2,1,0:T(8,128)(2,1)S(1)}, bf16[8,16,128]{2,1,0:T(8,128)(2,1)S(1)}, u32[]{:S(2)}, u32[]{:S(2)}) collective-permute-start(bf16[8,16,128]{2,1,0:T(8,128)(2,1)S(1)} %get-tuple-element.23), channel_id=1, source_target_pairs={{0,3},{1,2},{2,1},{3,0},{4,7},{5,6},{6,5},{7,4},{8,11},{9,10},{10,... | collective-permute-start | bytes 98312 | tf_op jit(solution)/shard_map/ppermute | solution.py:438
  3.7 5.4 %collective-permute-start.2 = (bf16[8,16,128]{2,1,0:T(8,128)(2,1)S(1)}, bf16[8,16,128]{2,1,0:T(8,128)(2,1)S(1)}, u32[]{:S(2)}, u32[]{:S(2)}) collective-permute-start(bf16[8,16,128]{2,1,0:T(8,128)(2,1)S(1)} %pad_maximum_fusion), channel_id=1, source_target_pairs={{0,1},{1,0},{2,5},{3,4},{4,3},{5,2},{6,9},{7,8},{8,7},{9,6},{10,13... | collective-permute-start | bytes 98312 | tf_op jit(solution)/shard_map/ppermute | solution.py:441
  6.7 1.7 %collective-permute-start.3 = (bf16[4,16,128]{2,1,0:T(8,128)(2,1)S(1)}, bf16[4,16,128]{2,1,0:T(8,128)(2,1)S(1)}, u32[]{:S(2)}, u32[]{:S(2)}) collective-permute-start(bf16[4,16,128]{2,1,0:T(8,128)(2,1)S(1)} %relay.2), channel_id=1, source_target_pairs={{0,1},{1,0},{2,3},{3,2},{4,5},{5,4},{6,7},{7,6},{8,9},{9,8},{10,11... | collective-permute-start | bytes 49160 | tf_op jit(solution)/shard_map/ppermute | solution.py:502
  9.6 1.3 %collective-permute-start.4 = (bf16[8,16,128]{2,1,0:T(8,128)(2,1)S(1)}, bf16[8,16,128]{2,1,0:T(8,128)(2,1)S(1)}, u32[]{:S(2)}, u32[]{:S(2)}) collective-permute-start(bf16[8,16,128]{2,1,0:T(8,128)(2,1)S(1)} %get-tuple-element.26), channel_id=1, source_target_pairs={{0,1},{1,0},{2,3},{3,2},{4,5},{5,4},{6,7},{7,6},{8,9},{9,8},{10,11... | collective-permute-start | bytes 98312 | tf_op jit(solution)/shard_map/ppermute | solution.py:439
  10.1 3.3 %collective-permute-start.5 = (bf16[8,16,128]{2,1,0:T(8,128)(2,1)S(1)}, bf16[8,16,128]{2,1,0:T(8,128)(2,1)S(1)}, u32[]{:S(2)}, u32[]{:S(2)}) collective-permute-start(bf16[8,16,128]{2,1,0:T(8,128)(2,1)S(1)} %get-tuple-element.27), channel_id=1, source_target_pairs={{0,3},{1,2},{2,1},{3,0},{4,7},{5,6},{6,5},{7,4},{8,11},{9,10},{10,... | collective-permute-start | bytes 98312 | tf_op jit(solution)/shard_map/ppermute | solution.py:438
  10.9 5.2 %collective-permute-start.7 = (bf16[8,16,128]{2,1,0:T(8,128)(2,1)S(1)}, bf16[8,16,128]{2,1,0:T(8,128)(2,1)S(1)}, u32[]{:S(2)}, u32[]{:S(2)}) collective-permute-start(bf16[8,16,128]{2,1,0:T(8,128)(2,1)S(1)} %pad_maximum_fusion.1), channel_id=1, source_target_pairs={{0,1},{1,0},{2,5},{3,4},{4,3},{5,2},{6,9},{7,8},{8,7},{9,6},{10,13... | collective-permute-start | bytes 98312 | tf_op jit(solution)/shard_map/ppermute | solution.py:441
  13.4 1.2 %collective-permute-start.6 = (bf16[4,16,128]{2,1,0:T(8,128)(2,1)S(1)}, bf16[4,16,128]{2,1,0:T(8,128)(2,1)S(1)}, u32[]{:S(2)}, u32[]{:S(2)}) collective-permute-start(bf16[4,16,128]{2,1,0:T(8,128)(2,1)S(1)} %relay.3), channel_id=1, source_target_pairs={{0,1},{1,0},{2,3},{3,2},{4,5},{5,4},{6,7},{7,6},{8,9},{9,8},{10,11... | collective-permute-start | bytes 49160 | tf_op jit(solution)/shard_map/ppermute | solution.py:502
